TPU v7x, 32 devices: a whole 2x2x4 slice. The times are simulated.
32 devices in a mesh: horiz: 8 (over y, x, core), vert: 4 (over z).
Axes of the slice: x: 2, y: 2, z: 4, core: 2. Of those that a mesh axis runs over, the one named last changes fastest.
Arguments:
- velocity: float32 [3, 64, 32, 128], P(None, 'horiz', 'vert'), may hold values from -3 to 3
- heights: float32 [4], P('vert'), may hold values from 0.5 to 2
- time_step: float32 [], replicated, may hold values from 0.005 to 0.02
Outputs:
- rate: float32 [3, 64, 32, 128], P(None, 'horiz', 'vert')
All inputs are finite; a program needn't handle non-finite values.
Results may differ from a plain program's by a relative error of at most 0.000084.
Values sent between devices are 32-bit elements; how exact they have to be, the bound alone decides.
No kernel may reach another device: no remote copies, remote signals or barrier semaphores. Data moves between devices by JAX's collectives and lax.ppermute only.
A program may use at most 64 MiB of HBM per device.

v0:
```python
import functools

import jax
import jax.numpy as jnp
import ml_dtypes
import numpy as np
from jax import lax
from jax.experimental import pallas as pl
from jax.experimental.pallas import tpu as pltpu
from jax.sharding import PartitionSpec as P

gll_half = [1.0, 0.8717401485096066, 0.5917001814331423, 0.2092992179024789]
gll_half_weights = [
    0.03571428571428571,
    0.21070422714350603,
    0.34112269248350435,
    0.4124587946587038,
]
gauss_half = [
    0.9815606342467192,
    0.9041172563704749,
    0.7699026741943047,
    0.5873179542866175,
    0.3678314989981802,
    0.1252334085114689,
]
gauss_half_weights = [
    0.0471753363865118,
    0.1069393259953184,
    0.1600783285433462,
    0.2031674267230659,
    0.2334925365383548,
    0.2491470458134028,
]

f32 = jnp.float32
bf16 = jnp.bfloat16
ROWS = 192
SPAN = 128
SPAN_ELEMENTS = 16


def mirrored(values, sign):
    return np.concatenate([sign * np.array(values), np.array(values[::-1])])


def lagrange(targets, sources):
    matrix = np.ones((targets.size, sources.size))
    for j in range(sources.size):
        for k in range(sources.size):
            if k != j:
                matrix[:, j] = matrix[:, j] * (targets - sources[k]) / (sources[j] - sources[k])
    return matrix


def node_tables():
    gll_points = mirrored(gll_half, -1.0)
    gll_weights = mirrored(gll_half_weights, 1.0)
    fine_points = mirrored(gauss_half, -1.0)
    fine_weights = mirrored(gauss_half_weights, 1.0)
    to_fine = lagrange(fine_points, gll_points)
    products = np.ones(8)
    for i in range(8):
        for k in range(8):
            if k != i:
                products[i] = products[i] * (gll_points[i] - gll_points[k])
    deriv_mat = np.zeros((8, 8))
    for i in range(8):
        for j in range(8):
            if i != j:
                deriv_mat[i, j] = products[i] / (products[j] * (gll_points[i] - gll_points[j]))
                deriv_mat[i, i] = deriv_mat[i, i] + 1.0 / (gll_points[i] - gll_points[j])
    return to_fine, to_fine @ deriv_mat, gll_weights, fine_weights


def halves(matrix):
    high = matrix.astype(ml_dtypes.bfloat16)
    low = (matrix - high.astype(np.float64)).astype(ml_dtypes.bfloat16)
    return high, low


def stack_rows(matrix):
    high, low = halves(matrix)
    return np.concatenate([high, high, low], axis=0)


def stack_columns(matrix):
    high, low = halves(matrix)
    return np.concatenate([high, high, low], axis=1)


def span_blocks(block, first, count):
    out = np.zeros((SPAN, SPAN_ELEMENTS * count))
    for e in range(SPAN_ELEMENTS):
        out[e * 8 : e * 8 + 8, e * count : (e + 1) * count] = block[first : first + count].T
    return out


@functools.cache
def matrices():
    interp, deriv, gll_w, fine_w = node_tables()
    a_both = np.concatenate([span_blocks(interp, 0, 8), span_blocks(2.0 * deriv, 0, 8)], axis=1)
    span_a = stack_rows(a_both)
    interp_b = span_blocks(interp, 8, 4)
    deriv_b = span_blocks(2.0 * deriv, 8, 4)
    none = np.zeros_like(interp_b)
    first_b = stack_rows(np.concatenate([interp_b, none, deriv_b, none], axis=1))
    second_b = stack_rows(np.concatenate([none, interp_b, none, deriv_b], axis=1))
    span_b = np.concatenate([first_b, second_b], axis=0)
    values = np.kron(interp, interp)
    plane = np.concatenate([values, np.kron(2.0 * deriv, interp), np.kron(interp, 2.0 * deriv)])
    plane = stack_columns(plane)
    values = stack_columns(values)
    back = interp.T * fine_w[None, :] / gll_w[:, None]
    plane_back = stack_columns(-np.kron(back, back))
    a_back = np.zeros((SPAN, SPAN))
    b_back = np.zeros((SPAN // 2, SPAN))
    for e in range(SPAN_ELEMENTS):
        a_back[e * 8 : e * 8 + 8, e * 8 : e * 8 + 8] = back[:, :8].T
        b_back[e * 4 : e * 4 + 4, e * 8 : e * 8 + 8] = back[:, 8:].T
    span = np.concatenate([a_back, b_back], axis=0)
    summed = span.copy()
    for e in range(SPAN_ELEMENTS):
        last, first = e * 8 + 7, (e * 8 + 8) % SPAN
        mean = 0.5 * (span[:, last] + span[:, first])
        summed[:, last] = mean
        summed[:, first] = mean
    a_back, b_back = summed[:SPAN], summed[SPAN:]
    zero_a, zero_b = np.zeros_like(a_back), np.zeros_like(b_back)
    pair_back = np.concatenate(
        [
            np.concatenate([a_back, zero_a], axis=1),
            np.concatenate([zero_a, a_back], axis=1),
            np.concatenate([b_back, zero_b], axis=1),
            np.concatenate([zero_b, b_back], axis=1),
        ],
        axis=0,
    )
    one_back = np.concatenate([a_back, b_back, zero_b], axis=0)
    return span_a, span_b, plane, values, plane_back, stack_rows(pair_back), stack_rows(one_back)


def split(x):
    high = x.astype(bf16)
    return high, (x - high.astype(f32)).astype(bf16)


def dot(a, b):
    return jnp.dot(a, b, preferred_element_type=f32)


def weak_layers(fields, inverse_heights, mats):
    span_a, span_b, plane, values, plane_back, pair_back, one_back = (m[...] for m in mats)
    count = len(fields)
    parts = [split(field) for field in fields]
    lefts = [jnp.concatenate([high, low, high], axis=1) for high, low in parts]
    spots = []
    lane = lax.broadcasted_iota(jnp.int32, (1, SPAN), 1)
    for first in range(0, count, 2):
        group = range(first, min(first + 2, count))
        for l in group:
            out = dot(lefts[l], span_a)
            spots.append((out[:, :SPAN], out[:, SPAN:], inverse_heights[l]))
        if len(group) == 2:
            out = dot(jnp.concatenate([lefts[first], lefts[first + 1]], axis=1), span_b)
            inverse = jnp.where(lane < 64, inverse_heights[first], inverse_heights[first + 1])
        else:
            out = dot(lefts[first], span_b[: 3 * SPAN])
            inverse = inverse_heights[first]
        spots.append((out[:, :SPAN], out[:, SPAN:], inverse))
    backs = []
    for first in range(0, len(spots), 2):
        group = spots[first : first + 2]
        interp, deriv, inverse = (jnp.concatenate([s[i] for s in group], axis=1) for i in range(3))
        planes, spans = [], []
        interp_parts = split(interp)
        deriv_parts = split(deriv)
        for c in range(3):
            rows = slice(c * 64, c * 64 + 64)
            high, low = interp_parts[0][rows], interp_parts[1][rows]
            planes.append(dot(plane, jnp.concatenate([high, low, high], axis=0)))
            high, low = deriv_parts[0][rows], deriv_parts[1][rows]
            spans.append(dot(values, jnp.concatenate([high, low, high], axis=0)))
        speed_x, speed_y = planes[0][:144], planes[1][:144]
        speed_z = planes[2][:144] * inverse
        outs = []
        for c in range(3):
            convect = (
                speed_x * planes[c][144:288] + speed_y * spans[c] + speed_z * planes[c][288:]
            )
            high, low = split(convect)
            outs.append(dot(plane_back, jnp.concatenate([high, low, high], axis=0)))
        out = jnp.concatenate(outs, axis=0)
        for i in range(len(group)):
            backs.append(out[:, i * SPAN : (i + 1) * SPAN])
    results = []
    place = 0
    for first in range(0, count, 2):
        size = min(2, count - first)
        joined = jnp.concatenate(backs[place : place + size + 1], axis=1)
        place += size + 1
        high, low = split(joined)
        left = jnp.concatenate([high, low, high], axis=1)
        out = dot(left, pair_back if size == 2 else one_back)
        for i in range(size):
            results.append(out[:, i * SPAN : (i + 1) * SPAN])
    return results


def join_heights(own, above, below, height, height_above, height_below, has_above, has_below):
    level = lax.broadcasted_iota(jnp.int32, (8, SPAN), 0)
    keep = jnp.ones((8, SPAN), f32)
    out = own.reshape(24, 8, SPAN)
    if above is not None:
        share = jnp.where(has_above, height_above / (height + height_above), 0.0)
        take = jnp.where(level == 7, share, 0.0)
        keep = keep - take
        taken_above = pltpu.roll(above.reshape(24, 8, SPAN), 7, 1) * take[None]
    if below is not None:
        share = jnp.where(has_below, height_below / (height + height_below), 0.0)
        take = jnp.where(level == 0, share, 0.0)
        keep = keep - take
        taken_below = pltpu.roll(below.reshape(24, 8, SPAN), 1, 1) * take[None]
    out = out * keep[None]
    if above is not None:
        out = out + taken_above
    if below is not None:
        out = out + taken_below
    return out.reshape(ROWS, SPAN)


def join_stream(own, cross, core):
    place = lax.axis_index("horiz")
    odd = lax.rem(place, 2) == 1
    left = jnp.where(odd, core, cross)
    right = jnp.where(odd, cross, core)
    left_share = jnp.where(place > 0, 0.5, 0.0).astype(f32)
    right_share = jnp.where(place < lax.axis_size("horiz") - 1, 0.5, 0.0).astype(f32)
    own = own.reshape(3, 8, 8, SPAN)
    first = own[:, 0] * (1.0 - left_share) + left * left_share
    last = own[:, 7] * (1.0 - right_share) + right * right_share
    out = jnp.concatenate([first[:, None], own[:, 1:7], last[:, None]], axis=1)
    return out.reshape(ROWS, SPAN)


def put_faces(own, cross_ref, core_ref, at):
    odd = lax.rem(lax.axis_index("horiz"), 2) == 1
    own = own.reshape(3, 8, 8, SPAN)
    first, last = own[:, 0], own[:, 7]
    cross_ref[at] = jnp.where(odd, last, first)
    core_ref[at] = jnp.where(odd, first, last)


def put_layers(results, heights, partial_ref, cross_ref, core_ref):
    count = len(results)
    for l in range(count):
        above = results[l + 1] if l + 1 < count else None
        below = results[l - 1] if l > 0 else None
        joined = join_heights(
            results[l],
            above,
            below,
            heights[l],
            heights[l + 1] if l + 1 < count else None,
            heights[l - 1] if l > 0 else None,
            True,
            True,
        )
        partial_ref[l] = joined
        put_faces(joined, cross_ref, core_ref, l)


def pack_kernel(velocity_ref, height_ref, packed_ref):
    packed_ref[:ROWS] = velocity_ref[...]
    packed_ref[ROWS:] = jnp.full((8, SPAN), height_ref[0], f32)


def own_layer_kernel(*refs):
    mats, (packed_ref, out_ref) = refs[:7], refs[7:]
    inverse = 1.0 / packed_ref[ROWS : ROWS + 1]
    out_ref[...] = weak_layers([packed_ref[:ROWS]], [inverse], mats)[0]


def other_layers_kernel(count, *refs):
    mats, refs = refs[:7], refs[7:]
    packed, done_ref = refs[:count], refs[count]
    field_ref, heights_ref, partial_ref, cross_ref, core_ref, raw_ref = refs[count + 1 :]
    place = lax.axis_index("vert")
    slots = [jnp.bitwise_xor(place, j) for j in range(count)]
    for j in range(count):
        field_ref[slots[j]] = packed[j][:ROWS]
        heights_ref[slots[j]] = packed[j][ROWS:]
    raw_ref[place] = done_ref[...]
    if count > 1:
        results = weak_layers(
            [packed[j][:ROWS] for j in range(1, count)],
            [1.0 / packed[j][ROWS : ROWS + 1] for j in range(1, count)],
            mats,
        )
        for j in range(1, count):
            raw_ref[slots[j]] = results[j - 1]
    heights = [heights_ref[l] for l in range(count)]
    put_layers([raw_ref[l] for l in range(count)], heights, partial_ref, cross_ref, core_ref)


def first_kernel(count, *refs):
    mats, refs = refs[:7], refs[7:]
    packed_ref, field_ref, heights_ref, partial_ref, cross_ref, core_ref = refs
    for l in range(count):
        field_ref[l] = packed_ref[l, :ROWS]
        heights_ref[l] = packed_ref[l, ROWS:]
    heights = [packed_ref[l, ROWS:] for l in range(count)]
    results = weak_layers(
        [packed_ref[l, :ROWS] for l in range(count)], [1.0 / h[:1] for h in heights], mats
    )
    put_layers(results, heights, partial_ref, cross_ref, core_ref)


def middle_kernel(count, step_share, first, *refs):
    mats, refs = refs[:7], refs[7:]
    step_ref, field_ref, heights_ref, partial_ref, cross_ref, core_ref = refs[:6]
    refs = refs[6:]
    if first:
        total = None
    else:
        total, refs = refs[0][...], refs[1:]
    total_ref, next_partial_ref, next_cross_ref, next_core_ref = refs
    place = lax.axis_index("vert")
    step = step_ref[0] * step_share
    own = join_stream(partial_ref[place], cross_ref[place], core_ref[place])
    total_ref[...] = own if first else total + 2.0 * own
    fields = []
    for l in range(count):
        slope = join_stream(partial_ref[l], cross_ref[l], core_ref[l])
        fields.append(field_ref[l] + step * slope)
    heights = [heights_ref[l] for l in range(count)]
    results = weak_layers(fields, [1.0 / h[:1] for h in heights], mats)
    put_layers(results, heights, next_partial_ref, next_cross_ref, next_core_ref)


def last_kernel(count, *refs):
    mats, refs = refs[:7], refs[7:]
    step_ref, field_ref, heights_ref, partial_ref, cross_ref, core_ref, total_ref = refs[:7]
    next_total_ref, next_partial_ref, next_cross_ref, next_core_ref = refs[7:]
    place = lax.axis_index("vert")
    step = step_ref[0]
    layers = [place, jnp.minimum(place + 1, count - 1), jnp.maximum(place - 1, 0)]
    fields, heights = [], []
    for l in layers:
        slope = join_stream(partial_ref[l], cross_ref[l], core_ref[l])
        if not fields:
            next_total_ref[...] = total_ref[...] + 2.0 * slope
        fields.append(field_ref[l] + step * slope)
        heights.append(heights_ref[l])
    own, above, below = weak_layers(fields, [1.0 / h[:1] for h in heights], mats)
    joined = join_heights(own, above, below, *heights, place < count - 1, place > 0)
    next_partial_ref[...] = joined
    put_faces(joined, next_cross_ref, next_core_ref, slice(None))


def rate_kernel(partial_ref, cross_ref, core_ref, total_ref, rate_ref):
    slope = join_stream(partial_ref[...], cross_ref[...], core_ref[...])
    rate_ref[...] = (total_ref[...] + slope) / 6.0


VMEM = pl.BlockSpec(memory_space=pltpu.VMEM)
SMEM = pl.BlockSpec(memory_space=pltpu.SMEM)


def call(kernel, outs, args, smem=(), scratch=(), flops=0):
    shapes = [jax.ShapeDtypeStruct(shape, f32) for shape in outs]
    one = len(shapes) == 1
    return pl.pallas_call(
        kernel,
        out_shape=shapes[0] if one else shapes,
        in_specs=[SMEM if i in smem else VMEM for i in range(len(args))],
        out_specs=VMEM if one else [VMEM] * len(shapes),
        scratch_shapes=list(scratch),
        compiler_params=pltpu.CompilerParams(vmem_limit_bytes=48 * 1024 * 1024),
        cost_estimate=pl.CostEstimate(flops=flops, bytes_accessed=1 << 20, transcendentals=0),
    )(*args)


def swap_stream(cross, core):
    count = lax.axis_size("horiz")
    cores = [(i, i ^ 1) for i in range(count)]
    crosses = [(i, (i + 1) % count if i % 2 else (i - 1) % count) for i in range(count)]
    return lax.ppermute(cross, "horiz", crosses), lax.ppermute(core, "horiz", cores)


def on_device(velocity, heights, time_step):
    layers = lax.axis_size("vert")
    mats = [jnp.asarray(m) for m in matrices()]
    unit = 2 * 256 * 256 * 3000
    field = (layers, ROWS, SPAN)
    face = (layers, 3, 8, SPAN)
    small = (3, 8, SPAN)
    first_outs = [field, (layers, 8, SPAN), field, face, face]
    step = time_step.reshape(1)
    packed = call(
        pack_kernel, [(ROWS + 8, SPAN)], [velocity.reshape(ROWS, SPAN), heights], smem=(1,)
    )
    if layers in (1, 2, 4):
        slots = [packed]
        for j in range(1, layers):
            slots.append(lax.ppermute(packed, "vert", [(i, i ^ j) for i in range(layers)]))
        own = call(own_layer_kernel, [(ROWS, SPAN)], mats + [packed], flops=unit)
        fields, all_heights, partial, cross, core = call(
            functools.partial(other_layers_kernel, layers),
            first_outs,
            mats + slots + [own],
            scratch=[pltpu.VMEM(field, f32)],
            flops=(layers - 1) * unit,
        )
    else:
        gathered = lax.all_gather(packed, "vert")
        fields, all_heights, partial, cross, core = call(
            functools.partial(first_kernel, layers), first_outs, mats + [gathered]
        )
    cross, core = swap_stream(cross, core)
    total = None
    for stage in range(2):
        args = mats + [step, fields, all_heights, partial, cross, core]
        if stage:
            args.append(total)
        total, partial, cross, core = call(
            functools.partial(middle_kernel, layers, 0.5, stage == 0),
            [(ROWS, SPAN), field, face, face],
            args,
            smem=(7,),
            flops=layers * unit,
        )
        cross, core = swap_stream(cross, core)
    total, partial, cross, core = call(
        functools.partial(last_kernel, layers),
        [(ROWS, SPAN), (ROWS, SPAN), small, small],
        mats + [step, fields, all_heights, partial, cross, core, total],
        smem=(7,),
        flops=3 * unit,
    )
    cross, core = swap_stream(cross, core)
    rate = call(rate_kernel, [(ROWS, SPAN)], [partial, cross, core, total])
    return rate.reshape(velocity.shape)


def solution(mesh):
    in_specs = (P(None, "horiz", "vert", None), P("vert"), P())
    out_specs = P(None, "horiz", "vert", None)
    return jax.shard_map(
        on_device, mesh=mesh, in_specs=in_specs, out_specs=out_specs, check_vma=False
    )
```

profile of v0, /device:TPU:0, one launch (start us, length us, event | category | flops | bytes accessed | tf_op | source)
XLA Modules:
  0.0 42.5 jit_solution(10990904359734267145)
XLA Ops:
  0.7 0.0 copy-start.9
  0.7 0.9 %copy-done.9 = f32[3,8,8,128]{3,2,1,0:T(8,128)S(1)} copy-done((f32[3,8,8,128]{3,2,1,0:T(8,128)S(1)}, f32[3,8,8,128]{3,2,1,0:T(8,128)}, u32[]{:S(2)}) %copy-start.9) | copy-done | bytes 98328
  1.6 5.1 %collective-permute-start.2 = (f32[200,128]{1,0:T(8,128)S(1)}, f32[200,128]{1,0:T(8,128)S(1)}, u32[]{:S(2)}, u32[]{:S(2)}) collective-permute-start(f32[200,128]{1,0:T(8,128)S(1)} %shard_map.100.refs_7_), channel_id=1, source_target_pairs={{0,3},{1,2},{2,1},{3,0},{4,7},{5,6},{6,5},{7,4},{8,11},{9,10},{10,... | collective-permute-start | bytes 307208 | tf_op jit(solution)/shard_map/ppermute | solution.py:406
  6.7 0.0 collective-permute-start.1
  6.7 0.6 %collective-permute-start = (f32[200,128]{1,0:T(8,128)S(1)}, f32[200,128]{1,0:T(8,128)S(1)}, u32[]{:S(2)}, u32[]{:S(2)}) collective-permute-start(f32[200,128]{1,0:T(8,128)S(1)} %shard_map.100.refs_7_), channel_id=1, source_target_pairs={{0,1},{1,0},{2,3},{3,2},{4,5},{5,4},{6,7},{7,6},{8,9},{9,8},{10,11... | collective-permute-start | bytes 307208 | tf_op jit(solution)/shard_map/ppermute | solution.py:406
  7.4 0.0 copy-done.6
  7.4 1.1 %copy-done = bf16[1152,256]{1,0:T(8,128)(2,1)S(1)} copy-done((bf16[1152,256]{1,0:T(8,128)(2,1)S(1)}, bf16[1152,256]{1,0:T(8,128)(2,1)}, u32[]{:S(2)}) %copy-start) | copy-done | bytes 589848
  8.4 1.0 %copy-done.2 = bf16[768,256]{1,0:T(8,128)(2,1)S(1)} copy-done((bf16[768,256]{1,0:T(8,128)(2,1)S(1)}, bf16[768,256]{1,0:T(8,128)(2,1)}, u32[]{:S(2)}) %copy-start.2) | copy-done | bytes 393240
  9.4 0.9 %copy-done.4 = bf16[432,192]{1,0:T(8,128)(2,1)S(1)} copy-done((bf16[432,192]{1,0:T(8,128)(2,1)S(1)}, bf16[432,192]{1,0:T(8,128)(2,1)}, u32[]{:S(2)}) %copy-start.4) | copy-done | bytes 165912
  10.4 0.9 %copy-done.7 = bf16[384,256]{1,0:T(8,128)(2,1)S(1)} copy-done((bf16[384,256]{1,0:T(8,128)(2,1)S(1)}, bf16[384,256]{1,0:T(8,128)(2,1)}, u32[]{:S(2)}) %copy-start.7) | copy-done | bytes 196632
  11.3 0.9 %copy-done.10 = bf16[144,192]{1,0:T(8,128)(2,1)S(1)} copy-done((bf16[144,192]{1,0:T(8,128)(2,1)S(1)}, bf16[144,192]{1,0:T(8,128)(2,1)}, u32[]{:S(2)}) %copy-start.10) | copy-done | bytes 55320
  12.2 0.8 %copy-done.12 = bf16[64,432]{1,0:T(8,128)(2,1)S(1)} copy-done((bf16[64,432]{1,0:T(8,128)(2,1)S(1)}, bf16[64,432]{1,0:T(8,128)(2,1)}, u32[]{:S(2)}) %copy-start.12) | copy-done | bytes 55320
  13.0 1.0 %shard_map.101.refs_11_ = f32[192,128]{1,0:T(8,128)S(1)} custom-call(bf16[384,256]{1,0:T(8,128)(2,1)S(1)} %copy-done.7, bf16[768,256]{1,0:T(8,128)(2,1)S(1)} %copy-done.2, bf16[432,192]{1,0:T(8,128)(2,1)S(1)} %copy-done.4, bf16[144,192]{1,0:T(8,128)(2,1)S(1)} %copy-done.10, bf16[64,432]{1,0:T(8,128)(2,1)S(1)} %copy-done.12, bf16[1152,256]{1,0:T(8,128)(2,1)S(1)} %copy-done, ...), custom_call_target="tpu_custom_call" | custom-call | flops 393216000 | bytes 1048576 | tf_op jit(solution)/shard_map/pallas_call | solution.py:373
  14.0 0.0 copy-start.1
  14.0 0.0 copy-start.3
  14.1 0.0 copy-start.5
  14.1 0.0 copy-start.8
  14.1 0.0 copy-start.11
  14.1 0.0 copy-start.13
  14.1 0.0 collective-permute-done.2.refs_10_
  14.1 1.2 %collective-permute-done.1.refs_9_ = f32[200,128]{1,0:T(8,128)S(1)} collective-permute-done((f32[200,128]{1,0:T(8,128)S(1)}, f32[200,128]{1,0:T(8,128)S(1)}, u32[]{:S(2)}, u32[]{:S(2)}) %collective-permute-start.1) | collective-permute-done | bytes 102432 | tf_op jit(solution)/shard_map/ppermute | solution.py:406
  15.3 0.0 collective-permute-done.refs_8_
  15.3 2.1 %shard_map.102 = (f32[4,192,128]{2,1,0:T(8,128)S(1)}, f32[4,8,128]{2,1,0:T(8,128)S(1)}, f32[4,192,128]{2,1,0:T(8,128)S(1)}, f32[4,3,8,128]{3,2,1,0:T(8,128)S(1)}, f32[4,3,8,128]{3,2,1,0:T(8,128)S(1)}) custom-call(bf16[384,256]{1,0:T(8,128)(2,1)S(1)} %copy-done.7, bf16[768,256]{1,0:T(8,128)(2,1)S(1)} %copy-done.2, bf16[432,192]{1,0:T(8,128)(2,1)S(1)} %copy-done.4, ...), custom_call_target="tpu_custom_call" | custom-call | flops 1179648000 | bytes 1048576 | tf_op jit(solution)/shard_map/pallas_call | solution.py:373
  17.5 1.3 %collective-permute-start.3 = (f32[4,3,8,128]{3,2,1,0:T(8,128)S(1)}, f32[4,3,8,128]{3,2,1,0:T(8,128)S(1)}, u32[]{:S(2)}, u32[]{:S(2)}) collective-permute-start(f32[4,3,8,128]{3,2,1,0:T(8,128)S(1)} %get-tuple-element.25), channel_id=1, source_target_pairs={{0,28},{4,8},{8,4},{12,16},{16,12},{20,24},{24,20},{28,0},{1,29},{... | collective-permute-start | bytes 147464 | tf_op jit(solution)/shard_map/ppermute | solution.py:388
  18.7 0.4 collective-permute-start.4
  19.8 2.6 %collective-permute-done.3.refs_11_ = f32[4,3,8,128]{3,2,1,0:T(8,128)S(1)} collective-permute-done((f32[4,3,8,128]{3,2,1,0:T(8,128)S(1)}, f32[4,3,8,128]{3,2,1,0:T(8,128)S(1)}, u32[]{:S(2)}, u32[]{:S(2)}) %collective-permute-start.3) | collective-permute-done | bytes 49184 | tf_op jit(solution)/shard_map/ppermute | solution.py:388
  22.4 0.0 collective-permute-done.4.refs_12_
  22.4 0.0 copy-done.1
  22.4 0.0 copy-done.3
  22.4 0.0 copy-done.5
  22.4 0.0 copy-done.8
  22.4 0.0 copy-done.11
  22.4 2.2 %shard_map.103 = (f32[192,128]{1,0:T(8,128)S(1)}, f32[4,192,128]{2,1,0:T(8,128)S(1)}, f32[4,3,8,128]{3,2,1,0:T(8,128)S(1)}, f32[4,3,8,128]{3,2,1,0:T(8,128)S(1)}) custom-call(bf16[384,256]{1,0:T(8,128)(2,1)S(1)} %copy-done.8, bf16[768,256]{1,0:T(8,128)(2,1)S(1)} %copy-done.3, bf16[432,192]{1,0:T(8,128)(2,1)S(1)} %copy-done.5, ...), custom_call_target="tpu_custom_call" | custom-call | flops 1572864000 | bytes 1048576 | tf_op jit(solution)/shard_map/pallas_call | solution.py:373
  24.6 1.1 %collective-permute-start.5 = (f32[4,3,8,128]{3,2,1,0:T(8,128)S(1)}, f32[4,3,8,128]{3,2,1,0:T(8,128)S(1)}, u32[]{:S(2)}, u32[]{:S(2)}) collective-permute-start(f32[4,3,8,128]{3,2,1,0:T(8,128)S(1)} %get-tuple-element.28), channel_id=1, source_target_pairs={{0,28},{4,8},{8,4},{12,16},{16,12},{20,24},{24,20},{28,0},{1,29},{... | collective-permute-start | bytes 147464 | tf_op jit(solution)/shard_map/ppermute | solution.py:388
  25.7 0.0 collective-permute-start.6
  25.7 3.4 %collective-permute-done.5.refs_11_ = f32[4,3,8,128]{3,2,1,0:T(8,128)S(1)} collective-permute-done((f32[4,3,8,128]{3,2,1,0:T(8,128)S(1)}, f32[4,3,8,128]{3,2,1,0:T(8,128)S(1)}, u32[]{:S(2)}, u32[]{:S(2)}) %collective-permute-start.5) | collective-permute-done | bytes 49184 | tf_op jit(solution)/shard_map/ppermute | solution.py:388
  29.1 0.0 collective-permute-done.6.refs_12_
  29.1 2.2 %shard_map.104 = (f32[192,128]{1,0:T(8,128)S(1)}, f32[4,192,128]{2,1,0:T(8,128)S(1)}, f32[4,3,8,128]{3,2,1,0:T(8,128)S(1)}, f32[4,3,8,128]{3,2,1,0:T(8,128)S(1)}) custom-call(bf16[384,256]{1,0:T(8,128)(2,1)S(1)} %copy-done.8, bf16[768,256]{1,0:T(8,128)(2,1)S(1)} %copy-done.3, bf16[432,192]{1,0:T(8,128)(2,1)S(1)} %copy-done.5, ...), custom_call_target="tpu_custom_call" | custom-call | flops 1572864000 | bytes 1048576 | tf_op jit(solution)/shard_map/pallas_call | solution.py:373
  31.3 1.1 %collective-permute-start.7 = (f32[4,3,8,128]{3,2,1,0:T(8,128)S(1)}, f32[4,3,8,128]{3,2,1,0:T(8,128)S(1)}, u32[]{:S(2)}, u32[]{:S(2)}) collective-permute-start(f32[4,3,8,128]{3,2,1,0:T(8,128)S(1)} %get-tuple-element.32), channel_id=1, source_target_pairs={{0,28},{4,8},{8,4},{12,16},{16,12},{20,24},{24,20},{28,0},{1,29},{... | collective-permute-start | bytes 147464 | tf_op jit(solution)/shard_map/ppermute | solution.py:388
  32.4 0.0 collective-permute-start.8
  32.4 3.4 %collective-permute-done.7.refs_11_ = f32[4,3,8,128]{3,2,1,0:T(8,128)S(1)} collective-permute-done((f32[4,3,8,128]{3,2,1,0:T(8,128)S(1)}, f32[4,3,8,128]{3,2,1,0:T(8,128)S(1)}, u32[]{:S(2)}, u32[]{:S(2)}) %collective-permute-start.7) | collective-permute-done | bytes 49184 | tf_op jit(solution)/shard_map/ppermute | solution.py:388
  35.8 0.0 collective-permute-done.8.refs_12_
  35.8 2.0 %shard_map.105 = (f32[192,128]{1,0:T(8,128)S(1)}, f32[192,128]{1,0:T(8,128)S(1)}, f32[3,8,128]{2,1,0:T(8,128)S(1)}, f32[3,8,128]{2,1,0:T(8,128)S(1)}) custom-call(bf16[384,256]{1,0:T(8,128)(2,1)S(1)} %copy-done.8, bf16[768,256]{1,0:T(8,128)(2,1)S(1)} %copy-done.3, bf16[432,192]{1,0:T(8,128)(2,1)S(1)} %copy-done.5, bf16[144,192]{1,0:T(8,128)(2,1)S(1)} %copy-done.11, ...), custom_call_target="tpu_custom_call" | custom-call | flops 1179648000 | bytes 1048576 | tf_op jit(solution)/shard_map/pallas_call | solution.py:373
  37.8 1.1 %collective-permute-start.9 = (f32[3,8,128]{2,1,0:T(8,128)S(1)}, f32[3,8,128]{2,1,0:T(8,128)S(1)}, u32[]{:S(2)}, u32[]{:S(2)}) collective-permute-start(f32[3,8,128]{2,1,0:T(8,128)S(1)} %get-tuple-element.36), channel_id=1, source_target_pairs={{0,28},{4,8},{8,4},{12,16},{16,12},{20,24},{24,20},{28,0},{1,29},{... | collective-permute-start | bytes 36872 | tf_op jit(solution)/shard_map/ppermute | solution.py:388
  38.8 0.0 collective-permute-start.10
  38.8 3.0 %collective-permute-done.9.cross_ref = f32[3,8,128]{2,1,0:T(8,128)S(1)} collective-permute-done((f32[3,8,128]{2,1,0:T(8,128)S(1)}, f32[3,8,128]{2,1,0:T(8,128)S(1)}, u32[]{:S(2)}, u32[]{:S(2)}) %collective-permute-start.9) | collective-permute-done | bytes 12320 | tf_op jit(solution)/shard_map/ppermute | solution.py:388
  41.8 0.0 collective-permute-done.10.core_ref
  41.9 0.7 %shard_map.106 = f32[192,128]{1,0:T(8,128)} custom-call(f32[192,128]{1,0:T(8,128)S(1)} %get-tuple-element.35.partial_ref, f32[3,8,128]{2,1,0:T(8,128)S(1)} %collective-permute-done.9.cross_ref, f32[3,8,128]{2,1,0:T(8,128)S(1)} %collective-permute-done.10.core_ref, f32[192,128]{1,0:T(8,128)S(1)} %get-tuple-element.38.total_ref), custom_call_target="tpu_custom_call" | custom-call | bytes 1048576 | tf_op jit(solution)/shard_map/pallas_call | solution.py:373
  (9 shorter events, 0.0 us)
Async XLA Ops:
  0.0 7.4 %copy-start.6 = (bf16[768,128]{1,0:T(8,128)(2,1)S(1)}, bf16[768,128]{1,0:T(8,128)(2,1)}, u32[]{:S(2)}) copy-start(bf16[768,128]{1,0:T(8,128)(2,1)} %constant.20.clone.refs_6_) | copy-start | bytes 589828
  0.7 0.9 %copy-start.9 = (f32[3,8,8,128]{3,2,1,0:T(8,128)S(1)}, f32[3,8,8,128]{3,2,1,0:T(8,128)}, u32[]{:S(2)}) copy-start(f32[3,8,8,128]{3,2,1,0:T(8,128)} %param.10) | copy-start | bytes 294916
  1.6 12.5 %collective-permute-start.2 = (f32[200,128]{1,0:T(8,128)S(1)}, f32[200,128]{1,0:T(8,128)S(1)}, u32[]{:S(2)}, u32[]{:S(2)}) collective-permute-start(f32[200,128]{1,0:T(8,128)S(1)} %shard_map.100.refs_7_), channel_id=1, source_target_pairs={{0,3},{1,2},{2,1},{3,0},{4,7},{5,6},{6,5},{7,4},{8,11},{9,10},{10,... | collective-permute-start | bytes 307208 | tf_op jit(solution)/shard_map/ppermute | solution.py:406
  6.7 8.6 %collective-permute-start.1 = (f32[200,128]{1,0:T(8,128)S(1)}, f32[200,128]{1,0:T(8,128)S(1)}, u32[]{:S(2)}, u32[]{:S(2)}) collective-permute-start(f32[200,128]{1,0:T(8,128)S(1)} %shard_map.100.refs_7_), channel_id=1, source_target_pairs={{0,2},{1,3},{2,0},{3,1},{4,6},{5,7},{6,4},{7,5},{8,10},{9,11},{10,... | collective-permute-start | bytes 307208 | tf_op jit(solution)/shard_map/ppermute | solution.py:406
  6.7 8.6 %collective-permute-start = (f32[200,128]{1,0:T(8,128)S(1)}, f32[200,128]{1,0:T(8,128)S(1)}, u32[]{:S(2)}, u32[]{:S(2)}) collective-permute-start(f32[200,128]{1,0:T(8,128)S(1)} %shard_map.100.refs_7_), channel_id=1, source_target_pairs={{0,1},{1,0},{2,3},{3,2},{4,5},{5,4},{6,7},{7,6},{8,9},{9,8},{10,11... | collective-permute-start | bytes 307208 | tf_op jit(solution)/shard_map/ppermute | solution.py:406
  7.4 1.1 %copy-start = (bf16[1152,256]{1,0:T(8,128)(2,1)S(1)}, bf16[1152,256]{1,0:T(8,128)(2,1)}, u32[]{:S(2)}) copy-start(bf16[1152,256]{1,0:T(8,128)(2,1)} %constant.19.clone.refs_5_) | copy-start | bytes 1769476
  8.4 1.0 %copy-start.2 = (bf16[768,256]{1,0:T(8,128)(2,1)S(1)}, bf16[768,256]{1,0:T(8,128)(2,1)}, u32[]{:S(2)}) copy-start(bf16[768,256]{1,0:T(8,128)(2,1)} %constant.15.clone.refs_1_) | copy-start | bytes 1179652
  9.4 0.9 %copy-start.4 = (bf16[432,192]{1,0:T(8,128)(2,1)S(1)}, bf16[432,192]{1,0:T(8,128)(2,1)}, u32[]{:S(2)}) copy-start(bf16[432,192]{1,0:T(8,128)(2,1)} %constant.16.clone.refs_2_) | copy-start | bytes 497668
  10.4 0.9 %copy-start.7 = (bf16[384,256]{1,0:T(8,128)(2,1)S(1)}, bf16[384,256]{1,0:T(8,128)(2,1)}, u32[]{:S(2)}) copy-start(bf16[384,256]{1,0:T(8,128)(2,1)} %constant.14.clone.refs_0_) | copy-start | bytes 589828
  11.3 0.9 %copy-start.10 = (bf16[144,192]{1,0:T(8,128)(2,1)S(1)}, bf16[144,192]{1,0:T(8,128)(2,1)}, u32[]{:S(2)}) copy-start(bf16[144,192]{1,0:T(8,128)(2,1)} %constant.17.clone.refs_3_) | copy-start | bytes 165892
  12.2 0.8 %copy-start.12 = (bf16[64,432]{1,0:T(8,128)(2,1)S(1)}, bf16[64,432]{1,0:T(8,128)(2,1)}, u32[]{:S(2)}) copy-start(bf16[64,432]{1,0:T(8,128)(2,1)} %constant.18.clone.refs_4_) | copy-start | bytes 165892
  14.0 8.3 %copy-start.1 = (bf16[1152,256]{1,0:T(8,128)(2,1)S(1)}, bf16[1152,256]{1,0:T(8,128)(2,1)}, u32[]{:S(2)}) copy-start(bf16[1152,256]{1,0:T(8,128)(2,1)} %constant.19.clone.refs_5_) | copy-start | bytes 1769476
  14.0 8.3 %copy-start.3 = (bf16[768,256]{1,0:T(8,128)(2,1)S(1)}, bf16[768,256]{1,0:T(8,128)(2,1)}, u32[]{:S(2)}) copy-start(bf16[768,256]{1,0:T(8,128)(2,1)} %constant.15.clone.refs_1_) | copy-start | bytes 1179652
  14.1 8.3 %copy-start.5 = (bf16[432,192]{1,0:T(8,128)(2,1)S(1)}, bf16[432,192]{1,0:T(8,128)(2,1)}, u32[]{:S(2)}) copy-start(bf16[432,192]{1,0:T(8,128)(2,1)} %constant.16.clone.refs_2_) | copy-start | bytes 497668
  14.1 8.3 %copy-start.8 = (bf16[384,256]{1,0:T(8,128)(2,1)S(1)}, bf16[384,256]{1,0:T(8,128)(2,1)}, u32[]{:S(2)}) copy-start(bf16[384,256]{1,0:T(8,128)(2,1)} %constant.14.clone.refs_0_) | copy-start | bytes 589828
  14.1 8.3 %copy-start.11 = (bf16[144,192]{1,0:T(8,128)(2,1)S(1)}, bf16[144,192]{1,0:T(8,128)(2,1)}, u32[]{:S(2)}) copy-start(bf16[144,192]{1,0:T(8,128)(2,1)} %constant.17.clone.refs_3_) | copy-start | bytes 165892
  14.1 8.3 %copy-start.13 = (bf16[64,432]{1,0:T(8,128)(2,1)S(1)}, bf16[64,432]{1,0:T(8,128)(2,1)}, u32[]{:S(2)}) copy-start(bf16[64,432]{1,0:T(8,128)(2,1)} %constant.18.clone.refs_4_) | copy-start | bytes 165892
  17.5 4.9 %collective-permute-start.3 = (f32[4,3,8,128]{3,2,1,0:T(8,128)S(1)}, f32[4,3,8,128]{3,2,1,0:T(8,128)S(1)}, u32[]{:S(2)}, u32[]{:S(2)}) collective-permute-start(f32[4,3,8,128]{3,2,1,0:T(8,128)S(1)} %get-tuple-element.25), channel_id=1, source_target_pairs={{0,28},{4,8},{8,4},{12,16},{16,12},{20,24},{24,20},{28,0},{1,29},{... | collective-permute-start | bytes 147464 | tf_op jit(solution)/shard_map/ppermute | solution.py:388
  18.7 3.6 %collective-permute-start.4 = (f32[4,3,8,128]{3,2,1,0:T(8,128)S(1)}, f32[4,3,8,128]{3,2,1,0:T(8,128)S(1)}, u32[]{:S(2)}, u32[]{:S(2)}) collective-permute-start(f32[4,3,8,128]{3,2,1,0:T(8,128)S(1)} %get-tuple-element.26), channel_id=1, source_target_pairs={{0,4},{4,0},{8,12},{12,8},{16,20},{20,16},{24,28},{28,24},{1,5},{5... | collective-permute-start | bytes 147464 | tf_op jit(solution)/shard_map/ppermute | solution.py:388
  24.6 4.5 %collective-permute-start.5 = (f32[4,3,8,128]{3,2,1,0:T(8,128)S(1)}, f32[4,3,8,128]{3,2,1,0:T(8,128)S(1)}, u32[]{:S(2)}, u32[]{:S(2)}) collective-permute-start(f32[4,3,8,128]{3,2,1,0:T(8,128)S(1)} %get-tuple-element.28), channel_id=1, source_target_pairs={{0,28},{4,8},{8,4},{12,16},{16,12},{20,24},{24,20},{28,0},{1,29},{... | collective-permute-start | bytes 147464 | tf_op jit(solution)/shard_map/ppermute | solution.py:388
  25.7 3.4 %collective-permute-start.6 = (f32[4,3,8,128]{3,2,1,0:T(8,128)S(1)}, f32[4,3,8,128]{3,2,1,0:T(8,128)S(1)}, u32[]{:S(2)}, u32[]{:S(2)}) collective-permute-start(f32[4,3,8,128]{3,2,1,0:T(8,128)S(1)} %get-tuple-element.29), channel_id=1, source_target_pairs={{0,4},{4,0},{8,12},{12,8},{16,20},{20,16},{24,28},{28,24},{1,5},{5... | collective-permute-start | bytes 147464 | tf_op jit(solution)/shard_map/ppermute | solution.py:388
  31.3 4.5 %collective-permute-start.7 = (f32[4,3,8,128]{3,2,1,0:T(8,128)S(1)}, f32[4,3,8,128]{3,2,1,0:T(8,128)S(1)}, u32[]{:S(2)}, u32[]{:S(2)}) collective-permute-start(f32[4,3,8,128]{3,2,1,0:T(8,128)S(1)} %get-tuple-element.32), channel_id=1, source_target_pairs={{0,28},{4,8},{8,4},{12,16},{16,12},{20,24},{24,20},{28,0},{1,29},{... | collective-permute-start | bytes 147464 | tf_op jit(solution)/shard_map/ppermute | solution.py:388
  32.4 3.4 %collective-permute-start.8 = (f32[4,3,8,128]{3,2,1,0:T(8,128)S(1)}, f32[4,3,8,128]{3,2,1,0:T(8,128)S(1)}, u32[]{:S(2)}, u32[]{:S(2)}) collective-permute-start(f32[4,3,8,128]{3,2,1,0:T(8,128)S(1)} %get-tuple-element.33), channel_id=1, source_target_pairs={{0,4},{4,0},{8,12},{12,8},{16,20},{20,16},{24,28},{28,24},{1,5},{5... | collective-permute-start | bytes 147464 | tf_op jit(solution)/shard_map/ppermute | solution.py:388
  37.8 4.1 %collective-permute-start.9 = (f32[3,8,128]{2,1,0:T(8,128)S(1)}, f32[3,8,128]{2,1,0:T(8,128)S(1)}, u32[]{:S(2)}, u32[]{:S(2)}) collective-permute-start(f32[3,8,128]{2,1,0:T(8,128)S(1)} %get-tuple-element.36), channel_id=1, source_target_pairs={{0,28},{4,8},{8,4},{12,16},{16,12},{20,24},{24,20},{28,0},{1,29},{... | collective-permute-start | bytes 36872 | tf_op jit(solution)/shard_map/ppermute | solution.py:388
  38.8 3.0 %collective-permute-start.10 = (f32[3,8,128]{2,1,0:T(8,128)S(1)}, f32[3,8,128]{2,1,0:T(8,128)S(1)}, u32[]{:S(2)}, u32[]{:S(2)}) collective-permute-start(f32[3,8,128]{2,1,0:T(8,128)S(1)} %get-tuple-element.37), channel_id=1, source_target_pairs={{0,4},{4,0},{8,12},{12,8},{16,20},{20,16},{24,28},{28,24},{1,5},{5... | collective-permute-start | bytes 36872 | tf_op jit(solution)/shard_map/ppermute | solution.py:388
where the time goes:
time: 42.9 us; the launch traced here: 42.5 us
  waiting for transfers between devices  13.6 us (32%)
  starting transfers between devices  10.7 us (25%)
  Pallas kernels  10.1 us (24%)
  local copies, waits for them, and re-layouts  6.57 us (15%)
  between operations  1.5 us (3%)
    ppermute x4, waiting for transfers between devices, swap_stream(): lax.ppermute(cross, 'horiz', crosses)  12.4 us
    pallas_call x7, Pallas kernels, call(): pl.pallas_call(kernel, out_shape=shapes[0] if one else shapes, in_specs=[...  10.1 us
    unnamed x28, local copies, waits for them, and re-layouts  6.57 us
    ppermute x3, starting transfers between devices, on_device(): lax.ppermute(packed, 'vert', [(i, i ^ j) for i in range(layers)])  5.76 us
    ppermute x4, starting transfers between devices, swap_stream(): lax.ppermute(cross, 'horiz', crosses)  4.51 us
    ppermute x3, waiting for transfers between devices, on_device(): lax.ppermute(packed, 'vert', [(i, i ^ j) for i in range(layers)])  1.22 us
  transfers between devices with their start and end apart: 11, of which 5 were waited for; matrix products, arithmetic and copies ran while one was open for 0% of the time, Pallas kernels for 2%

commit v1 on v0

v1 whole, which is shorter than its diff:
```python
import functools

import jax
import jax.numpy as jnp
import ml_dtypes
import numpy as np
from jax import lax
from jax.experimental import pallas as pl
from jax.experimental.pallas import tpu as pltpu
from jax.sharding import PartitionSpec as P

gll_half = [1.0, 0.8717401485096066, 0.5917001814331423, 0.2092992179024789]
gll_half_weights = [
    0.03571428571428571,
    0.21070422714350603,
    0.34112269248350435,
    0.4124587946587038,
]
gauss_half = [
    0.9815606342467192,
    0.9041172563704749,
    0.7699026741943047,
    0.5873179542866175,
    0.3678314989981802,
    0.1252334085114689,
]
gauss_half_weights = [
    0.0471753363865118,
    0.1069393259953184,
    0.1600783285433462,
    0.2031674267230659,
    0.2334925365383548,
    0.2491470458134028,
]

f32 = jnp.float32
bf16 = jnp.bfloat16
ROWS = 192
SPAN = 128
SPAN_ELEMENTS = 16


def mirrored(values, sign):
    return np.concatenate([sign * np.array(values), np.array(values[::-1])])


def lagrange(targets, sources):
    matrix = np.ones((targets.size, sources.size))
    for j in range(sources.size):
        for k in range(sources.size):
            if k != j:
                matrix[:, j] = matrix[:, j] * (targets - sources[k]) / (sources[j] - sources[k])
    return matrix


def node_tables():
    gll_points = mirrored(gll_half, -1.0)
    gll_weights = mirrored(gll_half_weights, 1.0)
    fine_points = mirrored(gauss_half, -1.0)
    fine_weights = mirrored(gauss_half_weights, 1.0)
    to_fine = lagrange(fine_points, gll_points)
    products = np.ones(8)
    for i in range(8):
        for k in range(8):
            if k != i:
                products[i] = products[i] * (gll_points[i] - gll_points[k])
    deriv_mat = np.zeros((8, 8))
    for i in range(8):
        for j in range(8):
            if i != j:
                deriv_mat[i, j] = products[i] / (products[j] * (gll_points[i] - gll_points[j]))
                deriv_mat[i, i] = deriv_mat[i, i] + 1.0 / (gll_points[i] - gll_points[j])
    return to_fine, to_fine @ deriv_mat, gll_weights, fine_weights


def halves(matrix):
    high = matrix.astype(ml_dtypes.bfloat16)
    low = (matrix - high.astype(np.float64)).astype(ml_dtypes.bfloat16)
    return high, low


def stack_columns(matrix):
    high, low = halves(matrix)
    return np.concatenate([high, high, low], axis=1)


def span_blocks(block, first, count):
    out = np.zeros((SPAN, SPAN_ELEMENTS * count))
    for e in range(SPAN_ELEMENTS):
        out[e * 8 : e * 8 + 8, e * count : (e + 1) * count] = block[first : first + count].T
    return out


@functools.cache
def matrices():
    interp, deriv, gll_w, fine_w = node_tables()
    a_both = np.concatenate([span_blocks(interp, 0, 8), span_blocks(2.0 * deriv, 0, 8)], axis=1)
    span_a = np.concatenate(halves(a_both), axis=0)
    interp_b = span_blocks(interp, 8, 4)
    deriv_b = span_blocks(2.0 * deriv, 8, 4)
    none = np.zeros_like(interp_b)
    first_b = halves(np.concatenate([interp_b, none, deriv_b, none], axis=1))
    second_b = halves(np.concatenate([none, interp_b, none, deriv_b], axis=1))
    span_b = np.concatenate(first_b + second_b, axis=0)
    values = np.kron(interp, interp)
    plane = np.concatenate([values, np.kron(2.0 * deriv, interp), np.kron(interp, 2.0 * deriv)])
    plane = stack_columns(plane)
    values = stack_columns(values)
    back = interp.T * fine_w[None, :] / gll_w[:, None]
    plane_back = stack_columns(-np.kron(back, back))
    a_back = np.zeros((SPAN, SPAN))
    b_back = np.zeros((SPAN // 2, SPAN))
    for e in range(SPAN_ELEMENTS):
        a_back[e * 8 : e * 8 + 8, e * 8 : e * 8 + 8] = back[:, :8].T
        b_back[e * 4 : e * 4 + 4, e * 8 : e * 8 + 8] = back[:, 8:].T
    span = np.concatenate([a_back, b_back], axis=0)
    summed = span.copy()
    for e in range(SPAN_ELEMENTS):
        last, first = e * 8 + 7, (e * 8 + 8) % SPAN
        mean = 0.5 * (span[:, last] + span[:, first])
        summed[:, last] = mean
        summed[:, first] = mean
    a_back, b_back = summed[:SPAN], summed[SPAN:]
    zero_a, zero_b = np.zeros_like(a_back), np.zeros_like(b_back)
    pair_back = np.concatenate(
        [
            np.concatenate([a_back, zero_a], axis=1),
            np.concatenate([zero_a, a_back], axis=1),
            np.concatenate([b_back, zero_b], axis=1),
            np.concatenate([zero_b, b_back], axis=1),
        ],
        axis=0,
    )
    wide = {
        "span_a": span_a,
        "span_b": span_b,
        "plane": plane,
        "values": values,
        "plane_back": plane_back[:, :256],
        "plane_back_rest": plane_back[:, 256:],
        "pair_back": np.concatenate(halves(pair_back), axis=0),
    }
    rows, places = [], {}
    start = 0
    for name, matrix in wide.items():
        places[name] = (start, matrix.shape[0], matrix.shape[1])
        rows.append(np.pad(matrix, ((0, 0), (0, 256 - matrix.shape[1]))))
        start += matrix.shape[0]
    return np.concatenate(rows, axis=0), places


def read(mats_ref, name):
    start, count, width = matrices()[1][name]
    return mats_ref[start : start + count, :width]


def read_rows(mats_ref, name, *pieces):
    start, count, width = matrices()[1][name]
    half = count // 2
    out = []
    for offset in (0, 0, half):
        for first, rows in pieces:
            at = start + offset + first
            out.append(mats_ref[at : at + rows, :width])
    return jnp.concatenate(out, axis=0)


def read_span_a(mats_ref):
    return read_rows(mats_ref, "span_a", (0, SPAN))


def read_span_b(mats_ref):
    start = matrices()[1]["span_b"][0]
    order = (0, 0, 1, 2, 2, 3)
    return jnp.concatenate(
        [mats_ref[start + i * SPAN : start + i * SPAN + SPAN] for i in order], axis=0
    )


def read_back(mats_ref, size):
    if size == 2:
        return read_rows(mats_ref, "pair_back", (0, 3 * SPAN))
    return read_rows(mats_ref, "pair_back", (0, SPAN), (2 * SPAN, SPAN))[:, :SPAN]


def split(x):
    high = x.astype(bf16)
    return high, (x - high.astype(f32)).astype(bf16)


def dot(a, b):
    return jnp.dot(a, b, preferred_element_type=f32)


def triple(x, axis):
    high, low = split(x)
    return jnp.concatenate([high, low, high], axis=axis)


def spots_of(count):
    spots = []
    for first in range(0, count, 2):
        group = tuple(range(first, min(first + 2, count)))
        spots += [(l,) for l in group] + [group + (None,) * (3 - len(group))]
    return spots


def chunks_of(count):
    spots = spots_of(count)
    return [spots[first : first + 2] for first in range(0, len(spots), 2)]


def span_forward(fields, mats):
    span_a, span_b = read_span_a(mats), read_span_b(mats)
    lefts = [triple(field, 1) for field in fields]
    spots = []
    for spot in spots_of(len(fields)):
        if len(spot) == 1:
            out = dot(lefts[spot[0]], span_a)
        elif spot[1] is None:
            out = dot(lefts[spot[0]], span_b[: 3 * SPAN])
        else:
            out = dot(jnp.concatenate([lefts[spot[0]], lefts[spot[1]]], axis=1), span_b)
        spots.append((out[:, :SPAN], out[:, SPAN:]))
    return spots


def plane_forward(spots, mats):
    plane, values = read(mats, "plane"), read(mats, "values")
    interp, deriv = (jnp.concatenate([s[i] for s in spots], axis=1) for i in range(2))
    interp, deriv = split(interp), split(deriv)
    outs = []
    for c in range(3):
        rows = slice(c * 64, c * 64 + 64)
        high, low = interp[0][rows], interp[1][rows]
        first = dot(plane, jnp.concatenate([high, low, high], axis=0))
        high, low = deriv[0][rows], deriv[1][rows]
        outs.append((first, dot(values, jnp.concatenate([high, low, high], axis=0))))
    return outs


def chunk_inverse(chunk, inverses):
    lane = lax.broadcasted_iota(jnp.int32, (1, SPAN), 1)
    out = []
    for spot in chunk:
        if len(spot) == 1 or spot[1] is None:
            out.append(inverses[spot[0]])
        else:
            out.append(jnp.where(lane < 64, inverses[spot[0]], inverses[spot[1]]))
    return jnp.concatenate(out, axis=1)


def convect_back(fine, inverse, mats):
    back = jnp.concatenate([read(mats, "plane_back"), read(mats, "plane_back_rest")], axis=1)
    parts = [([], []) for _ in range(3)]
    for first in range(0, 144, 48):
        rows = slice(first, first + 48)
        speeds = [fine(c, 0, rows) for c in range(3)]
        speeds[2] = speeds[2] * inverse
        for c in range(3):
            convect = (
                speeds[0] * fine(c, 1, rows)
                + speeds[1] * fine(c, 3, rows)
                + speeds[2] * fine(c, 2, rows)
            )
            for part, half in zip(parts[c], split(convect)):
                part.append(half)
    outs = []
    for high, low in parts:
        outs.append(dot(back, jnp.concatenate(high + low + high, axis=0)))
    return jnp.concatenate(outs, axis=0)


def span_back(count, backs, results, mats):
    for place, spot in enumerate(spots_of(count)):
        if len(spot) == 1 or place >= len(backs) or spot[0] < len(results):
            continue
        size = 1 if spot[1] is None else 2
        joined = jnp.concatenate(backs[place - size : place + 1], axis=1)
        out = dot(triple(joined, 1), read_back(mats, size))
        results += [out[:, i * SPAN : (i + 1) * SPAN] for i in range(size)]


def weak_layers(fields, inverses, mats):
    return weak_spots(span_forward(fields, mats), inverses, mats)


def weak_spots(spots, inverses, mats):
    count = len(inverses)
    chunks = chunks_of(count)
    planes = []
    backs, results = [], []

    def finish(i):
        def fine(c, kind, rows):
            first, along_y = planes[i][c]
            if kind == 3:
                return along_y[rows]
            return first[kind * 144 + rows.start : kind * 144 + rows.stop]

        out = convect_back(fine, chunk_inverse(chunks[i], inverses), mats)
        backs.extend(out[:, j * SPAN : (j + 1) * SPAN] for j in range(len(chunks[i])))
        span_back(count, backs, results, mats)

    for i in range(len(chunks)):
        planes.append(plane_forward(spots[2 * i : 2 * i + 2], mats))
        if i > 0:
            finish(i - 1)
    finish(len(chunks) - 1)
    return results


def face_spots(faces, mats):
    out_a = dot(triple(jnp.concatenate(faces, axis=0), 1), read_span_a(mats))
    even, odd = faces[0::2], faces[1::2]
    odd = odd + [jnp.zeros_like(faces[0])] * (len(even) - len(odd))
    even, odd = (triple(jnp.concatenate(x, axis=0), 1) for x in (even, odd))
    out_b = dot(jnp.concatenate([even, odd], axis=1), read_span_b(mats))
    spots = []
    for spot in spots_of(len(faces)):
        if len(spot) == 1:
            out = out_a[spot[0] * 48 : spot[0] * 48 + 48]
        else:
            out = out_b[spot[0] * 24 : spot[0] * 24 + 48]
        spots.append((out[:, :SPAN], out[:, SPAN:]))
    return spots


def with_faces(inner, faces):
    inner = inner.reshape(3, 6, 8, SPAN)
    faces = faces.reshape(3, 2, 8, SPAN)
    return jnp.concatenate([faces[:, :1], inner, faces[:, 1:]], axis=1).reshape(ROWS, SPAN)


def join_heights(own, above, below, height, height_above, height_below, has_above, has_below):
    level = lax.broadcasted_iota(jnp.int32, (8, SPAN), 0)
    keep = jnp.ones((8, SPAN), f32)
    out = own.reshape(24, 8, SPAN)
    if above is not None:
        share = jnp.where(has_above, height_above / (height + height_above), 0.0)
        take = jnp.where(level == 7, share, 0.0)
        keep = keep - take
        taken_above = pltpu.roll(above.reshape(24, 8, SPAN), 7, 1) * take[None]
    if below is not None:
        share = jnp.where(has_below, height_below / (height + height_below), 0.0)
        take = jnp.where(level == 0, share, 0.0)
        keep = keep - take
        taken_below = pltpu.roll(below.reshape(24, 8, SPAN), 1, 1) * take[None]
    out = out * keep[None]
    if above is not None:
        out = out + taken_above
    if below is not None:
        out = out + taken_below
    return out.reshape(ROWS, SPAN)


def sides():
    place = lax.axis_index("horiz")
    left_share = jnp.where(place > 0, 0.5, 0.0).astype(f32)
    right_share = jnp.where(place < lax.axis_size("horiz") - 1, 0.5, 0.0).astype(f32)
    return lax.rem(place, 2) == 1, left_share, right_share


def join_ends(own, cross, core):
    odd, left_share, right_share = sides()
    left = jnp.where(odd, core, cross)
    right = jnp.where(odd, cross, core)
    own = own.reshape(3, 8, 8, SPAN)
    first = own[:, 0] * (1.0 - left_share) + left * left_share
    last = own[:, 7] * (1.0 - right_share) + right * right_share
    return first, last


def join_stream(own, cross, core):
    first, last = join_ends(own, cross, core)
    own = own.reshape(3, 8, 8, SPAN)
    out = jnp.concatenate([first[:, None], own[:, 1:7], last[:, None]], axis=1)
    return out.reshape(ROWS, SPAN)


def put_faces(own, cross_ref, core_ref, at):
    odd = lax.rem(lax.axis_index("horiz"), 2) == 1
    own = own.reshape(3, 8, 8, SPAN)
    first, last = own[:, 0], own[:, 7]
    cross_ref[at] = jnp.where(odd, last, first)
    core_ref[at] = jnp.where(odd, first, last)


def put_layers(results, heights, partial_ref, cross_ref, core_ref):
    count = len(results)
    for l in range(count):
        above = results[l + 1] if l + 1 < count else None
        below = results[l - 1] if l > 0 else None
        joined = join_heights(
            results[l],
            above,
            below,
            heights[l],
            heights[l + 1] if l + 1 < count else None,
            heights[l - 1] if l > 0 else None,
            True,
            True,
        )
        partial_ref[l] = joined
        put_faces(joined, cross_ref, core_ref, l)


def pack_kernel(velocity_ref, height_ref, packed_ref):
    packed_ref[:ROWS] = velocity_ref[...]
    packed_ref[ROWS:] = jnp.broadcast_to(height_ref[...], (8, SPAN))


def own_layer_kernel(mats, packed_ref, step_ref, out_ref, step_tile_ref):
    inverse = 1.0 / packed_ref[ROWS : ROWS + 1]
    out_ref[...] = weak_layers([packed_ref[:ROWS]], [inverse], mats)[0]
    step_tile_ref[...] = jnp.broadcast_to(step_ref[...], (8, SPAN))


def other_layers_kernel(count, *refs):
    mats, packed, done_ref, refs = refs[0], refs[1 : count + 1], refs[count + 1], refs[count + 2 :]
    field_ref, heights_ref, partial_ref, cross_ref, core_ref, raw_ref = refs
    place = lax.axis_index("vert")
    slots = [jnp.bitwise_xor(place, j) for j in range(count)]
    for j in range(count):
        field_ref[slots[j]] = packed[j][:ROWS]
        heights_ref[slots[j]] = packed[j][ROWS:]
    raw_ref[place] = done_ref[...]
    if count > 1:
        results = weak_layers(
            [packed[j][:ROWS] for j in range(1, count)],
            [1.0 / packed[j][ROWS : ROWS + 1] for j in range(1, count)],
            mats,
        )
        for j in range(1, count):
            raw_ref[slots[j]] = results[j - 1]
    heights = [heights_ref[l] for l in range(count)]
    put_layers([raw_ref[l] for l in range(count)], heights, partial_ref, cross_ref, core_ref)


def first_kernel(count, *refs):
    mats, refs = refs[0], refs[1:]
    packed_ref, step_ref, field_ref, heights_ref, partial_ref, cross_ref, core_ref = refs[:7]
    refs[7][...] = jnp.broadcast_to(step_ref[...], (8, SPAN))
    heights = [packed_ref[l, ROWS:] for l in range(count)]
    for l in range(count):
        field_ref[l] = packed_ref[l, :ROWS]
        heights_ref[l] = heights[l]
    results = weak_layers(
        [packed_ref[l, :ROWS] for l in range(count)], [1.0 / h[:1] for h in heights], mats
    )
    put_layers(results, heights, partial_ref, cross_ref, core_ref)


def stage_layers(count, last):
    if not last:
        return list(range(count))
    place = lax.axis_index("vert")
    return [place, jnp.minimum(place + 1, count - 1), jnp.maximum(place - 1, 0)]


def inner_kernel(count, share, last, mats, step_ref, field_ref, partial_ref, spots_ref):
    step = step_ref[:1] * share
    fields = []
    for l in stage_layers(count, last):
        field = (field_ref[l] + step * partial_ref[l]).reshape(3, 8, 8, SPAN)
        fields.append(field[:, 1:7].reshape(144, SPAN))
    for i, pair in enumerate(span_forward(fields, mats)):
        for part in range(2):
            spots_ref[i, part] = pair[part]


def stage_kernel(count, share, first, last, *refs):
    mats, step_ref, field_ref, heights_ref, partial_ref, cross_ref, core_ref, spots_ref = refs[:8]
    refs = refs[8:]
    total = None if first else refs[0][...]
    total_ref, next_partial_ref, next_cross_ref, next_core_ref = refs[-4:]
    place = lax.axis_index("vert")
    step = step_ref[:1] * share
    layers = stage_layers(count, last)
    heights = [heights_ref[l] for l in layers]
    faces = []
    for l in layers:
        ends = join_ends(partial_ref[l], cross_ref[l], core_ref[l])
        ends = jnp.concatenate([end[:, None] for end in ends], axis=1)
        field = field_ref[l].reshape(3, 8, 8, SPAN)
        field = jnp.concatenate([field[:, :1], field[:, 7:]], axis=1)
        faces.append((field + step * ends).reshape(48, SPAN))
    spots = []
    for i, pair in enumerate(face_spots(faces, mats)):
        spots.append([with_faces(spots_ref[i, part], pair[part]) for part in range(2)])
    results = weak_spots(spots, [1.0 / h[:1] for h in heights], mats)
    own = join_stream(partial_ref[place], cross_ref[place], core_ref[place])
    total_ref[...] = own if first else total + 2.0 * own
    if last:
        joined = join_heights(*results, *heights, place < count - 1, place > 0)
        next_partial_ref[...] = joined
        put_faces(joined, next_cross_ref, next_core_ref, slice(None))
    else:
        put_layers(results, heights, next_partial_ref, next_cross_ref, next_core_ref)


def rate_kernel(partial_ref, cross_ref, core_ref, total_ref, rate_ref):
    slope = join_stream(partial_ref[...], cross_ref[...], core_ref[...])
    rate_ref[...] = (total_ref[...] + slope) / 6.0


VMEM = pl.BlockSpec(memory_space=pltpu.VMEM)


def call(kernel, outs, args, scratch=(), flops=0):
    shapes = [jax.ShapeDtypeStruct(shape, f32) for shape in outs]
    one = len(shapes) == 1
    return pl.pallas_call(
        kernel,
        out_shape=shapes[0] if one else shapes,
        in_specs=[VMEM] * len(args),
        out_specs=VMEM if one else [VMEM] * len(shapes),
        scratch_shapes=list(scratch),
        compiler_params=pltpu.CompilerParams(vmem_limit_bytes=32 * 1024 * 1024),
        cost_estimate=pl.CostEstimate(flops=flops, bytes_accessed=1 << 20, transcendentals=0),
    )(*args)


def swap_stream(cross, core):
    count = lax.axis_size("horiz")
    cores = [(i, i ^ 1) for i in range(count)]
    crosses = [(i, (i + 1) % count if i % 2 else (i - 1) % count) for i in range(count)]
    return lax.ppermute(cross, "horiz", crosses), lax.ppermute(core, "horiz", cores)


def on_device(velocity, heights, time_step):
    layers = lax.axis_size("vert")
    mats = jnp.asarray(matrices()[0])
    unit = 2 * 256 * 256 * 3000
    field = (layers, ROWS, SPAN)
    face = (layers, 3, 8, SPAN)
    small = (3, 8, SPAN)
    first_outs = [field, (layers, 8, SPAN), field, face, face]
    step = time_step.reshape(1, 1)
    tile = (8, SPAN)
    packed = call(
        pack_kernel,
        [(ROWS + 8, SPAN)],
        [velocity.reshape(ROWS, SPAN), heights.reshape(1, 1)],
    )
    if layers in (1, 2, 4):
        slots = [packed]
        for j in range(1, layers):
            slots.append(lax.ppermute(packed, "vert", [(i, i ^ j) for i in range(layers)]))
        own, step = call(own_layer_kernel, [(ROWS, SPAN), tile], [mats, packed, step], flops=unit)
        fields, all_heights, partial, cross, core = call(
            functools.partial(other_layers_kernel, layers),
            first_outs,
            [mats] + slots + [own],
            scratch=[pltpu.VMEM(field, f32)],
            flops=(layers - 1) * unit,
        )
    else:
        gathered = lax.all_gather(packed, "vert")
        fields, all_heights, partial, cross, core, step = call(
            functools.partial(first_kernel, layers), first_outs + [tile], [mats, gathered, step]
        )
    cross, core = swap_stream(cross, core)
    total = None
    for stage, share in enumerate((0.5, 0.5, 1.0)):
        last = stage == 2
        used = 3 if last else layers
        spots = call(
            functools.partial(inner_kernel, layers, share, last),
            [(len(spots_of(used)), 2, 144, SPAN)],
            [mats, step, fields, partial],
            flops=used * unit // 4,
        )
        args = [mats, step, fields, all_heights, partial, cross, core, spots]
        total, partial, cross, core = call(
            functools.partial(stage_kernel, layers, share, stage == 0, last),
            [(ROWS, SPAN)] + ([(ROWS, SPAN), small, small] if last else [field, face, face]),
            args + ([] if stage == 0 else [total]),
            flops=used * unit,
        )
        cross, core = swap_stream(cross, core)
    rate = call(rate_kernel, [(ROWS, SPAN)], [partial, cross, core, total])
    return rate.reshape(velocity.shape)


def solution(mesh):
    in_specs = (P(None, "horiz", "vert", None), P("vert"), P())
    out_specs = P(None, "horiz", "vert", None)
    return jax.shard_map(
        on_device, mesh=mesh, in_specs=in_specs, out_specs=out_specs, check_vma=False
    )
```

time: 42.9 us -> 41.8 us (0.974)
  local copies, waits for them, and re-layouts: 6.57 us -> 2.14 us
  waiting for transfers between devices: 13.6 us -> 16.9 us
  Pallas kernels: 10.1 us -> 10.6 us
    unnamed x28 -> x6, local copies, waits for them, and re-layouts: 6.57 us -> 2.14 us
    ppermute x3, waiting for transfers between devices: 1.22 us -> 5.04 us  [on_device(): lax.ppermute(packed, 'vert', [(i, i ^ j) for i in range(layers)])]
    ppermute x4, waiting for transfers between devices: 12.4 us -> 11.8 us  [swap_stream(): lax.ppermute(cross, 'horiz', crosses)]
    pallas_call x7 -> x10, Pallas kernels: 10.1 us -> 10.6 us  [call(): pl.pallas_call(kernel, out_shape=shapes[0] if one else shapes, in_specs=[...]
  transfers between devices with their start and end apart: 11 -> 11, of which waited for: 5 -> 6; matrix products, arithmetic and copies ran while one was open for 0% -> 0% of each run, Pallas kernels for 2% -> 5%
where the time goes in v1:
time: 41.8 us; the launch traced here: 41.6 us
  waiting for transfers between devices  16.9 us (40%)
  Pallas kernels  10.6 us (25%)
  starting transfers between devices  10.6 us (25%)
  local copies, waits for them, and re-layouts  2.14 us (5%)
  between operations  1.38 us (3%)
    ppermute x4, waiting for transfers between devices, swap_stream(): lax.ppermute(cross, 'horiz', crosses)  11.8 us
    pallas_call x10, Pallas kernels, call(): pl.pallas_call(kernel, out_shape=shapes[0] if one else shapes, in_specs=[...  10.6 us
    ppermute x3, starting transfers between devices, on_device(): lax.ppermute(packed, 'vert', [(i, i ^ j) for i in range(layers)])  5.69 us
    ppermute x3, waiting for transfers between devices, on_device(): lax.ppermute(packed, 'vert', [(i, i ^ j) for i in range(layers)])  5.04 us
    ppermute x4, starting transfers between devices, swap_stream(): lax.ppermute(cross, 'horiz', crosses)  4.47 us
    unnamed x6, local copies, waits for them, and re-layouts  2.14 us
  transfers between devices with their start and end apart: 11, of which 6 were waited for; matrix products, arithmetic and copies ran while one was open for 0% of the time, Pallas kernels for 5%

profile of v1, /device:TPU:0, one launch (start us, length us, event | category | flops | bytes accessed | tf_op | source)
XLA Modules:
  0.0 41.6 jit_solution(5915385802511014871)
XLA Ops:
  0.7 0.0 copy-start.2
  0.7 0.9 %copy-done.2 = f32[3,8,8,128]{3,2,1,0:T(8,128)S(1)} copy-done((f32[3,8,8,128]{3,2,1,0:T(8,128)S(1)}, f32[3,8,8,128]{3,2,1,0:T(8,128)}, u32[]{:S(2)}) %copy-start.2) | copy-done | bytes 98328
  1.5 0.1 shard_map.46.packed_ref.refs_1_
  1.6 5.1 %collective-permute-start.2 = (f32[200,128]{1,0:T(8,128)S(1)}, f32[200,128]{1,0:T(8,128)S(1)}, u32[]{:S(2)}, u32[]{:S(2)}) collective-permute-start(f32[200,128]{1,0:T(8,128)S(1)} %shard_map.46.packed_ref.refs_1_), channel_id=1, source_target_pairs={{0,3},{1,2},{2,1},{3,0},{4,7},{5,6},{6,5},{7,4},{8,11},{9,10},{10,... | collective-permute-start | bytes 307208 | tf_op jit(solution)/shard_map/ppermute | solution.py:549
  6.7 0.0 collective-permute-start.1
  6.7 0.6 %collective-permute-start = (f32[200,128]{1,0:T(8,128)S(1)}, f32[200,128]{1,0:T(8,128)S(1)}, u32[]{:S(2)}, u32[]{:S(2)}) collective-permute-start(f32[200,128]{1,0:T(8,128)S(1)} %shard_map.46.packed_ref.refs_1_), channel_id=1, source_target_pairs={{0,1},{1,0},{2,3},{3,2},{4,5},{5,4},{6,7},{7,6},{8,9},{9,8},{10,11... | collective-permute-start | bytes 307208 | tf_op jit(solution)/shard_map/ppermute | solution.py:549
  8.0 0.0 copy-start
  8.0 1.2 %copy-done = bf16[2240,256]{1,0:T(8,128)(2,1)S(1)} copy-done((bf16[2240,256]{1,0:T(8,128)(2,1)S(1)}, bf16[2240,256]{1,0:T(8,128)(2,1)}, u32[]{:S(2)}) %copy-start) | copy-done | bytes 1146904
  9.2 1.0 %shard_map.47 = (f32[192,128]{1,0:T(8,128)S(1)}, f32[8,128]{1,0:T(8,128)S(1)}) custom-call(bf16[2240,256]{1,0:T(8,128)(2,1)S(1)} %copy-done, f32[200,128]{1,0:T(8,128)S(1)} %shard_map.46.packed_ref.refs_1_, f32[1,1]{1,0:T(1,128)} %bitcast.5.step_ref), custom_call_target="tpu_custom_call" | custom-call | flops 393216000 | bytes 1048576 | tf_op jit(solution)/shard_map/pallas_call | solution.py:513
  10.2 0.2 collective-permute-done.2.refs_4_
  10.5 4.8 %collective-permute-done.1.refs_3_ = f32[200,128]{1,0:T(8,128)S(1)} collective-permute-done((f32[200,128]{1,0:T(8,128)S(1)}, f32[200,128]{1,0:T(8,128)S(1)}, u32[]{:S(2)}, u32[]{:S(2)}) %collective-permute-start.1) | collective-permute-done | bytes 102432 | tf_op jit(solution)/shard_map/ppermute | solution.py:549
  15.3 0.0 collective-permute-done.refs_2_
  15.3 0.0 copy-start.1
  15.3 1.9 %shard_map.48 = (f32[4,192,128]{2,1,0:T(8,128)S(1)}, f32[4,8,128]{2,1,0:T(8,128)S(1)}, f32[4,192,128]{2,1,0:T(8,128)S(1)}, f32[4,3,8,128]{3,2,1,0:T(8,128)S(1)}, f32[4,3,8,128]{3,2,1,0:T(8,128)S(1)}) custom-call(bf16[2240,256]{1,0:T(8,128)(2,1)S(1)} %copy-done, f32[200,128]{1,0:T(8,128)S(1)} %shard_map.46.packed_ref.refs_1_, ...), custom_call_target="tpu_custom_call" | custom-call | flops 1179648000 | bytes 1048576 | tf_op jit(solution)/shard_map/pallas_call | solution.py:513
  17.2 1.3 %collective-permute-start.3 = (f32[4,3,8,128]{3,2,1,0:T(8,128)S(1)}, f32[4,3,8,128]{3,2,1,0:T(8,128)S(1)}, u32[]{:S(2)}, u32[]{:S(2)}) collective-permute-start(f32[4,3,8,128]{3,2,1,0:T(8,128)S(1)} %get-tuple-element.29), channel_id=1, source_target_pairs={{0,28},{4,8},{8,4},{12,16},{16,12},{20,24},{24,20},{28,0},{1,29},{... | collective-permute-start | bytes 147464 | tf_op jit(solution)/shard_map/ppermute | solution.py:528
  18.5 0.4 collective-permute-start.4
  18.9 0.0 copy-done.1
  18.9 0.4 %shard_map.49.refs_7_ = f32[6,2,144,128]{3,2,1,0:T(8,128)S(1)} custom-call(bf16[2240,256]{1,0:T(8,128)(2,1)S(1)} %copy-done.1, f32[8,128]{1,0:T(8,128)S(1)} %get-tuple-element.24.step_ref.refs_1_, f32[4,192,128]{2,1,0:T(8,128)S(1)} %get-tuple-element.26.field_ref.refs_2_, f32[4,192,128]{2,1,0:T(8,128)S(1)} %get-tuple-element.28.partial_ref.refs_4_), custom_call_target="tpu_custom_call" | custom-call | flops 393216000 | bytes 1048576 | tf_op jit(solution)/shard_map/pallas_call | solution.py:513
  19.3 2.8 %collective-permute-done.3.refs_5_ = f32[4,3,8,128]{3,2,1,0:T(8,128)S(1)} collective-permute-done((f32[4,3,8,128]{3,2,1,0:T(8,128)S(1)}, f32[4,3,8,128]{3,2,1,0:T(8,128)S(1)}, u32[]{:S(2)}, u32[]{:S(2)}) %collective-permute-start.3) | collective-permute-done | bytes 49184 | tf_op jit(solution)/shard_map/ppermute | solution.py:528
  22.1 0.0 collective-permute-done.4.refs_6_
  22.1 2.0 %shard_map.50 = (f32[192,128]{1,0:T(8,128)S(1)}, f32[4,192,128]{2,1,0:T(8,128)S(1)}, f32[4,3,8,128]{3,2,1,0:T(8,128)S(1)}, f32[4,3,8,128]{3,2,1,0:T(8,128)S(1)}) custom-call(bf16[2240,256]{1,0:T(8,128)(2,1)S(1)} %copy-done.1, f32[8,128]{1,0:T(8,128)S(1)} %get-tuple-element.24.step_ref.refs_1_, f32[4,192,128]{2,1,0:T(8,128)S(1)} %get-tuple-element.26.field_ref.refs_2_, ...), custom_call_target="tpu_custom_call" | custom-call | flops 1572864000 | bytes 1048576 | tf_op jit(solution)/shard_map/pallas_call | solution.py:513
  24.1 1.1 %collective-permute-start.5 = (f32[4,3,8,128]{3,2,1,0:T(8,128)S(1)}, f32[4,3,8,128]{3,2,1,0:T(8,128)S(1)}, u32[]{:S(2)}, u32[]{:S(2)}) collective-permute-start(f32[4,3,8,128]{3,2,1,0:T(8,128)S(1)} %get-tuple-element.32), channel_id=1, source_target_pairs={{0,28},{4,8},{8,4},{12,16},{16,12},{20,24},{24,20},{28,0},{1,29},{... | collective-permute-start | bytes 147464 | tf_op jit(solution)/shard_map/ppermute | solution.py:528
  25.2 0.0 collective-permute-start.6
  25.2 0.4 %shard_map.51.refs_7_ = f32[6,2,144,128]{3,2,1,0:T(8,128)S(1)} custom-call(bf16[2240,256]{1,0:T(8,128)(2,1)S(1)} %copy-done.1, f32[8,128]{1,0:T(8,128)S(1)} %get-tuple-element.24.step_ref.refs_1_, f32[4,192,128]{2,1,0:T(8,128)S(1)} %get-tuple-element.26.field_ref.refs_2_, f32[4,192,128]{2,1,0:T(8,128)S(1)} %get-tuple-element.31.partial_ref.refs_4_), custom_call_target="tpu_custom_call" | custom-call | flops 393216000 | bytes 1048576 | tf_op jit(solution)/shard_map/pallas_call | solution.py:513
  25.6 3.0 %collective-permute-done.5.refs_5_ = f32[4,3,8,128]{3,2,1,0:T(8,128)S(1)} collective-permute-done((f32[4,3,8,128]{3,2,1,0:T(8,128)S(1)}, f32[4,3,8,128]{3,2,1,0:T(8,128)S(1)}, u32[]{:S(2)}, u32[]{:S(2)}) %collective-permute-start.5) | collective-permute-done | bytes 49184 | tf_op jit(solution)/shard_map/ppermute | solution.py:528
  28.6 0.0 collective-permute-done.6.refs_6_
  28.6 2.0 %shard_map.52 = (f32[192,128]{1,0:T(8,128)S(1)}, f32[4,192,128]{2,1,0:T(8,128)S(1)}, f32[4,3,8,128]{3,2,1,0:T(8,128)S(1)}, f32[4,3,8,128]{3,2,1,0:T(8,128)S(1)}) custom-call(bf16[2240,256]{1,0:T(8,128)(2,1)S(1)} %copy-done.1, f32[8,128]{1,0:T(8,128)S(1)} %get-tuple-element.24.step_ref.refs_1_, f32[4,192,128]{2,1,0:T(8,128)S(1)} %get-tuple-element.26.field_ref.refs_2_, ...), custom_call_target="tpu_custom_call" | custom-call | flops 1572864000 | bytes 1048576 | tf_op jit(solution)/shard_map/pallas_call | solution.py:513
  30.6 1.1 %collective-permute-start.7 = (f32[4,3,8,128]{3,2,1,0:T(8,128)S(1)}, f32[4,3,8,128]{3,2,1,0:T(8,128)S(1)}, u32[]{:S(2)}, u32[]{:S(2)}) collective-permute-start(f32[4,3,8,128]{3,2,1,0:T(8,128)S(1)} %get-tuple-element.36), channel_id=1, source_target_pairs={{0,28},{4,8},{8,4},{12,16},{16,12},{20,24},{24,20},{28,0},{1,29},{... | collective-permute-start | bytes 147464 | tf_op jit(solution)/shard_map/ppermute | solution.py:528
  31.7 0.0 collective-permute-start.8
  31.7 0.4 shard_map.53.refs_7_
  32.1 3.0 %collective-permute-done.7.refs_5_ = f32[4,3,8,128]{3,2,1,0:T(8,128)S(1)} collective-permute-done((f32[4,3,8,128]{3,2,1,0:T(8,128)S(1)}, f32[4,3,8,128]{3,2,1,0:T(8,128)S(1)}, u32[]{:S(2)}, u32[]{:S(2)}) %collective-permute-start.7) | collective-permute-done | bytes 49184 | tf_op jit(solution)/shard_map/ppermute | solution.py:528
  35.1 0.0 collective-permute-done.8.refs_6_
  35.1 1.7 %shard_map.54 = (f32[192,128]{1,0:T(8,128)S(1)}, f32[192,128]{1,0:T(8,128)S(1)}, f32[3,8,128]{2,1,0:T(8,128)S(1)}, f32[3,8,128]{2,1,0:T(8,128)S(1)}) custom-call(bf16[2240,256]{1,0:T(8,128)(2,1)S(1)} %copy-done.1, f32[8,128]{1,0:T(8,128)S(1)} %get-tuple-element.24.step_ref.refs_1_, f32[4,192,128]{2,1,0:T(8,128)S(1)} %get-tuple-element.26.field_ref.refs_2_, ...), custom_call_target="tpu_custom_call" | custom-call | flops 1179648000 | bytes 1048576 | tf_op jit(solution)/shard_map/pallas_call | solution.py:513
  36.8 1.1 %collective-permute-start.9 = (f32[3,8,128]{2,1,0:T(8,128)S(1)}, f32[3,8,128]{2,1,0:T(8,128)S(1)}, u32[]{:S(2)}, u32[]{:S(2)}) collective-permute-start(f32[3,8,128]{2,1,0:T(8,128)S(1)} %get-tuple-element.40), channel_id=1, source_target_pairs={{0,28},{4,8},{8,4},{12,16},{16,12},{20,24},{24,20},{28,0},{1,29},{... | collective-permute-start | bytes 36872 | tf_op jit(solution)/shard_map/ppermute | solution.py:528
  37.9 0.0 collective-permute-start.10
  37.9 3.0 %collective-permute-done.9.cross_ref = f32[3,8,128]{2,1,0:T(8,128)S(1)} collective-permute-done((f32[3,8,128]{2,1,0:T(8,128)S(1)}, f32[3,8,128]{2,1,0:T(8,128)S(1)}, u32[]{:S(2)}, u32[]{:S(2)}) %collective-permute-start.9) | collective-permute-done | bytes 12320 | tf_op jit(solution)/shard_map/ppermute | solution.py:528
  40.9 0.0 collective-permute-done.10.core_ref
  40.9 0.7 %shard_map.55 = f32[192,128]{1,0:T(8,128)} custom-call(f32[192,128]{1,0:T(8,128)S(1)} %get-tuple-element.39.partial_ref, f32[3,8,128]{2,1,0:T(8,128)S(1)} %collective-permute-done.9.cross_ref, f32[3,8,128]{2,1,0:T(8,128)S(1)} %collective-permute-done.10.core_ref, f32[192,128]{1,0:T(8,128)S(1)} %get-tuple-element.42.total_ref), custom_call_target="tpu_custom_call" | custom-call | bytes 1048576 | tf_op jit(solution)/shard_map/pallas_call | solution.py:513
Async XLA Ops:
  0.7 0.9 %copy-start.2 = (f32[3,8,8,128]{3,2,1,0:T(8,128)S(1)}, f32[3,8,8,128]{3,2,1,0:T(8,128)}, u32[]{:S(2)}) copy-start(f32[3,8,8,128]{3,2,1,0:T(8,128)} %param.4) | copy-start | bytes 294916
  1.6 8.9 %collective-permute-start.2 = (f32[200,128]{1,0:T(8,128)S(1)}, f32[200,128]{1,0:T(8,128)S(1)}, u32[]{:S(2)}, u32[]{:S(2)}) collective-permute-start(f32[200,128]{1,0:T(8,128)S(1)} %shard_map.46.packed_ref.refs_1_), channel_id=1, source_target_pairs={{0,3},{1,2},{2,1},{3,0},{4,7},{5,6},{6,5},{7,4},{8,11},{9,10},{10,... | collective-permute-start | bytes 307208 | tf_op jit(solution)/shard_map/ppermute | solution.py:549
  6.7 8.6 %collective-permute-start.1 = (f32[200,128]{1,0:T(8,128)S(1)}, f32[200,128]{1,0:T(8,128)S(1)}, u32[]{:S(2)}, u32[]{:S(2)}) collective-permute-start(f32[200,128]{1,0:T(8,128)S(1)} %shard_map.46.packed_ref.refs_1_), channel_id=1, source_target_pairs={{0,2},{1,3},{2,0},{3,1},{4,6},{5,7},{6,4},{7,5},{8,10},{9,11},{10,... | collective-permute-start | bytes 307208 | tf_op jit(solution)/shard_map/ppermute | solution.py:549
  6.7 8.6 %collective-permute-start = (f32[200,128]{1,0:T(8,128)S(1)}, f32[200,128]{1,0:T(8,128)S(1)}, u32[]{:S(2)}, u32[]{:S(2)}) collective-permute-start(f32[200,128]{1,0:T(8,128)S(1)} %shard_map.46.packed_ref.refs_1_), channel_id=1, source_target_pairs={{0,1},{1,0},{2,3},{3,2},{4,5},{5,4},{6,7},{7,6},{8,9},{9,8},{10,11... | collective-permute-start | bytes 307208 | tf_op jit(solution)/shard_map/ppermute | solution.py:549
  8.0 1.3 %copy-start = (bf16[2240,256]{1,0:T(8,128)(2,1)S(1)}, bf16[2240,256]{1,0:T(8,128)(2,1)}, u32[]{:S(2)}) copy-start(bf16[2240,256]{1,0:T(8,128)(2,1)} %constant.2.clone.mats.refs_0_) | copy-start | bytes 3440644
  15.3 3.6 %copy-start.1 = (bf16[2240,256]{1,0:T(8,128)(2,1)S(1)}, bf16[2240,256]{1,0:T(8,128)(2,1)}, u32[]{:S(2)}) copy-start(bf16[2240,256]{1,0:T(8,128)(2,1)} %constant.2.clone.mats.refs_0_) | copy-start | bytes 3440644
  17.2 4.9 %collective-permute-start.3 = (f32[4,3,8,128]{3,2,1,0:T(8,128)S(1)}, f32[4,3,8,128]{3,2,1,0:T(8,128)S(1)}, u32[]{:S(2)}, u32[]{:S(2)}) collective-permute-start(f32[4,3,8,128]{3,2,1,0:T(8,128)S(1)} %get-tuple-element.29), channel_id=1, source_target_pairs={{0,28},{4,8},{8,4},{12,16},{16,12},{20,24},{24,20},{28,0},{1,29},{... | collective-permute-start | bytes 147464 | tf_op jit(solution)/shard_map/ppermute | solution.py:528
  18.5 3.6 %collective-permute-start.4 = (f32[4,3,8,128]{3,2,1,0:T(8,128)S(1)}, f32[4,3,8,128]{3,2,1,0:T(8,128)S(1)}, u32[]{:S(2)}, u32[]{:S(2)}) collective-permute-start(f32[4,3,8,128]{3,2,1,0:T(8,128)S(1)} %get-tuple-element.30), channel_id=1, source_target_pairs={{0,4},{4,0},{8,12},{12,8},{16,20},{20,16},{24,28},{28,24},{1,5},{5... | collective-permute-start | bytes 147464 | tf_op jit(solution)/shard_map/ppermute | solution.py:528
  24.1 4.5 %collective-permute-start.5 = (f32[4,3,8,128]{3,2,1,0:T(8,128)S(1)}, f32[4,3,8,128]{3,2,1,0:T(8,128)S(1)}, u32[]{:S(2)}, u32[]{:S(2)}) collective-permute-start(f32[4,3,8,128]{3,2,1,0:T(8,128)S(1)} %get-tuple-element.32), channel_id=1, source_target_pairs={{0,28},{4,8},{8,4},{12,16},{16,12},{20,24},{24,20},{28,0},{1,29},{... | collective-permute-start | bytes 147464 | tf_op jit(solution)/shard_map/ppermute | solution.py:528
  25.2 3.4 %collective-permute-start.6 = (f32[4,3,8,128]{3,2,1,0:T(8,128)S(1)}, f32[4,3,8,128]{3,2,1,0:T(8,128)S(1)}, u32[]{:S(2)}, u32[]{:S(2)}) collective-permute-start(f32[4,3,8,128]{3,2,1,0:T(8,128)S(1)} %get-tuple-element.33), channel_id=1, source_target_pairs={{0,4},{4,0},{8,12},{12,8},{16,20},{20,16},{24,28},{28,24},{1,5},{5... | collective-permute-start | bytes 147464 | tf_op jit(solution)/shard_map/ppermute | solution.py:528
  30.6 4.5 %collective-permute-start.7 = (f32[4,3,8,128]{3,2,1,0:T(8,128)S(1)}, f32[4,3,8,128]{3,2,1,0:T(8,128)S(1)}, u32[]{:S(2)}, u32[]{:S(2)}) collective-permute-start(f32[4,3,8,128]{3,2,1,0:T(8,128)S(1)} %get-tuple-element.36), channel_id=1, source_target_pairs={{0,28},{4,8},{8,4},{12,16},{16,12},{20,24},{24,20},{28,0},{1,29},{... | collective-permute-start | bytes 147464 | tf_op jit(solution)/shard_map/ppermute | solution.py:528
  31.7 3.4 %collective-permute-start.8 = (f32[4,3,8,128]{3,2,1,0:T(8,128)S(1)}, f32[4,3,8,128]{3,2,1,0:T(8,128)S(1)}, u32[]{:S(2)}, u32[]{:S(2)}) collective-permute-start(f32[4,3,8,128]{3,2,1,0:T(8,128)S(1)} %get-tuple-element.37), channel_id=1, source_target_pairs={{0,4},{4,0},{8,12},{12,8},{16,20},{20,16},{24,28},{28,24},{1,5},{5... | collective-permute-start | bytes 147464 | tf_op jit(solution)/shard_map/ppermute | solution.py:528
  36.8 4.1 %collective-permute-start.9 = (f32[3,8,128]{2,1,0:T(8,128)S(1)}, f32[3,8,128]{2,1,0:T(8,128)S(1)}, u32[]{:S(2)}, u32[]{:S(2)}) collective-permute-start(f32[3,8,128]{2,1,0:T(8,128)S(1)} %get-tuple-element.40), channel_id=1, source_target_pairs={{0,28},{4,8},{8,4},{12,16},{16,12},{20,24},{24,20},{28,0},{1,29},{... | collective-permute-start | bytes 36872 | tf_op jit(solution)/shard_map/ppermute | solution.py:528
  37.9 3.0 %collective-permute-start.10 = (f32[3,8,128]{2,1,0:T(8,128)S(1)}, f32[3,8,128]{2,1,0:T(8,128)S(1)}, u32[]{:S(2)}, u32[]{:S(2)}) collective-permute-start(f32[3,8,128]{2,1,0:T(8,128)S(1)} %get-tuple-element.41), channel_id=1, source_target_pairs={{0,4},{4,0},{8,12},{12,8},{16,20},{20,16},{24,28},{28,24},{1,5},{5... | collective-permute-start | bytes 36872 | tf_op jit(solution)/shard_map/ppermute | solution.py:528

commit v2 on v1

--- a/solution.py
+++ b/solution.py
@@ -410,31 +410,40 @@
     packed_ref[ROWS:] = jnp.broadcast_to(height_ref[...], (8, SPAN))
 
 
-def own_layer_kernel(mats, packed_ref, step_ref, out_ref, step_tile_ref):
+def one_layer_kernel_with_step(mats, packed_ref, step_ref, out_ref, step_tile_ref):
     inverse = 1.0 / packed_ref[ROWS : ROWS + 1]
     out_ref[...] = weak_layers([packed_ref[:ROWS]], [inverse], mats)[0]
     step_tile_ref[...] = jnp.broadcast_to(step_ref[...], (8, SPAN))
 
 
-def other_layers_kernel(count, *refs):
-    mats, packed, done_ref, refs = refs[0], refs[1 : count + 1], refs[count + 1], refs[count + 2 :]
+def other_layers_kernel(order, *refs):
+    count = len(order)
+    ready = min(count, 2)
+    mats, packed, refs = refs[0], refs[1 : count + 1], refs[count + 1 :]
+    given, refs = refs[:ready], refs[ready:]
     field_ref, heights_ref, partial_ref, cross_ref, core_ref, raw_ref = refs
     place = lax.axis_index("vert")
-    slots = [jnp.bitwise_xor(place, j) for j in range(count)]
-    for j in range(count):
-        field_ref[slots[j]] = packed[j][:ROWS]
-        heights_ref[slots[j]] = packed[j][ROWS:]
-    raw_ref[place] = done_ref[...]
-    if count > 1:
+    slots = [jnp.bitwise_xor(place, j) for j in order]
+    for i in range(count):
+        field_ref[slots[i]] = packed[i][:ROWS]
+        heights_ref[slots[i]] = packed[i][ROWS:]
+    for i in range(ready):
+        raw_ref[slots[i]] = given[i][...]
+    if count > ready:
         results = weak_layers(
-            [packed[j][:ROWS] for j in range(1, count)],
-            [1.0 / packed[j][ROWS : ROWS + 1] for j in range(1, count)],
+            [packed[i][:ROWS] for i in range(ready, count)],
+            [1.0 / packed[i][ROWS : ROWS + 1] for i in range(ready, count)],
             mats,
         )
-        for j in range(1, count):
-            raw_ref[slots[j]] = results[j - 1]
+        for i in range(ready, count):
+            raw_ref[slots[i]] = results[i - ready]
     heights = [heights_ref[l] for l in range(count)]
     put_layers([raw_ref[l] for l in range(count)], heights, partial_ref, cross_ref, core_ref)
+
+
+def one_layer_kernel(mats, packed_ref, out_ref):
+    inverse = 1.0 / packed_ref[ROWS : ROWS + 1]
+    out_ref[...] = weak_layers([packed_ref[:ROWS]], [inverse], mats)[0]
 
 
 def first_kernel(count, *refs):
@@ -547,13 +556,21 @@
         slots = [packed]
         for j in range(1, layers):
             slots.append(lax.ppermute(packed, "vert", [(i, i ^ j) for i in range(layers)]))
-        own, step = call(own_layer_kernel, [(ROWS, SPAN), tile], [mats, packed, step], flops=unit)
+        order = [0] + [layers - 1] * (layers > 1) + list(range(1, layers - 1))
+        own, step = call(
+            one_layer_kernel_with_step, [(ROWS, SPAN), tile], [mats, packed, step], flops=unit
+        )
+        given = [own]
+        if layers > 1:
+            given.append(
+                call(one_layer_kernel, [(ROWS, SPAN)], [mats, slots[layers - 1]], flops=unit)
+            )
         fields, all_heights, partial, cross, core = call(
-            functools.partial(other_layers_kernel, layers),
+            functools.partial(other_layers_kernel, order),
             first_outs,
-            [mats] + slots + [own],
+            [mats] + [slots[j] for j in order] + given,
             scratch=[pltpu.VMEM(field, f32)],
-            flops=(layers - 1) * unit,
+            flops=max(layers - 2, 0) * unit,
         )
     else:
         gathered = lax.all_gather(packed, "vert")

time: 41.8 us -> 41.5 us (level)
  waiting for transfers between devices: 16.9 us -> 15.8 us
  Pallas kernels: 10.6 us -> 11.3 us
    ppermute x3, waiting for transfers between devices: 5.04 us -> 4.02 us  [on_device(): lax.ppermute(packed, 'vert', [(i, i ^ j) for i in range(layers)])]
    pallas_call x10 -> x11, Pallas kernels: 10.6 us -> 11.3 us  [call(): pl.pallas_call(kernel, out_shape=shapes[0] if one else shapes, in_specs=[...]
  transfers between devices with their start and end apart: 11 -> 11, of which waited for: 6 -> 6; matrix products, arithmetic and copies ran while one was open for 0% -> 0% of each run, Pallas kernels for 5% -> 8%
where the time goes in v2:
time: 41.5 us; the launch traced here: 41.3 us
  waiting for transfers between devices  15.8 us (38%)
  Pallas kernels  11.3 us (27%)
  starting transfers between devices  10.6 us (26%)
  local copies, waits for them, and re-layouts  2.15 us (5%)
  between operations  1.39 us (3%)
    ppermute x4, waiting for transfers between devices, swap_stream(): lax.ppermute(cross, 'horiz', crosses)  11.8 us
    pallas_call x11, Pallas kernels, call(): pl.pallas_call(kernel, out_shape=shapes[0] if one else shapes, in_specs=[...  11.3 us
    ppermute x3, starting transfers between devices, on_device(): lax.ppermute(packed, 'vert', [(i, i ^ j) for i in range(layers)])  5.69 us
    ppermute x4, starting transfers between devices, swap_stream(): lax.ppermute(cross, 'horiz', crosses)  4.49 us
    ppermute x3, waiting for transfers between devices, on_device(): lax.ppermute(packed, 'vert', [(i, i ^ j) for i in range(layers)])  4.02 us
    unnamed x6, local copies, waits for them, and re-layouts  2.15 us
  transfers between devices with their start and end apart: 11, of which 6 were waited for; matrix products, arithmetic and copies ran while one was open for 0% of the time, Pallas kernels for 8%

profile of v2, /device:TPU:0, one launch (start us, length us, event | category | flops | bytes accessed | tf_op | source)
XLA Modules:
  0.0 41.3 jit_solution(4523827208341830304)
XLA Ops:
  0.7 0.0 copy-start.2
  0.7 0.9 %copy-done.2 = f32[3,8,8,128]{3,2,1,0:T(8,128)S(1)} copy-done((f32[3,8,8,128]{3,2,1,0:T(8,128)S(1)}, f32[3,8,8,128]{3,2,1,0:T(8,128)}, u32[]{:S(2)}) %copy-start.2) | copy-done | bytes 98328
  1.5 0.1 shard_map.46.packed_ref.refs_1_
  1.6 5.1 %collective-permute-start = (f32[200,128]{1,0:T(8,128)S(1)}, f32[200,128]{1,0:T(8,128)S(1)}, u32[]{:S(2)}, u32[]{:S(2)}) collective-permute-start(f32[200,128]{1,0:T(8,128)S(1)} %shard_map.46.packed_ref.refs_1_), channel_id=1, source_target_pairs={{0,3},{1,2},{2,1},{3,0},{4,7},{5,6},{6,5},{7,4},{8,11},{9,10},{10,... | collective-permute-start | bytes 307208 | tf_op jit(solution)/shard_map/ppermute | solution.py:558
  6.7 0.0 collective-permute-start.2
  6.7 0.6 %collective-permute-start.1 = (f32[200,128]{1,0:T(8,128)S(1)}, f32[200,128]{1,0:T(8,128)S(1)}, u32[]{:S(2)}, u32[]{:S(2)}) collective-permute-start(f32[200,128]{1,0:T(8,128)S(1)} %shard_map.46.packed_ref.refs_1_), channel_id=1, source_target_pairs={{0,1},{1,0},{2,3},{3,2},{4,5},{5,4},{6,7},{7,6},{8,9},{9,8},{10,11... | collective-permute-start | bytes 307208 | tf_op jit(solution)/shard_map/ppermute | solution.py:558
  8.0 0.0 copy-start
  8.0 1.2 %copy-done = bf16[2240,256]{1,0:T(8,128)(2,1)S(1)} copy-done((bf16[2240,256]{1,0:T(8,128)(2,1)S(1)}, bf16[2240,256]{1,0:T(8,128)(2,1)}, u32[]{:S(2)}) %copy-start) | copy-done | bytes 1146904
  9.2 0.0 copy-start.1
  9.2 1.0 %shard_map.47 = (f32[192,128]{1,0:T(8,128)S(1)}, f32[8,128]{1,0:T(8,128)S(1)}) custom-call(bf16[2240,256]{1,0:T(8,128)(2,1)S(1)} %copy-done, f32[200,128]{1,0:T(8,128)S(1)} %shard_map.46.packed_ref.refs_1_, f32[1,1]{1,0:T(1,128)} %bitcast.5.step_ref), custom_call_target="tpu_custom_call" | custom-call | flops 393216000 | bytes 1048576 | tf_op jit(solution)/shard_map/pallas_call | solution.py:522
  10.3 0.2 collective-permute-done.packed_ref.refs_2_
  10.5 0.0 copy-done.1
  10.5 1.0 %shard_map.48.refs_6_ = f32[192,128]{1,0:T(8,128)S(1)} custom-call(bf16[2240,256]{1,0:T(8,128)(2,1)S(1)} %copy-done.1, f32[200,128]{1,0:T(8,128)S(1)} %collective-permute-done.packed_ref.refs_2_), custom_call_target="tpu_custom_call" | custom-call | flops 393216000 | bytes 1048576 | tf_op jit(solution)/shard_map/pallas_call | solution.py:522
  11.5 3.8 %collective-permute-done.2.refs_4_ = f32[200,128]{1,0:T(8,128)S(1)} collective-permute-done((f32[200,128]{1,0:T(8,128)S(1)}, f32[200,128]{1,0:T(8,128)S(1)}, u32[]{:S(2)}, u32[]{:S(2)}) %collective-permute-start.2) | collective-permute-done | bytes 102432 | tf_op jit(solution)/shard_map/ppermute | solution.py:558
  15.3 0.0 collective-permute-done.1.refs_3_
  15.3 1.6 %shard_map.49 = (f32[4,192,128]{2,1,0:T(8,128)S(1)}, f32[4,8,128]{2,1,0:T(8,128)S(1)}, f32[4,192,128]{2,1,0:T(8,128)S(1)}, f32[4,3,8,128]{3,2,1,0:T(8,128)S(1)}, f32[4,3,8,128]{3,2,1,0:T(8,128)S(1)}) custom-call(bf16[2240,256]{1,0:T(8,128)(2,1)S(1)} %copy-done.1, f32[200,128]{1,0:T(8,128)S(1)} %shard_map.46.packed_ref.refs_1_, ...), custom_call_target="tpu_custom_call" | custom-call | flops 786432000 | bytes 1048576 | tf_op jit(solution)/shard_map/pallas_call | solution.py:522
  16.9 1.3 %collective-permute-start.3 = (f32[4,3,8,128]{3,2,1,0:T(8,128)S(1)}, f32[4,3,8,128]{3,2,1,0:T(8,128)S(1)}, u32[]{:S(2)}, u32[]{:S(2)}) collective-permute-start(f32[4,3,8,128]{3,2,1,0:T(8,128)S(1)} %get-tuple-element.29), channel_id=1, source_target_pairs={{0,28},{4,8},{8,4},{12,16},{16,12},{20,24},{24,20},{28,0},{1,29},{... | collective-permute-start | bytes 147464 | tf_op jit(solution)/shard_map/ppermute | solution.py:537
  18.2 0.4 collective-permute-start.4
  18.6 0.4 %shard_map.50.refs_7_ = f32[6,2,144,128]{3,2,1,0:T(8,128)S(1)} custom-call(bf16[2240,256]{1,0:T(8,128)(2,1)S(1)} %copy-done.1, f32[8,128]{1,0:T(8,128)S(1)} %get-tuple-element.24.step_ref.refs_1_, f32[4,192,128]{2,1,0:T(8,128)S(1)} %get-tuple-element.26.field_ref.refs_2_, f32[4,192,128]{2,1,0:T(8,128)S(1)} %get-tuple-element.28.partial_ref.refs_4_), custom_call_target="tpu_custom_call" | custom-call | flops 393216000 | bytes 1048576 | tf_op jit(solution)/shard_map/pallas_call | solution.py:522
  19.0 2.8 %collective-permute-done.3.refs_5_ = f32[4,3,8,128]{3,2,1,0:T(8,128)S(1)} collective-permute-done((f32[4,3,8,128]{3,2,1,0:T(8,128)S(1)}, f32[4,3,8,128]{3,2,1,0:T(8,128)S(1)}, u32[]{:S(2)}, u32[]{:S(2)}) %collective-permute-start.3) | collective-permute-done | bytes 49184 | tf_op jit(solution)/shard_map/ppermute | solution.py:537
  21.8 0.0 collective-permute-done.4.refs_6_
  21.8 2.0 %shard_map.51 = (f32[192,128]{1,0:T(8,128)S(1)}, f32[4,192,128]{2,1,0:T(8,128)S(1)}, f32[4,3,8,128]{3,2,1,0:T(8,128)S(1)}, f32[4,3,8,128]{3,2,1,0:T(8,128)S(1)}) custom-call(bf16[2240,256]{1,0:T(8,128)(2,1)S(1)} %copy-done.1, f32[8,128]{1,0:T(8,128)S(1)} %get-tuple-element.24.step_ref.refs_1_, f32[4,192,128]{2,1,0:T(8,128)S(1)} %get-tuple-element.26.field_ref.refs_2_, ...), custom_call_target="tpu_custom_call" | custom-call | flops 1572864000 | bytes 1048576 | tf_op jit(solution)/shard_map/pallas_call | solution.py:522
  23.8 1.1 %collective-permute-start.5 = (f32[4,3,8,128]{3,2,1,0:T(8,128)S(1)}, f32[4,3,8,128]{3,2,1,0:T(8,128)S(1)}, u32[]{:S(2)}, u32[]{:S(2)}) collective-permute-start(f32[4,3,8,128]{3,2,1,0:T(8,128)S(1)} %get-tuple-element.32), channel_id=1, source_target_pairs={{0,28},{4,8},{8,4},{12,16},{16,12},{20,24},{24,20},{28,0},{1,29},{... | collective-permute-start | bytes 147464 | tf_op jit(solution)/shard_map/ppermute | solution.py:537
  24.9 0.0 collective-permute-start.6
  24.9 0.4 %shard_map.52.refs_7_ = f32[6,2,144,128]{3,2,1,0:T(8,128)S(1)} custom-call(bf16[2240,256]{1,0:T(8,128)(2,1)S(1)} %copy-done.1, f32[8,128]{1,0:T(8,128)S(1)} %get-tuple-element.24.step_ref.refs_1_, f32[4,192,128]{2,1,0:T(8,128)S(1)} %get-tuple-element.26.field_ref.refs_2_, f32[4,192,128]{2,1,0:T(8,128)S(1)} %get-tuple-element.31.partial_ref.refs_4_), custom_call_target="tpu_custom_call" | custom-call | flops 393216000 | bytes 1048576 | tf_op jit(solution)/shard_map/pallas_call | solution.py:522
  25.4 3.0 %collective-permute-done.5.refs_5_ = f32[4,3,8,128]{3,2,1,0:T(8,128)S(1)} collective-permute-done((f32[4,3,8,128]{3,2,1,0:T(8,128)S(1)}, f32[4,3,8,128]{3,2,1,0:T(8,128)S(1)}, u32[]{:S(2)}, u32[]{:S(2)}) %collective-permute-start.5) | collective-permute-done | bytes 49184 | tf_op jit(solution)/shard_map/ppermute | solution.py:537
  28.3 0.0 collective-permute-done.6.refs_6_
  28.3 2.0 %shard_map.53 = (f32[192,128]{1,0:T(8,128)S(1)}, f32[4,192,128]{2,1,0:T(8,128)S(1)}, f32[4,3,8,128]{3,2,1,0:T(8,128)S(1)}, f32[4,3,8,128]{3,2,1,0:T(8,128)S(1)}) custom-call(bf16[2240,256]{1,0:T(8,128)(2,1)S(1)} %copy-done.1, f32[8,128]{1,0:T(8,128)S(1)} %get-tuple-element.24.step_ref.refs_1_, f32[4,192,128]{2,1,0:T(8,128)S(1)} %get-tuple-element.26.field_ref.refs_2_, ...), custom_call_target="tpu_custom_call" | custom-call | flops 1572864000 | bytes 1048576 | tf_op jit(solution)/shard_map/pallas_call | solution.py:522
  30.4 1.1 %collective-permute-start.7 = (f32[4,3,8,128]{3,2,1,0:T(8,128)S(1)}, f32[4,3,8,128]{3,2,1,0:T(8,128)S(1)}, u32[]{:S(2)}, u32[]{:S(2)}) collective-permute-start(f32[4,3,8,128]{3,2,1,0:T(8,128)S(1)} %get-tuple-element.36), channel_id=1, source_target_pairs={{0,28},{4,8},{8,4},{12,16},{16,12},{20,24},{24,20},{28,0},{1,29},{... | collective-permute-start | bytes 147464 | tf_op jit(solution)/shard_map/ppermute | solution.py:537
  31.4 0.0 collective-permute-start.8
  31.4 0.4 shard_map.54.refs_7_
  31.8 3.0 %collective-permute-done.7.refs_5_ = f32[4,3,8,128]{3,2,1,0:T(8,128)S(1)} collective-permute-done((f32[4,3,8,128]{3,2,1,0:T(8,128)S(1)}, f32[4,3,8,128]{3,2,1,0:T(8,128)S(1)}, u32[]{:S(2)}, u32[]{:S(2)}) %collective-permute-start.7) | collective-permute-done | bytes 49184 | tf_op jit(solution)/shard_map/ppermute | solution.py:537
  34.8 0.0 collective-permute-done.8.refs_6_
  34.8 1.7 %shard_map.55 = (f32[192,128]{1,0:T(8,128)S(1)}, f32[192,128]{1,0:T(8,128)S(1)}, f32[3,8,128]{2,1,0:T(8,128)S(1)}, f32[3,8,128]{2,1,0:T(8,128)S(1)}) custom-call(bf16[2240,256]{1,0:T(8,128)(2,1)S(1)} %copy-done.1, f32[8,128]{1,0:T(8,128)S(1)} %get-tuple-element.24.step_ref.refs_1_, f32[4,192,128]{2,1,0:T(8,128)S(1)} %get-tuple-element.26.field_ref.refs_2_, ...), custom_call_target="tpu_custom_call" | custom-call | flops 1179648000 | bytes 1048576 | tf_op jit(solution)/shard_map/pallas_call | solution.py:522
  36.5 1.1 %collective-permute-start.9 = (f32[3,8,128]{2,1,0:T(8,128)S(1)}, f32[3,8,128]{2,1,0:T(8,128)S(1)}, u32[]{:S(2)}, u32[]{:S(2)}) collective-permute-start(f32[3,8,128]{2,1,0:T(8,128)S(1)} %get-tuple-element.40), channel_id=1, source_target_pairs={{0,28},{4,8},{8,4},{12,16},{16,12},{20,24},{24,20},{28,0},{1,29},{... | collective-permute-start | bytes 36872 | tf_op jit(solution)/shard_map/ppermute | solution.py:537
  37.6 0.0 collective-permute-start.10
  37.6 3.0 %collective-permute-done.9.cross_ref = f32[3,8,128]{2,1,0:T(8,128)S(1)} collective-permute-done((f32[3,8,128]{2,1,0:T(8,128)S(1)}, f32[3,8,128]{2,1,0:T(8,128)S(1)}, u32[]{:S(2)}, u32[]{:S(2)}) %collective-permute-start.9) | collective-permute-done | bytes 12320 | tf_op jit(solution)/shard_map/ppermute | solution.py:537
  40.6 0.0 collective-permute-done.10.core_ref
  40.6 0.7 %shard_map.56 = f32[192,128]{1,0:T(8,128)} custom-call(f32[192,128]{1,0:T(8,128)S(1)} %get-tuple-element.39.partial_ref, f32[3,8,128]{2,1,0:T(8,128)S(1)} %collective-permute-done.9.cross_ref, f32[3,8,128]{2,1,0:T(8,128)S(1)} %collective-permute-done.10.core_ref, f32[192,128]{1,0:T(8,128)S(1)} %get-tuple-element.42.total_ref), custom_call_target="tpu_custom_call" | custom-call | bytes 1048576 | tf_op jit(solution)/shard_map/pallas_call | solution.py:522
Async XLA Ops:
  0.7 0.9 %copy-start.2 = (f32[3,8,8,128]{3,2,1,0:T(8,128)S(1)}, f32[3,8,8,128]{3,2,1,0:T(8,128)}, u32[]{:S(2)}) copy-start(f32[3,8,8,128]{3,2,1,0:T(8,128)} %param.4) | copy-start | bytes 294916
  1.6 8.9 %collective-permute-start = (f32[200,128]{1,0:T(8,128)S(1)}, f32[200,128]{1,0:T(8,128)S(1)}, u32[]{:S(2)}, u32[]{:S(2)}) collective-permute-start(f32[200,128]{1,0:T(8,128)S(1)} %shard_map.46.packed_ref.refs_1_), channel_id=1, source_target_pairs={{0,3},{1,2},{2,1},{3,0},{4,7},{5,6},{6,5},{7,4},{8,11},{9,10},{10,... | collective-permute-start | bytes 307208 | tf_op jit(solution)/shard_map/ppermute | solution.py:558
  6.7 8.6 %collective-permute-start.2 = (f32[200,128]{1,0:T(8,128)S(1)}, f32[200,128]{1,0:T(8,128)S(1)}, u32[]{:S(2)}, u32[]{:S(2)}) collective-permute-start(f32[200,128]{1,0:T(8,128)S(1)} %shard_map.46.packed_ref.refs_1_), channel_id=1, source_target_pairs={{0,2},{1,3},{2,0},{3,1},{4,6},{5,7},{6,4},{7,5},{8,10},{9,11},{10,... | collective-permute-start | bytes 307208 | tf_op jit(solution)/shard_map/ppermute | solution.py:558
  6.7 8.6 %collective-permute-start.1 = (f32[200,128]{1,0:T(8,128)S(1)}, f32[200,128]{1,0:T(8,128)S(1)}, u32[]{:S(2)}, u32[]{:S(2)}) collective-permute-start(f32[200,128]{1,0:T(8,128)S(1)} %shard_map.46.packed_ref.refs_1_), channel_id=1, source_target_pairs={{0,1},{1,0},{2,3},{3,2},{4,5},{5,4},{6,7},{7,6},{8,9},{9,8},{10,11... | collective-permute-start | bytes 307208 | tf_op jit(solution)/shard_map/ppermute | solution.py:558
  8.0 1.3 %copy-start = (bf16[2240,256]{1,0:T(8,128)(2,1)S(1)}, bf16[2240,256]{1,0:T(8,128)(2,1)}, u32[]{:S(2)}) copy-start(bf16[2240,256]{1,0:T(8,128)(2,1)} %constant.2.clone.mats.refs_0_) | copy-start | bytes 3440644
  9.2 1.3 %copy-start.1 = (bf16[2240,256]{1,0:T(8,128)(2,1)S(1)}, bf16[2240,256]{1,0:T(8,128)(2,1)}, u32[]{:S(2)}) copy-start(bf16[2240,256]{1,0:T(8,128)(2,1)} %constant.2.clone.mats.refs_0_) | copy-start | bytes 3440644
  16.9 4.9 %collective-permute-start.3 = (f32[4,3,8,128]{3,2,1,0:T(8,128)S(1)}, f32[4,3,8,128]{3,2,1,0:T(8,128)S(1)}, u32[]{:S(2)}, u32[]{:S(2)}) collective-permute-start(f32[4,3,8,128]{3,2,1,0:T(8,128)S(1)} %get-tuple-element.29), channel_id=1, source_target_pairs={{0,28},{4,8},{8,4},{12,16},{16,12},{20,24},{24,20},{28,0},{1,29},{... | collective-permute-start | bytes 147464 | tf_op jit(solution)/shard_map/ppermute | solution.py:537
  18.2 3.6 %collective-permute-start.4 = (f32[4,3,8,128]{3,2,1,0:T(8,128)S(1)}, f32[4,3,8,128]{3,2,1,0:T(8,128)S(1)}, u32[]{:S(2)}, u32[]{:S(2)}) collective-permute-start(f32[4,3,8,128]{3,2,1,0:T(8,128)S(1)} %get-tuple-element.30), channel_id=1, source_target_pairs={{0,4},{4,0},{8,12},{12,8},{16,20},{20,16},{24,28},{28,24},{1,5},{5... | collective-permute-start | bytes 147464 | tf_op jit(solution)/shard_map/ppermute | solution.py:537
  23.8 4.5 %collective-permute-start.5 = (f32[4,3,8,128]{3,2,1,0:T(8,128)S(1)}, f32[4,3,8,128]{3,2,1,0:T(8,128)S(1)}, u32[]{:S(2)}, u32[]{:S(2)}) collective-permute-start(f32[4,3,8,128]{3,2,1,0:T(8,128)S(1)} %get-tuple-element.32), channel_id=1, source_target_pairs={{0,28},{4,8},{8,4},{12,16},{16,12},{20,24},{24,20},{28,0},{1,29},{... | collective-permute-start | bytes 147464 | tf_op jit(solution)/shard_map/ppermute | solution.py:537
  24.9 3.4 %collective-permute-start.6 = (f32[4,3,8,128]{3,2,1,0:T(8,128)S(1)}, f32[4,3,8,128]{3,2,1,0:T(8,128)S(1)}, u32[]{:S(2)}, u32[]{:S(2)}) collective-permute-start(f32[4,3,8,128]{3,2,1,0:T(8,128)S(1)} %get-tuple-element.33), channel_id=1, source_target_pairs={{0,4},{4,0},{8,12},{12,8},{16,20},{20,16},{24,28},{28,24},{1,5},{5... | collective-permute-start | bytes 147464 | tf_op jit(solution)/shard_map/ppermute | solution.py:537
  30.4 4.5 %collective-permute-start.7 = (f32[4,3,8,128]{3,2,1,0:T(8,128)S(1)}, f32[4,3,8,128]{3,2,1,0:T(8,128)S(1)}, u32[]{:S(2)}, u32[]{:S(2)}) collective-permute-start(f32[4,3,8,128]{3,2,1,0:T(8,128)S(1)} %get-tuple-element.36), channel_id=1, source_target_pairs={{0,28},{4,8},{8,4},{12,16},{16,12},{20,24},{24,20},{28,0},{1,29},{... | collective-permute-start | bytes 147464 | tf_op jit(solution)/shard_map/ppermute | solution.py:537
  31.4 3.4 %collective-permute-start.8 = (f32[4,3,8,128]{3,2,1,0:T(8,128)S(1)}, f32[4,3,8,128]{3,2,1,0:T(8,128)S(1)}, u32[]{:S(2)}, u32[]{:S(2)}) collective-permute-start(f32[4,3,8,128]{3,2,1,0:T(8,128)S(1)} %get-tuple-element.37), channel_id=1, source_target_pairs={{0,4},{4,0},{8,12},{12,8},{16,20},{20,16},{24,28},{28,24},{1,5},{5... | collective-permute-start | bytes 147464 | tf_op jit(solution)/shard_map/ppermute | solution.py:537
  36.5 4.1 %collective-permute-start.9 = (f32[3,8,128]{2,1,0:T(8,128)S(1)}, f32[3,8,128]{2,1,0:T(8,128)S(1)}, u32[]{:S(2)}, u32[]{:S(2)}) collective-permute-start(f32[3,8,128]{2,1,0:T(8,128)S(1)} %get-tuple-element.40), channel_id=1, source_target_pairs={{0,28},{4,8},{8,4},{12,16},{16,12},{20,24},{24,20},{28,0},{1,29},{... | collective-permute-start | bytes 36872 | tf_op jit(solution)/shard_map/ppermute | solution.py:537
  37.6 3.0 %collective-permute-start.10 = (f32[3,8,128]{2,1,0:T(8,128)S(1)}, f32[3,8,128]{2,1,0:T(8,128)S(1)}, u32[]{:S(2)}, u32[]{:S(2)}) collective-permute-start(f32[3,8,128]{2,1,0:T(8,128)S(1)} %get-tuple-element.41), channel_id=1, source_target_pairs={{0,4},{4,0},{8,12},{12,8},{16,20},{20,16},{24,28},{28,24},{1,5},{5... | collective-permute-start | bytes 36872 | tf_op jit(solution)/shard_map/ppermute | solution.py:537

commit v3 on v1

--- a/solution.py
+++ b/solution.py
@@ -107,7 +107,7 @@
     plane = stack_columns(plane)
     values = stack_columns(values)
     back = interp.T * fine_w[None, :] / gll_w[:, None]
-    plane_back = stack_columns(-np.kron(back, back))
+    plane_back = np.concatenate(halves(-np.kron(back, back)), axis=0)
     a_back = np.zeros((SPAN, SPAN))
     b_back = np.zeros((SPAN // 2, SPAN))
     for e in range(SPAN_ELEMENTS):
@@ -136,8 +136,7 @@
         "span_b": span_b,
         "plane": plane,
         "values": values,
-        "plane_back": plane_back[:, :256],
-        "plane_back_rest": plane_back[:, 256:],
+        "plane_back": plane_back,
         "pair_back": np.concatenate(halves(pair_back), axis=0),
     }
     rows, places = [], {}
@@ -251,7 +250,7 @@
 
 
 def convect_back(fine, inverse, mats):
-    back = jnp.concatenate([read(mats, "plane_back"), read(mats, "plane_back_rest")], axis=1)
+    back = read(mats, "plane_back")
     parts = [([], []) for _ in range(3)]
     for first in range(0, 144, 48):
         rows = slice(first, first + 48)
@@ -267,7 +266,8 @@
                 part.append(half)
     outs = []
     for high, low in parts:
-        outs.append(dot(back, jnp.concatenate(high + low + high, axis=0)))
+        out = dot(back, jnp.concatenate(high, axis=0))
+        outs.append(out[:64] + out[64:] + dot(back[:64], jnp.concatenate(low, axis=0)))
     return jnp.concatenate(outs, axis=0)
 
 
@@ -332,26 +332,23 @@
     return jnp.concatenate([faces[:, :1], inner, faces[:, 1:]], axis=1).reshape(ROWS, SPAN)
 
 
-def join_heights(own, above, below, height, height_above, height_below, has_above, has_below):
-    level = lax.broadcasted_iota(jnp.int32, (8, SPAN), 0)
-    keep = jnp.ones((8, SPAN), f32)
-    out = own.reshape(24, 8, SPAN)
-    if above is not None:
-        share = jnp.where(has_above, height_above / (height + height_above), 0.0)
-        take = jnp.where(level == 7, share, 0.0)
-        keep = keep - take
-        taken_above = pltpu.roll(above.reshape(24, 8, SPAN), 7, 1) * take[None]
-    if below is not None:
-        share = jnp.where(has_below, height_below / (height + height_below), 0.0)
-        take = jnp.where(level == 0, share, 0.0)
-        keep = keep - take
-        taken_below = pltpu.roll(below.reshape(24, 8, SPAN), 1, 1) * take[None]
-    out = out * keep[None]
-    if above is not None:
-        out = out + taken_above
-    if below is not None:
-        out = out + taken_below
-    return out.reshape(ROWS, SPAN)
+def height_rows(level, rows=ROWS):
+    return pl.ds(level, rows // 8, stride=8)
+
+
+def join_heights(layers, heights, joins):
+    for lower, upper, wanted in joins:
+        share = heights[upper] / (heights[lower] + heights[upper])
+        share = share[:1]
+        below = layers[lower][height_rows(7), :]
+        above = layers[upper][height_rows(0), :]
+        mean = below * (1.0 - share) + above * share
+        if wanted is True:
+            layers[lower][height_rows(7), :] = mean
+            layers[upper][height_rows(0), :] = mean
+        else:
+            layers[lower][height_rows(7), :] = jnp.where(wanted, mean, below)
+            layers[upper][height_rows(0), :] = jnp.where(wanted, mean, above)
 
 
 def sides():
@@ -389,58 +386,51 @@
 def put_layers(results, heights, partial_ref, cross_ref, core_ref):
     count = len(results)
     for l in range(count):
-        above = results[l + 1] if l + 1 < count else None
-        below = results[l - 1] if l > 0 else None
-        joined = join_heights(
-            results[l],
-            above,
-            below,
-            heights[l],
-            heights[l + 1] if l + 1 < count else None,
-            heights[l - 1] if l > 0 else None,
-            True,
-            True,
-        )
-        partial_ref[l] = joined
-        put_faces(joined, cross_ref, core_ref, l)
-
-
-def pack_kernel(velocity_ref, height_ref, packed_ref):
-    packed_ref[:ROWS] = velocity_ref[...]
-    packed_ref[ROWS:] = jnp.broadcast_to(height_ref[...], (8, SPAN))
-
-
-def own_layer_kernel(mats, packed_ref, step_ref, out_ref, step_tile_ref):
-    inverse = 1.0 / packed_ref[ROWS : ROWS + 1]
-    out_ref[...] = weak_layers([packed_ref[:ROWS]], [inverse], mats)[0]
-    step_tile_ref[...] = jnp.broadcast_to(step_ref[...], (8, SPAN))
-
-
-def other_layers_kernel(count, *refs):
-    mats, packed, done_ref, refs = refs[0], refs[1 : count + 1], refs[count + 1], refs[count + 2 :]
-    field_ref, heights_ref, partial_ref, cross_ref, core_ref, raw_ref = refs
+        partial_ref[l] = results[l]
+    layers = [partial_ref.at[l] for l in range(count)]
+    join_heights(layers, heights, [(l, l + 1, True) for l in range(count - 1)])
+    for l in range(count):
+        put_faces(partial_ref[l], cross_ref, core_ref, l)
+
+
+def step_kernel(mats, step_ref, tile_ref):
+    tile_ref[...] = jnp.broadcast_to(step_ref[...], (8, SPAN))
+
+
+def raw_kernel(count, *refs):
+    mats, packed, raws = refs[0], refs[2 : count + 2], refs[count + 2 :]
+    results = weak_layers(
+        [p[:ROWS] for p in packed], [1.0 / p[ROWS : ROWS + 1] for p in packed], mats
+    )
+    for raw_ref, result in zip(raws, results):
+        raw_ref[...] = result
+
+
+def slots_kernel(order, ready, *refs):
+    count = len(order)
+    mats, packed, given = refs[0], refs[2 : count + 2], refs[count + 2 : count + 2 + ready]
+    field_ref, heights_ref, partial_ref, cross_ref, core_ref, raw_ref = refs[count + 2 + ready :]
     place = lax.axis_index("vert")
-    slots = [jnp.bitwise_xor(place, j) for j in range(count)]
-    for j in range(count):
-        field_ref[slots[j]] = packed[j][:ROWS]
-        heights_ref[slots[j]] = packed[j][ROWS:]
-    raw_ref[place] = done_ref[...]
-    if count > 1:
-        results = weak_layers(
-            [packed[j][:ROWS] for j in range(1, count)],
-            [1.0 / packed[j][ROWS : ROWS + 1] for j in range(1, count)],
-            mats,
-        )
-        for j in range(1, count):
-            raw_ref[slots[j]] = results[j - 1]
+    slots = [jnp.bitwise_xor(place, j) for j in order]
+    for i in range(count):
+        field_ref[slots[i]] = packed[i][:ROWS]
+        heights_ref[slots[i]] = packed[i][ROWS:]
+    for i in range(ready):
+        raw_ref[slots[i]] = given[i][...]
+    results = weak_layers(
+        [packed[i][:ROWS] for i in range(ready, count)],
+        [1.0 / packed[i][ROWS : ROWS + 1] for i in range(ready, count)],
+        mats,
+    )
+    for i in range(ready, count):
+        raw_ref[slots[i]] = results[i - ready]
     heights = [heights_ref[l] for l in range(count)]
     put_layers([raw_ref[l] for l in range(count)], heights, partial_ref, cross_ref, core_ref)
 
 
 def first_kernel(count, *refs):
-    mats, refs = refs[0], refs[1:]
-    packed_ref, step_ref, field_ref, heights_ref, partial_ref, cross_ref, core_ref = refs[:7]
-    refs[7][...] = jnp.broadcast_to(step_ref[...], (8, SPAN))
+    mats, packed_ref, refs = refs[0], refs[2], refs[3:]
+    field_ref, heights_ref, partial_ref, cross_ref, core_ref = refs
     heights = [packed_ref[l, ROWS:] for l in range(count)]
     for l in range(count):
         field_ref[l] = packed_ref[l, :ROWS]
@@ -473,7 +463,8 @@
     mats, step_ref, field_ref, heights_ref, partial_ref, cross_ref, core_ref, spots_ref = refs[:8]
     refs = refs[8:]
     total = None if first else refs[0][...]
-    total_ref, next_partial_ref, next_cross_ref, next_core_ref = refs[-4:]
+    *outs, above_ref, below_ref = refs[-6:]
+    total_ref, next_partial_ref, next_cross_ref, next_core_ref = outs
     place = lax.axis_index("vert")
     step = step_ref[:1] * share
     layers = stage_layers(count, last)
@@ -492,9 +483,13 @@
     own = join_stream(partial_ref[place], cross_ref[place], core_ref[place])
     total_ref[...] = own if first else total + 2.0 * own
     if last:
-        joined = join_heights(*results, *heights, place < count - 1, place > 0)
-        next_partial_ref[...] = joined
-        put_faces(joined, next_cross_ref, next_core_ref, slice(None))
+        own, above, below = results
+        next_partial_ref[...] = own
+        above_ref[...] = above
+        below_ref[...] = below
+        joins = [(0, 1, place < count - 1), (2, 0, place > 0)]
+        join_heights([next_partial_ref, above_ref, below_ref], heights, joins)
+        put_faces(next_partial_ref[...], next_cross_ref, next_core_ref, slice(None))
     else:
         put_layers(results, heights, next_partial_ref, next_cross_ref, next_core_ref)
 
@@ -538,28 +533,31 @@
     first_outs = [field, (layers, 8, SPAN), field, face, face]
     step = time_step.reshape(1, 1)
     tile = (8, SPAN)
-    packed = call(
-        pack_kernel,
-        [(ROWS + 8, SPAN)],
-        [velocity.reshape(ROWS, SPAN), heights.reshape(1, 1)],
-    )
+    step = call(step_kernel, [tile], [mats, step], flops=2 * unit)
+    own_field = velocity.reshape(ROWS, SPAN)
+    packed = jnp.concatenate([own_field, jnp.broadcast_to(heights[:, None], (8, SPAN))], axis=0)
     if layers in (1, 2, 4):
-        slots = [packed]
-        for j in range(1, layers):
-            slots.append(lax.ppermute(packed, "vert", [(i, i ^ j) for i in range(layers)]))
-        own, step = call(own_layer_kernel, [(ROWS, SPAN), tile], [mats, packed, step], flops=unit)
-        fields, all_heights, partial, cross, core = call(
-            functools.partial(other_layers_kernel, layers),
-            first_outs,
-            [mats] + slots + [own],
-            scratch=[pltpu.VMEM(field, f32)],
-            flops=(layers - 1) * unit,
-        )
+        groups = {1: [[0]], 2: [[0], [1]], 4: [[0, 2], [3, 1]]}[layers]
+        slots = {0: packed}
+        for j in range(layers - 1, 0, -1):
+            slots[j] = lax.ppermute(packed, "vert", [(i, i ^ j) for i in range(layers)])
+        given = []
+        for group in groups[:-1]:
+            outs = [(ROWS, SPAN)] * len(group)
+            args = [mats, step] + [slots[j] for j in group]
+            raw = call(
+                functools.partial(raw_kernel, len(group)), outs, args, flops=len(group) * unit
+            )
+            given += [raw] if len(group) == 1 else raw
+        order = sum(groups, [])
+        args, scratch = [mats, step] + [slots[j] for j in order] + given, [pltpu.VMEM(field, f32)]
+        first = functools.partial(slots_kernel, order, len(given))
     else:
-        gathered = lax.all_gather(packed, "vert")
-        fields, all_heights, partial, cross, core, step = call(
-            functools.partial(first_kernel, layers), first_outs + [tile], [mats, gathered, step]
-        )
+        args, scratch = [mats, step, lax.all_gather(packed, "vert")], []
+        first = functools.partial(first_kernel, layers)
+    fields, all_heights, partial, cross, core = call(
+        first, first_outs, args, scratch=scratch, flops=layers * unit
+    )
     cross, core = swap_stream(cross, core)
     total = None
     for stage, share in enumerate((0.5, 0.5, 1.0)):
@@ -576,6 +574,7 @@
             functools.partial(stage_kernel, layers, share, stage == 0, last),
             [(ROWS, SPAN)] + ([(ROWS, SPAN), small, small] if last else [field, face, face]),
             args + ([] if stage == 0 else [total]),
+            scratch=[pltpu.VMEM((ROWS, SPAN), f32)] * 2,
             flops=used * unit,
         )
         cross, core = swap_stream(cross, core)

time: 41.8 us -> 39.9 us (0.955)
  waiting for transfers between devices: 16.9 us -> 15.2 us
    ppermute x3, waiting for transfers between devices: 5.04 us -> 3.37 us  [on_device(): slots[j] = lax.ppermute(packed, 'vert', [(i, i ^ j) for i in range(layers)])]
    concatenate x0 -> x1, local copies, waits for them, and re-layouts: none -> 0.9 us  [on_device(): jnp.concatenate([own_field, jnp.broadcast_to(heights[:, None], (8, SPAN))...]
    unnamed x6 -> x2, local copies, waits for them, and re-layouts: 2.14 us -> 1.25 us
  transfers between devices with their start and end apart: 11 -> 11, of which waited for: 6 -> 6; matrix products, arithmetic and copies ran while one was open for 0% -> 0% of each run, Pallas kernels for 5% -> 7%
where the time goes in v3:
time: 39.9 us; the launch traced here: 39.7 us
  waiting for transfers between devices  15.2 us (38%)
  starting transfers between devices  10.5 us (26%)
  Pallas kernels  10.5 us (26%)
  local copies, waits for them, and re-layouts  2.16 us (5%)
  between operations  1.37 us (3%)
    ppermute x4, waiting for transfers between devices, swap_stream(): lax.ppermute(cross, 'horiz', crosses)  11.8 us
    pallas_call x10, Pallas kernels, call(): pl.pallas_call(kernel, out_shape=shapes[0] if one else shapes, in_specs=[...  10.5 us
    ppermute x3, starting transfers between devices, on_device(): slots[j] = lax.ppermute(packed, 'vert', [(i, i ^ j) for i in range(layers)])  5.62 us
    ppermute x4, starting transfers between devices, swap_stream(): lax.ppermute(cross, 'horiz', crosses)  4.48 us
    ppermute x3, waiting for transfers between devices, on_device(): slots[j] = lax.ppermute(packed, 'vert', [(i, i ^ j) for i in range(layers)])  3.37 us
    unnamed x2, local copies, waits for them, and re-layouts  1.25 us
    concatenate x1, local copies, waits for them, and re-layouts, on_device(): jnp.concatenate([own_field, jnp.broadcast_to(heights[:, None], (8, SPAN))...  0.9 us
  transfers between devices with their start and end apart: 11, of which 6 were waited for; matrix products, arithmetic and copies ran while one was open for 0% of the time, Pallas kernels for 7%

profile of v3, /device:TPU:0, one launch (start us, length us, event | category | flops | bytes accessed | tf_op | source)
XLA Modules:
  0.0 39.7 jit_solution(12580625230322058955)
XLA Ops:
  0.7 0.9 %concatenate.3.refs_2_ = f32[200,128]{1,0:T(8,128)S(1)} pad(f32[192,128]{1,0:T(8,128)} %bitcast.6, f32[]{:T(128)} %bitcast.4), padding=0_8x0_0 | pad | bytes 200708 | tf_op jit(solution)/shard_map/concatenate | solution.py:538
  1.6 4.0 %collective-permute-start = (f32[200,128]{1,0:T(8,128)S(1)}, f32[200,128]{1,0:T(8,128)S(1)}, u32[]{:S(2)}, u32[]{:S(2)}) collective-permute-start(f32[200,128]{1,0:T(8,128)S(1)} %concatenate.3.refs_2_), channel_id=1, source_target_pairs={{0,2},{1,3},{2,0},{3,1},{4,6},{5,7},{6,4},{7,5},{8,10},{9,11},{10,... | collective-permute-start | bytes 307208 | tf_op jit(solution)/shard_map/ppermute | solution.py:543
  5.6 1.6 %collective-permute-start.2 = (f32[200,128]{1,0:T(8,128)S(1)}, f32[200,128]{1,0:T(8,128)S(1)}, u32[]{:S(2)}, u32[]{:S(2)}) collective-permute-start(f32[200,128]{1,0:T(8,128)S(1)} %concatenate.3.refs_2_), channel_id=1, source_target_pairs={{0,1},{1,0},{2,3},{3,2},{4,5},{5,4},{6,7},{7,6},{8,9},{9,8},{10,11... | collective-permute-start | bytes 307208 | tf_op jit(solution)/shard_map/ppermute | solution.py:543
  7.2 0.0 collective-permute-start.1
  7.8 0.0 copy-start
  7.8 1.2 %copy-done = bf16[2240,256]{1,0:T(8,128)(2,1)S(1)} copy-done((bf16[2240,256]{1,0:T(8,128)(2,1)S(1)}, bf16[2240,256]{1,0:T(8,128)(2,1)}, u32[]{:S(2)}) %copy-start) | copy-done | bytes 1146904
  9.1 0.1 shard_map.46.refs_1_.step_ref
  9.2 2.9 %collective-permute-done.refs_3_ = f32[200,128]{1,0:T(8,128)S(1)} collective-permute-done((f32[200,128]{1,0:T(8,128)S(1)}, f32[200,128]{1,0:T(8,128)S(1)}, u32[]{:S(2)}, u32[]{:S(2)}) %collective-permute-start) | collective-permute-done | bytes 102432 | tf_op jit(solution)/shard_map/ppermute | solution.py:543
  12.1 1.5 %shard_map.47 = (f32[192,128]{1,0:T(8,128)S(1)}, f32[192,128]{1,0:T(8,128)S(1)}) custom-call(bf16[2240,256]{1,0:T(8,128)(2,1)S(1)} %copy-done, f32[8,128]{1,0:T(8,128)S(1)} %shard_map.46.refs_1_.step_ref, f32[200,128]{1,0:T(8,128)S(1)} %concatenate.3.refs_2_, f32[200,128]{1,0:T(8,128)S(1)} %collective-permute-done.refs_3_), custom_call_target="tpu_custom_call" | custom-call | flops 786432000 | bytes 1048576 | tf_op jit(solution)/shard_map/pallas_call | solution.py:508
  13.6 0.0 collective-permute-done.2.refs_5_
  13.6 0.4 %collective-permute-done.1.refs_4_ = f32[200,128]{1,0:T(8,128)S(1)} collective-permute-done((f32[200,128]{1,0:T(8,128)S(1)}, f32[200,128]{1,0:T(8,128)S(1)}, u32[]{:S(2)}, u32[]{:S(2)}) %collective-permute-start.1) | collective-permute-done | bytes 102432 | tf_op jit(solution)/shard_map/ppermute | solution.py:543
  14.0 1.5 %shard_map.48 = (f32[4,192,128]{2,1,0:T(8,128)S(1)}, f32[4,8,128]{2,1,0:T(8,128)S(1)}, f32[4,192,128]{2,1,0:T(8,128)S(1)}, f32[4,3,8,128]{3,2,1,0:T(8,128)S(1)}, f32[4,3,8,128]{3,2,1,0:T(8,128)S(1)}) custom-call(bf16[2240,256]{1,0:T(8,128)(2,1)S(1)} %copy-done, f32[8,128]{1,0:T(8,128)S(1)} %shard_map.46.refs_1_.step_ref, f32[200,128]{1,0:T(8,128)S(1)} %concatenate.3.refs_2_, ...), custom_call_target="tpu_custom_call" | custom-call | flops 1572864000 | bytes 1048576 | tf_op jit(solution)/shard_map/pallas_call | solution.py:508
  15.6 1.3 %collective-permute-start.3 = (f32[4,3,8,128]{3,2,1,0:T(8,128)S(1)}, f32[4,3,8,128]{3,2,1,0:T(8,128)S(1)}, u32[]{:S(2)}, u32[]{:S(2)}) collective-permute-start(f32[4,3,8,128]{3,2,1,0:T(8,128)S(1)} %get-tuple-element.29), channel_id=1, source_target_pairs={{0,28},{4,8},{8,4},{12,16},{16,12},{20,24},{24,20},{28,0},{1,29},{... | collective-permute-start | bytes 147464 | tf_op jit(solution)/shard_map/ppermute | solution.py:523
  16.9 0.4 collective-permute-start.4
  17.2 0.4 %shard_map.49.refs_7_ = f32[6,2,144,128]{3,2,1,0:T(8,128)S(1)} custom-call(bf16[2240,256]{1,0:T(8,128)(2,1)S(1)} %copy-done, f32[8,128]{1,0:T(8,128)S(1)} %shard_map.46.refs_1_.step_ref, f32[4,192,128]{2,1,0:T(8,128)S(1)} %get-tuple-element.26.field_ref.refs_2_, f32[4,192,128]{2,1,0:T(8,128)S(1)} %get-tuple-element.28.partial_ref.refs_4_), custom_call_target="tpu_custom_call" | custom-call | flops 393216000 | bytes 1048576 | tf_op jit(solution)/shard_map/pallas_call | solution.py:508
  17.7 2.8 %collective-permute-done.3.refs_5_ = f32[4,3,8,128]{3,2,1,0:T(8,128)S(1)} collective-permute-done((f32[4,3,8,128]{3,2,1,0:T(8,128)S(1)}, f32[4,3,8,128]{3,2,1,0:T(8,128)S(1)}, u32[]{:S(2)}, u32[]{:S(2)}) %collective-permute-start.3) | collective-permute-done | bytes 49184 | tf_op jit(solution)/shard_map/ppermute | solution.py:523
  20.5 0.0 collective-permute-done.4.refs_6_
  20.5 1.9 %shard_map.50 = (f32[192,128]{1,0:T(8,128)S(1)}, f32[4,192,128]{2,1,0:T(8,128)S(1)}, f32[4,3,8,128]{3,2,1,0:T(8,128)S(1)}, f32[4,3,8,128]{3,2,1,0:T(8,128)S(1)}) custom-call(bf16[2240,256]{1,0:T(8,128)(2,1)S(1)} %copy-done, f32[8,128]{1,0:T(8,128)S(1)} %shard_map.46.refs_1_.step_ref, f32[4,192,128]{2,1,0:T(8,128)S(1)} %get-tuple-element.26.field_ref.refs_2_, ...), custom_call_target="tpu_custom_call" | custom-call | flops 1572864000 | bytes 1048576 | tf_op jit(solution)/shard_map/pallas_call | solution.py:508
  22.4 1.1 %collective-permute-start.5 = (f32[4,3,8,128]{3,2,1,0:T(8,128)S(1)}, f32[4,3,8,128]{3,2,1,0:T(8,128)S(1)}, u32[]{:S(2)}, u32[]{:S(2)}) collective-permute-start(f32[4,3,8,128]{3,2,1,0:T(8,128)S(1)} %get-tuple-element.32), channel_id=1, source_target_pairs={{0,28},{4,8},{8,4},{12,16},{16,12},{20,24},{24,20},{28,0},{1,29},{... | collective-permute-start | bytes 147464 | tf_op jit(solution)/shard_map/ppermute | solution.py:523
  23.5 0.0 collective-permute-start.6
  23.5 0.4 %shard_map.51.refs_7_ = f32[6,2,144,128]{3,2,1,0:T(8,128)S(1)} custom-call(bf16[2240,256]{1,0:T(8,128)(2,1)S(1)} %copy-done, f32[8,128]{1,0:T(8,128)S(1)} %shard_map.46.refs_1_.step_ref, f32[4,192,128]{2,1,0:T(8,128)S(1)} %get-tuple-element.26.field_ref.refs_2_, f32[4,192,128]{2,1,0:T(8,128)S(1)} %get-tuple-element.31.partial_ref.refs_4_), custom_call_target="tpu_custom_call" | custom-call | flops 393216000 | bytes 1048576 | tf_op jit(solution)/shard_map/pallas_call | solution.py:508
  23.9 3.0 %collective-permute-done.5.refs_5_ = f32[4,3,8,128]{3,2,1,0:T(8,128)S(1)} collective-permute-done((f32[4,3,8,128]{3,2,1,0:T(8,128)S(1)}, f32[4,3,8,128]{3,2,1,0:T(8,128)S(1)}, u32[]{:S(2)}, u32[]{:S(2)}) %collective-permute-start.5) | collective-permute-done | bytes 49184 | tf_op jit(solution)/shard_map/ppermute | solution.py:523
  26.9 0.0 collective-permute-done.6.refs_6_
  26.9 1.9 %shard_map.52 = (f32[192,128]{1,0:T(8,128)S(1)}, f32[4,192,128]{2,1,0:T(8,128)S(1)}, f32[4,3,8,128]{3,2,1,0:T(8,128)S(1)}, f32[4,3,8,128]{3,2,1,0:T(8,128)S(1)}) custom-call(bf16[2240,256]{1,0:T(8,128)(2,1)S(1)} %copy-done, f32[8,128]{1,0:T(8,128)S(1)} %shard_map.46.refs_1_.step_ref, f32[4,192,128]{2,1,0:T(8,128)S(1)} %get-tuple-element.26.field_ref.refs_2_, ...), custom_call_target="tpu_custom_call" | custom-call | flops 1572864000 | bytes 1048576 | tf_op jit(solution)/shard_map/pallas_call | solution.py:508
  28.8 1.1 %collective-permute-start.7 = (f32[4,3,8,128]{3,2,1,0:T(8,128)S(1)}, f32[4,3,8,128]{3,2,1,0:T(8,128)S(1)}, u32[]{:S(2)}, u32[]{:S(2)}) collective-permute-start(f32[4,3,8,128]{3,2,1,0:T(8,128)S(1)} %get-tuple-element.36), channel_id=1, source_target_pairs={{0,28},{4,8},{8,4},{12,16},{16,12},{20,24},{24,20},{28,0},{1,29},{... | collective-permute-start | bytes 147464 | tf_op jit(solution)/shard_map/ppermute | solution.py:523
  29.9 0.0 collective-permute-start.8
  29.9 0.4 shard_map.53.refs_7_
  30.3 3.0 %collective-permute-done.7.refs_5_ = f32[4,3,8,128]{3,2,1,0:T(8,128)S(1)} collective-permute-done((f32[4,3,8,128]{3,2,1,0:T(8,128)S(1)}, f32[4,3,8,128]{3,2,1,0:T(8,128)S(1)}, u32[]{:S(2)}, u32[]{:S(2)}) %collective-permute-start.7) | collective-permute-done | bytes 49184 | tf_op jit(solution)/shard_map/ppermute | solution.py:523
  33.3 0.0 collective-permute-done.8.refs_6_
  33.3 1.7 %shard_map.54 = (f32[192,128]{1,0:T(8,128)S(1)}, f32[192,128]{1,0:T(8,128)S(1)}, f32[3,8,128]{2,1,0:T(8,128)S(1)}, f32[3,8,128]{2,1,0:T(8,128)S(1)}) custom-call(bf16[2240,256]{1,0:T(8,128)(2,1)S(1)} %copy-done, f32[8,128]{1,0:T(8,128)S(1)} %shard_map.46.refs_1_.step_ref, f32[4,192,128]{2,1,0:T(8,128)S(1)} %get-tuple-element.26.field_ref.refs_2_, ...), custom_call_target="tpu_custom_call" | custom-call | flops 1179648000 | bytes 1048576 | tf_op jit(solution)/shard_map/pallas_call | solution.py:508
  35.0 1.1 %collective-permute-start.9 = (f32[3,8,128]{2,1,0:T(8,128)S(1)}, f32[3,8,128]{2,1,0:T(8,128)S(1)}, u32[]{:S(2)}, u32[]{:S(2)}) collective-permute-start(f32[3,8,128]{2,1,0:T(8,128)S(1)} %get-tuple-element.40), channel_id=1, source_target_pairs={{0,28},{4,8},{8,4},{12,16},{16,12},{20,24},{24,20},{28,0},{1,29},{... | collective-permute-start | bytes 36872 | tf_op jit(solution)/shard_map/ppermute | solution.py:523
  36.1 0.0 collective-permute-start.10
  36.1 3.0 %collective-permute-done.9.cross_ref = f32[3,8,128]{2,1,0:T(8,128)S(1)} collective-permute-done((f32[3,8,128]{2,1,0:T(8,128)S(1)}, f32[3,8,128]{2,1,0:T(8,128)S(1)}, u32[]{:S(2)}, u32[]{:S(2)}) %collective-permute-start.9) | collective-permute-done | bytes 12320 | tf_op jit(solution)/shard_map/ppermute | solution.py:523
  39.1 0.0 collective-permute-done.10.core_ref
  39.1 0.7 %shard_map.55 = f32[192,128]{1,0:T(8,128)} custom-call(f32[192,128]{1,0:T(8,128)S(1)} %get-tuple-element.39.partial_ref, f32[3,8,128]{2,1,0:T(8,128)S(1)} %collective-permute-done.9.cross_ref, f32[3,8,128]{2,1,0:T(8,128)S(1)} %collective-permute-done.10.core_ref, f32[192,128]{1,0:T(8,128)S(1)} %get-tuple-element.42.total_ref), custom_call_target="tpu_custom_call" | custom-call | bytes 1048576 | tf_op jit(solution)/shard_map/pallas_call | solution.py:508
Async XLA Ops:
  1.6 10.5 %collective-permute-start = (f32[200,128]{1,0:T(8,128)S(1)}, f32[200,128]{1,0:T(8,128)S(1)}, u32[]{:S(2)}, u32[]{:S(2)}) collective-permute-start(f32[200,128]{1,0:T(8,128)S(1)} %concatenate.3.refs_2_), channel_id=1, source_target_pairs={{0,2},{1,3},{2,0},{3,1},{4,6},{5,7},{6,4},{7,5},{8,10},{9,11},{10,... | collective-permute-start | bytes 307208 | tf_op jit(solution)/shard_map/ppermute | solution.py:543
  5.6 8.0 %collective-permute-start.2 = (f32[200,128]{1,0:T(8,128)S(1)}, f32[200,128]{1,0:T(8,128)S(1)}, u32[]{:S(2)}, u32[]{:S(2)}) collective-permute-start(f32[200,128]{1,0:T(8,128)S(1)} %concatenate.3.refs_2_), channel_id=1, source_target_pairs={{0,1},{1,0},{2,3},{3,2},{4,5},{5,4},{6,7},{7,6},{8,9},{9,8},{10,11... | collective-permute-start | bytes 307208 | tf_op jit(solution)/shard_map/ppermute | solution.py:543
  7.2 6.9 %collective-permute-start.1 = (f32[200,128]{1,0:T(8,128)S(1)}, f32[200,128]{1,0:T(8,128)S(1)}, u32[]{:S(2)}, u32[]{:S(2)}) collective-permute-start(f32[200,128]{1,0:T(8,128)S(1)} %concatenate.3.refs_2_), channel_id=1, source_target_pairs={{0,3},{1,2},{2,1},{3,0},{4,7},{5,6},{6,5},{7,4},{8,11},{9,10},{10,... | collective-permute-start | bytes 307208 | tf_op jit(solution)/shard_map/ppermute | solution.py:543
  7.8 1.3 %copy-start = (bf16[2240,256]{1,0:T(8,128)(2,1)S(1)}, bf16[2240,256]{1,0:T(8,128)(2,1)}, u32[]{:S(2)}) copy-start(bf16[2240,256]{1,0:T(8,128)(2,1)} %constant.2.clone.mats.refs_0_) | copy-start | bytes 3440644
  15.6 4.9 %collective-permute-start.3 = (f32[4,3,8,128]{3,2,1,0:T(8,128)S(1)}, f32[4,3,8,128]{3,2,1,0:T(8,128)S(1)}, u32[]{:S(2)}, u32[]{:S(2)}) collective-permute-start(f32[4,3,8,128]{3,2,1,0:T(8,128)S(1)} %get-tuple-element.29), channel_id=1, source_target_pairs={{0,28},{4,8},{8,4},{12,16},{16,12},{20,24},{24,20},{28,0},{1,29},{... | collective-permute-start | bytes 147464 | tf_op jit(solution)/shard_map/ppermute | solution.py:523
  16.9 3.6 %collective-permute-start.4 = (f32[4,3,8,128]{3,2,1,0:T(8,128)S(1)}, f32[4,3,8,128]{3,2,1,0:T(8,128)S(1)}, u32[]{:S(2)}, u32[]{:S(2)}) collective-permute-start(f32[4,3,8,128]{3,2,1,0:T(8,128)S(1)} %get-tuple-element.30), channel_id=1, source_target_pairs={{0,4},{4,0},{8,12},{12,8},{16,20},{20,16},{24,28},{28,24},{1,5},{5... | collective-permute-start | bytes 147464 | tf_op jit(solution)/shard_map/ppermute | solution.py:523
  22.4 4.5 %collective-permute-start.5 = (f32[4,3,8,128]{3,2,1,0:T(8,128)S(1)}, f32[4,3,8,128]{3,2,1,0:T(8,128)S(1)}, u32[]{:S(2)}, u32[]{:S(2)}) collective-permute-start(f32[4,3,8,128]{3,2,1,0:T(8,128)S(1)} %get-tuple-element.32), channel_id=1, source_target_pairs={{0,28},{4,8},{8,4},{12,16},{16,12},{20,24},{24,20},{28,0},{1,29},{... | collective-permute-start | bytes 147464 | tf_op jit(solution)/shard_map/ppermute | solution.py:523
  23.5 3.4 %collective-permute-start.6 = (f32[4,3,8,128]{3,2,1,0:T(8,128)S(1)}, f32[4,3,8,128]{3,2,1,0:T(8,128)S(1)}, u32[]{:S(2)}, u32[]{:S(2)}) collective-permute-start(f32[4,3,8,128]{3,2,1,0:T(8,128)S(1)} %get-tuple-element.33), channel_id=1, source_target_pairs={{0,4},{4,0},{8,12},{12,8},{16,20},{20,16},{24,28},{28,24},{1,5},{5... | collective-permute-start | bytes 147464 | tf_op jit(solution)/shard_map/ppermute | solution.py:523
  28.8 4.5 %collective-permute-start.7 = (f32[4,3,8,128]{3,2,1,0:T(8,128)S(1)}, f32[4,3,8,128]{3,2,1,0:T(8,128)S(1)}, u32[]{:S(2)}, u32[]{:S(2)}) collective-permute-start(f32[4,3,8,128]{3,2,1,0:T(8,128)S(1)} %get-tuple-element.36), channel_id=1, source_target_pairs={{0,28},{4,8},{8,4},{12,16},{16,12},{20,24},{24,20},{28,0},{1,29},{... | collective-permute-start | bytes 147464 | tf_op jit(solution)/shard_map/ppermute | solution.py:523
  29.9 3.4 %collective-permute-start.8 = (f32[4,3,8,128]{3,2,1,0:T(8,128)S(1)}, f32[4,3,8,128]{3,2,1,0:T(8,128)S(1)}, u32[]{:S(2)}, u32[]{:S(2)}) collective-permute-start(f32[4,3,8,128]{3,2,1,0:T(8,128)S(1)} %get-tuple-element.37), channel_id=1, source_target_pairs={{0,4},{4,0},{8,12},{12,8},{16,20},{20,16},{24,28},{28,24},{1,5},{5... | collective-permute-start | bytes 147464 | tf_op jit(solution)/shard_map/ppermute | solution.py:523
  35.0 4.1 %collective-permute-start.9 = (f32[3,8,128]{2,1,0:T(8,128)S(1)}, f32[3,8,128]{2,1,0:T(8,128)S(1)}, u32[]{:S(2)}, u32[]{:S(2)}) collective-permute-start(f32[3,8,128]{2,1,0:T(8,128)S(1)} %get-tuple-element.40), channel_id=1, source_target_pairs={{0,28},{4,8},{8,4},{12,16},{16,12},{20,24},{24,20},{28,0},{1,29},{... | collective-permute-start | bytes 36872 | tf_op jit(solution)/shard_map/ppermute | solution.py:523
  36.1 3.0 %collective-permute-start.10 = (f32[3,8,128]{2,1,0:T(8,128)S(1)}, f32[3,8,128]{2,1,0:T(8,128)S(1)}, u32[]{:S(2)}, u32[]{:S(2)}) collective-permute-start(f32[3,8,128]{2,1,0:T(8,128)S(1)} %get-tuple-element.41), channel_id=1, source_target_pairs={{0,4},{4,0},{8,12},{12,8},{16,20},{20,16},{24,28},{28,24},{1,5},{5... | collective-permute-start | bytes 36872 | tf_op jit(solution)/shard_map/ppermute | solution.py:523

commit v4 on v3

--- a/solution.py
+++ b/solution.py
@@ -281,15 +281,9 @@
         results += [out[:, i * SPAN : (i + 1) * SPAN] for i in range(size)]
 
 
-def weak_layers(fields, inverses, mats):
-    return weak_spots(span_forward(fields, mats), inverses, mats)
-
-
-def weak_spots(spots, inverses, mats):
-    count = len(inverses)
-    chunks = chunks_of(count)
+def weak_spots(spots, inverses, mats, put):
+    chunks = chunks_of(len(inverses))
     planes = []
-    backs, results = [], []
 
     def finish(i):
         def fine(c, kind, rows):
@@ -299,15 +293,34 @@
             return first[kind * 144 + rows.start : kind * 144 + rows.stop]
 
         out = convect_back(fine, chunk_inverse(chunks[i], inverses), mats)
-        backs.extend(out[:, j * SPAN : (j + 1) * SPAN] for j in range(len(chunks[i])))
-        span_back(count, backs, results, mats)
+        for j in range(len(chunks[i])):
+            put(2 * i + j, out[:, j * SPAN : (j + 1) * SPAN])
 
     for i in range(len(chunks)):
         planes.append(plane_forward(spots[2 * i : 2 * i + 2], mats))
         if i > 0:
             finish(i - 1)
     finish(len(chunks) - 1)
+
+
+def weak_layers(fields, inverses, mats):
+    backs, results = [], []
+
+    def put(place, back):
+        backs.append(back)
+        span_back(len(fields), backs, results, mats)
+
+    weak_spots(span_forward(fields, mats), inverses, mats, put)
     return results
+
+
+def end_rows(x):
+    x = x.reshape(3, 8, 8, SPAN)
+    return jnp.concatenate([x[:, :1], x[:, 7:]], axis=1).reshape(48, SPAN)
+
+
+def inner_rows(x):
+    return x.reshape(3, 8, 8, SPAN)[:, 1:7].reshape(144, SPAN)
 
 
 def face_spots(faces, mats):
@@ -332,23 +345,20 @@
     return jnp.concatenate([faces[:, :1], inner, faces[:, 1:]], axis=1).reshape(ROWS, SPAN)
 
 
-def height_rows(level, rows=ROWS):
-    return pl.ds(level, rows // 8, stride=8)
-
-
 def join_heights(layers, heights, joins):
+    rows = layers[0].shape[0] // 8
+    top, bottom = pl.ds(7, rows, stride=8), pl.ds(0, rows, stride=8)
     for lower, upper, wanted in joins:
         share = heights[upper] / (heights[lower] + heights[upper])
         share = share[:1]
-        below = layers[lower][height_rows(7), :]
-        above = layers[upper][height_rows(0), :]
+        below, above = layers[lower][top, :], layers[upper][bottom, :]
         mean = below * (1.0 - share) + above * share
         if wanted is True:
-            layers[lower][height_rows(7), :] = mean
-            layers[upper][height_rows(0), :] = mean
+            layers[lower][top, :] = mean
+            layers[upper][bottom, :] = mean
         else:
-            layers[lower][height_rows(7), :] = jnp.where(wanted, mean, below)
-            layers[upper][height_rows(0), :] = jnp.where(wanted, mean, above)
+            layers[lower][top, :] = jnp.where(wanted, mean, below)
+            layers[upper][bottom, :] = jnp.where(wanted, mean, above)
 
 
 def sides():
@@ -358,39 +368,34 @@
     return lax.rem(place, 2) == 1, left_share, right_share
 
 
-def join_ends(own, cross, core):
+def join_ends(own_cross, own_core, cross, core):
     odd, left_share, right_share = sides()
-    left = jnp.where(odd, core, cross)
-    right = jnp.where(odd, cross, core)
-    own = own.reshape(3, 8, 8, SPAN)
-    first = own[:, 0] * (1.0 - left_share) + left * left_share
-    last = own[:, 7] * (1.0 - right_share) + right * right_share
-    return first, last
-
-
-def join_stream(own, cross, core):
-    first, last = join_ends(own, cross, core)
-    own = own.reshape(3, 8, 8, SPAN)
-    out = jnp.concatenate([first[:, None], own[:, 1:7], last[:, None]], axis=1)
-    return out.reshape(ROWS, SPAN)
-
-
-def put_faces(own, cross_ref, core_ref, at):
-    odd = lax.rem(lax.axis_index("horiz"), 2) == 1
-    own = own.reshape(3, 8, 8, SPAN)
-    first, last = own[:, 0], own[:, 7]
+    cross_share = jnp.where(odd, right_share, left_share)
+    core_share = jnp.where(odd, left_share, right_share)
+    cross = own_cross * (1.0 - cross_share) + cross * cross_share
+    return cross, own_core * (1.0 - core_share) + core * core_share
+
+
+def in_order(cross, core):
+    odd = sides()[0]
+    ends = jnp.where(odd, core, cross), jnp.where(odd, cross, core)
+    return jnp.concatenate([end[:, None] for end in ends], axis=1)
+
+
+def put_faces(ends, cross_ref, core_ref, at):
+    odd = sides()[0]
+    ends = ends.reshape(3, 2, 8, SPAN)
+    first, last = ends[:, 0], ends[:, 1]
     cross_ref[at] = jnp.where(odd, last, first)
     core_ref[at] = jnp.where(odd, first, last)
 
 
-def put_layers(results, heights, partial_ref, cross_ref, core_ref):
-    count = len(results)
-    for l in range(count):
-        partial_ref[l] = results[l]
+def join_layers(heights, partial_ref, cross_ref, core_ref):
+    count = len(heights)
     layers = [partial_ref.at[l] for l in range(count)]
     join_heights(layers, heights, [(l, l + 1, True) for l in range(count - 1)])
     for l in range(count):
-        put_faces(partial_ref[l], cross_ref, core_ref, l)
+        put_faces(end_rows(partial_ref[l]), cross_ref, core_ref, l)
 
 
 def step_kernel(mats, step_ref, tile_ref):
@@ -409,23 +414,23 @@
 def slots_kernel(order, ready, *refs):
     count = len(order)
     mats, packed, given = refs[0], refs[2 : count + 2], refs[count + 2 : count + 2 + ready]
-    field_ref, heights_ref, partial_ref, cross_ref, core_ref, raw_ref = refs[count + 2 + ready :]
+    field_ref, heights_ref, partial_ref, cross_ref, core_ref = refs[count + 2 + ready :]
     place = lax.axis_index("vert")
     slots = [jnp.bitwise_xor(place, j) for j in order]
     for i in range(count):
         field_ref[slots[i]] = packed[i][:ROWS]
         heights_ref[slots[i]] = packed[i][ROWS:]
     for i in range(ready):
-        raw_ref[slots[i]] = given[i][...]
+        partial_ref[slots[i]] = given[i][...]
     results = weak_layers(
         [packed[i][:ROWS] for i in range(ready, count)],
         [1.0 / packed[i][ROWS : ROWS + 1] for i in range(ready, count)],
         mats,
     )
     for i in range(ready, count):
-        raw_ref[slots[i]] = results[i - ready]
+        partial_ref[slots[i]] = results[i - ready]
     heights = [heights_ref[l] for l in range(count)]
-    put_layers([raw_ref[l] for l in range(count)], heights, partial_ref, cross_ref, core_ref)
+    join_layers(heights, partial_ref, cross_ref, core_ref)
 
 
 def first_kernel(count, *refs):
@@ -438,7 +443,9 @@
     results = weak_layers(
         [packed_ref[l, :ROWS] for l in range(count)], [1.0 / h[:1] for h in heights], mats
     )
-    put_layers(results, heights, partial_ref, cross_ref, core_ref)
+    for l in range(count):
+        partial_ref[l] = results[l]
+    join_layers(heights, partial_ref, cross_ref, core_ref)
 
 
 def stage_layers(count, last):
@@ -448,55 +455,101 @@
     return [place, jnp.minimum(place + 1, count - 1), jnp.maximum(place - 1, 0)]
 
 
-def inner_kernel(count, share, last, mats, step_ref, field_ref, partial_ref, spots_ref):
+def put_spots(partial, count, share, last, mats, step_ref, field_ref, spots_ref):
     step = step_ref[:1] * share
     fields = []
     for l in stage_layers(count, last):
-        field = (field_ref[l] + step * partial_ref[l]).reshape(3, 8, 8, SPAN)
-        fields.append(field[:, 1:7].reshape(144, SPAN))
+        fields.append(inner_rows(field_ref[l]) + step * partial(l))
     for i, pair in enumerate(span_forward(fields, mats)):
         for part in range(2):
             spots_ref[i, part] = pair[part]
 
 
+def first_inner_kernel(
+    count, share, last, mats, step_ref, field_ref, partial_ref, spots_ref, total_ref
+):
+    def partial(l):
+        return inner_rows(partial_ref[l])
+
+    put_spots(partial, count, share, last, mats, step_ref, field_ref, spots_ref)
+    total_ref[...] = partial(lax.axis_index("vert"))
+
+
+def span_inner(backs_ref, partial_ref, count, mats):
+    results = []
+    span_back(count, [inner_rows(backs_ref[i]) for i in range(len(spots_of(count)))], results, mats)
+    for l in range(count):
+        partial_ref[l] = results[l]
+
+
+def inner_kernel(count, share, last, *refs):
+    mats, step_ref, field_ref, heights_ref, backs_ref, total_ref, spots_ref = refs[:7]
+    next_total_ref, partial_ref = refs[7:]
+    span_inner(backs_ref, partial_ref, count, mats)
+    layers = [partial_ref.at[l] for l in range(count)]
+    heights = [heights_ref[l] for l in range(count)]
+    join_heights(layers, heights, [(l, l + 1, True) for l in range(count - 1)])
+
+    def partial(l):
+        return partial_ref[l]
+
+    put_spots(partial, count, share, last, mats, step_ref, field_ref, spots_ref)
+    next_total_ref[...] = total_ref[...] + 2.0 * partial(lax.axis_index("vert"))
+
+
+def last_inner_kernel(count, mats, heights_ref, backs_ref, total_ref, rate_ref, partial_ref):
+    place = lax.axis_index("vert")
+    span_inner(backs_ref, partial_ref, 3, mats)
+    heights = [heights_ref[l] for l in stage_layers(count, True)]
+    layers = [partial_ref.at[i] for i in range(3)]
+    join_heights(layers, heights, [(0, 1, place < count - 1), (2, 0, place > 0)])
+    rate_ref[...] = (total_ref[...] + partial_ref[0]) / 6.0
+
+
 def stage_kernel(count, share, first, last, *refs):
-    mats, step_ref, field_ref, heights_ref, partial_ref, cross_ref, core_ref, spots_ref = refs[:8]
-    refs = refs[8:]
-    total = None if first else refs[0][...]
-    *outs, above_ref, below_ref = refs[-6:]
-    total_ref, next_partial_ref, next_cross_ref, next_core_ref = outs
+    mats, step_ref, field_ref, heights_ref, own_cross_ref, own_core_ref = refs[:6]
+    cross_ref, core_ref, spots_ref = refs[6:9]
+    total = None if first else refs[9]
+    total_ref, backs_ref, next_cross_ref, next_core_ref, faces_ref = refs[-5:]
     place = lax.axis_index("vert")
     step = step_ref[:1] * share
     layers = stage_layers(count, last)
     heights = [heights_ref[l] for l in layers]
-    faces = []
+    fields = []
     for l in layers:
-        ends = join_ends(partial_ref[l], cross_ref[l], core_ref[l])
-        ends = jnp.concatenate([end[:, None] for end in ends], axis=1)
-        field = field_ref[l].reshape(3, 8, 8, SPAN)
-        field = jnp.concatenate([field[:, :1], field[:, 7:]], axis=1)
-        faces.append((field + step * ends).reshape(48, SPAN))
+        ends = join_ends(own_cross_ref[l], own_core_ref[l], cross_ref[l], core_ref[l])
+        ends = in_order(*ends).reshape(48, SPAN)
+        fields.append(end_rows(field_ref[l]) + step * ends)
     spots = []
-    for i, pair in enumerate(face_spots(faces, mats)):
+    for i, pair in enumerate(face_spots(fields, mats)):
         spots.append([with_faces(spots_ref[i, part], pair[part]) for part in range(2)])
-    results = weak_spots(spots, [1.0 / h[:1] for h in heights], mats)
-    own = join_stream(partial_ref[place], cross_ref[place], core_ref[place])
-    total_ref[...] = own if first else total + 2.0 * own
+    ends, results = [], []
+
+    def put(i, back):
+        backs_ref[i] = back
+        ends.append(end_rows(back))
+        span_back(len(layers), ends, results, mats)
+
+    weak_spots(spots, [1.0 / h[:1] for h in heights], mats, put)
+    for i, result in enumerate(results):
+        faces_ref[i] = result
+    faces = [faces_ref.at[i] for i in range(len(layers))]
     if last:
-        own, above, below = results
-        next_partial_ref[...] = own
-        above_ref[...] = above
-        below_ref[...] = below
-        joins = [(0, 1, place < count - 1), (2, 0, place > 0)]
-        join_heights([next_partial_ref, above_ref, below_ref], heights, joins)
-        put_faces(next_partial_ref[...], next_cross_ref, next_core_ref, slice(None))
+        join_heights(faces, heights, [(0, 1, place < count - 1), (2, 0, place > 0)])
+        put_faces(faces_ref[0], next_cross_ref, next_core_ref, slice(None))
     else:
-        put_layers(results, heights, next_partial_ref, next_cross_ref, next_core_ref)
-
-
-def rate_kernel(partial_ref, cross_ref, core_ref, total_ref, rate_ref):
-    slope = join_stream(partial_ref[...], cross_ref[...], core_ref[...])
-    rate_ref[...] = (total_ref[...] + slope) / 6.0
+        join_heights(faces, heights, [(l, l + 1, True) for l in range(count - 1)])
+        for l in range(count):
+            put_faces(faces_ref[l], next_cross_ref, next_core_ref, l)
+    own = join_ends(own_cross_ref[place], own_core_ref[place], cross_ref[place], core_ref[place])
+    for k in range(2):
+        total_ref[k] = own[k] if first else total[k] + 2.0 * own[k]
+
+
+def rate_kernel(own_cross_ref, own_core_ref, cross_ref, core_ref, inner_ref, total_ref, rate_ref):
+    ends = join_ends(own_cross_ref[...], own_core_ref[...], cross_ref[...], core_ref[...])
+    ends = [(total_ref[k] + ends[k]) / 6.0 for k in range(2)]
+    rate_ref[...] = with_faces(inner_ref[...], in_order(*ends))
 
 
 VMEM = pl.BlockSpec(memory_space=pltpu.VMEM)
@@ -550,35 +603,55 @@
             )
             given += [raw] if len(group) == 1 else raw
         order = sum(groups, [])
-        args, scratch = [mats, step] + [slots[j] for j in order] + given, [pltpu.VMEM(field, f32)]
+        args = [mats, step] + [slots[j] for j in order] + given
         first = functools.partial(slots_kernel, order, len(given))
     else:
-        args, scratch = [mats, step, lax.all_gather(packed, "vert")], []
+        args = [mats, step, lax.all_gather(packed, "vert")]
         first = functools.partial(first_kernel, layers)
     fields, all_heights, partial, cross, core = call(
-        first, first_outs, args, scratch=scratch, flops=layers * unit
-    )
-    cross, core = swap_stream(cross, core)
-    total = None
+        first, first_outs, args, flops=layers * unit
+    )
+    own_ends = cross, core
+    ends = swap_stream(cross, core)
+    backs = face_total = None
     for stage, share in enumerate((0.5, 0.5, 1.0)):
         last = stage == 2
         used = 3 if last else layers
-        spots = call(
-            functools.partial(inner_kernel, layers, share, last),
-            [(len(spots_of(used)), 2, 144, SPAN)],
-            [mats, step, fields, partial],
-            flops=used * unit // 4,
-        )
-        args = [mats, step, fields, all_heights, partial, cross, core, spots]
-        total, partial, cross, core = call(
+        outs = [(len(spots_of(used)), 2, 144, SPAN), (144, SPAN)]
+        if stage == 0:
+            spots, total = call(
+                functools.partial(first_inner_kernel, layers, share, last),
+                outs,
+                [mats, step, fields, partial],
+                flops=used * unit // 4,
+            )
+        else:
+            spots, total = call(
+                functools.partial(inner_kernel, layers, share, last),
+                outs,
+                [mats, step, fields, all_heights, backs, total],
+                scratch=[pltpu.VMEM((layers, 144, SPAN), f32)],
+                flops=used * unit // 2,
+            )
+        args = [mats, step, fields, all_heights, *own_ends, *ends, spots]
+        end = small if last else face
+        face_total, backs, cross, core = call(
             functools.partial(stage_kernel, layers, share, stage == 0, last),
-            [(ROWS, SPAN)] + ([(ROWS, SPAN), small, small] if last else [field, face, face]),
-            args + ([] if stage == 0 else [total]),
-            scratch=[pltpu.VMEM((ROWS, SPAN), f32)] * 2,
+            [(2,) + small, (len(spots_of(used)), ROWS, SPAN), end, end],
+            args + ([] if stage == 0 else [face_total]),
+            scratch=[pltpu.VMEM((used, 48, SPAN), f32)],
             flops=used * unit,
         )
-        cross, core = swap_stream(cross, core)
-    rate = call(rate_kernel, [(ROWS, SPAN)], [partial, cross, core, total])
+        own_ends = cross, core
+        ends = swap_stream(cross, core)
+    inner = call(
+        functools.partial(last_inner_kernel, layers),
+        [(144, SPAN)],
+        [mats, all_heights, backs, total],
+        scratch=[pltpu.VMEM((3, 144, SPAN), f32)],
+        flops=unit // 2,
+    )
+    rate = call(rate_kernel, [(ROWS, SPAN)], [*own_ends, *ends, inner, face_total])
     return rate.reshape(velocity.shape)
 
 

time: 39.9 us -> 39.5 us (0.990)
  waiting for transfers between devices: 15.2 us -> 14.1 us
  Pallas kernels: 10.5 us -> 11.1 us
    ppermute x4, waiting for transfers between devices: 11.8 us -> 10.7 us  [swap_stream(): lax.ppermute(cross, 'horiz', crosses)]
    pallas_call x10 -> x11, Pallas kernels: 10.5 us -> 11.1 us  [call(): pl.pallas_call(kernel, out_shape=shapes[0] if one else shapes, in_specs=[...]
  transfers between devices with their start and end apart: 11 -> 11, of which waited for: 6 -> 6; matrix products, arithmetic and copies ran while one was open for 0% -> 0% of each run, Pallas kernels for 7% -> 10%
where the time goes in v4:
time: 39.5 us; the launch traced here: 39.3 us
  waiting for transfers between devices  14.1 us (36%)
  Pallas kernels  11.1 us (28%)
  starting transfers between devices  10.5 us (27%)
  local copies, waits for them, and re-layouts  2.16 us (5%)
  between operations  1.38 us (3%)
    pallas_call x11, Pallas kernels, call(): pl.pallas_call(kernel, out_shape=shapes[0] if one else shapes, in_specs=[...  11.1 us
    ppermute x4, waiting for transfers between devices, swap_stream(): lax.ppermute(cross, 'horiz', crosses)  10.7 us
    ppermute x3, starting transfers between devices, on_device(): slots[j] = lax.ppermute(packed, 'vert', [(i, i ^ j) for i in range(layers)])  5.62 us
    ppermute x4, starting transfers between devices, swap_stream(): lax.ppermute(cross, 'horiz', crosses)  4.51 us
    ppermute x3, waiting for transfers between devices, on_device(): slots[j] = lax.ppermute(packed, 'vert', [(i, i ^ j) for i in range(layers)])  3.37 us
    unnamed x2, local copies, waits for them, and re-layouts  1.25 us
    concatenate x1, local copies, waits for them, and re-layouts, on_device(): jnp.concatenate([own_field, jnp.broadcast_to(heights[:, None], (8, SPAN))...  0.9 us
  transfers between devices with their start and end apart: 11, of which 6 were waited for; matrix products, arithmetic and copies ran while one was open for 0% of the time, Pallas kernels for 10%

profile of v4, /device:TPU:0, one launch (start us, length us, event | category | flops | bytes accessed | tf_op | source)
XLA Modules:
  0.0 39.3 jit_solution(10120328992142257043)
XLA Ops:
  0.7 0.9 %concatenate.3.refs_2_ = f32[200,128]{1,0:T(8,128)S(1)} pad(f32[192,128]{1,0:T(8,128)} %bitcast.6, f32[]{:T(128)} %bitcast.4), padding=0_8x0_0 | pad | bytes 200708 | tf_op jit(solution)/shard_map/concatenate | solution.py:591
  1.6 4.0 %collective-permute-start = (f32[200,128]{1,0:T(8,128)S(1)}, f32[200,128]{1,0:T(8,128)S(1)}, u32[]{:S(2)}, u32[]{:S(2)}) collective-permute-start(f32[200,128]{1,0:T(8,128)S(1)} %concatenate.3.refs_2_), channel_id=1, source_target_pairs={{0,2},{1,3},{2,0},{3,1},{4,6},{5,7},{6,4},{7,5},{8,10},{9,11},{10,... | collective-permute-start | bytes 307208 | tf_op jit(solution)/shard_map/ppermute | solution.py:596
  5.6 1.6 %collective-permute-start.2 = (f32[200,128]{1,0:T(8,128)S(1)}, f32[200,128]{1,0:T(8,128)S(1)}, u32[]{:S(2)}, u32[]{:S(2)}) collective-permute-start(f32[200,128]{1,0:T(8,128)S(1)} %concatenate.3.refs_2_), channel_id=1, source_target_pairs={{0,1},{1,0},{2,3},{3,2},{4,5},{5,4},{6,7},{7,6},{8,9},{9,8},{10,11... | collective-permute-start | bytes 307208 | tf_op jit(solution)/shard_map/ppermute | solution.py:596
  7.2 0.0 collective-permute-start.1
  7.8 0.0 copy-start
  7.8 1.2 %copy-done = bf16[2240,256]{1,0:T(8,128)(2,1)S(1)} copy-done((bf16[2240,256]{1,0:T(8,128)(2,1)S(1)}, bf16[2240,256]{1,0:T(8,128)(2,1)}, u32[]{:S(2)}) %copy-start) | copy-done | bytes 1146904
  9.1 0.1 shard_map.46.refs_1_.step_ref
  9.2 2.9 %collective-permute-done.refs_3_ = f32[200,128]{1,0:T(8,128)S(1)} collective-permute-done((f32[200,128]{1,0:T(8,128)S(1)}, f32[200,128]{1,0:T(8,128)S(1)}, u32[]{:S(2)}, u32[]{:S(2)}) %collective-permute-start) | collective-permute-done | bytes 102432 | tf_op jit(solution)/shard_map/ppermute | solution.py:596
  12.1 1.5 %shard_map.47 = (f32[192,128]{1,0:T(8,128)S(1)}, f32[192,128]{1,0:T(8,128)S(1)}) custom-call(bf16[2240,256]{1,0:T(8,128)(2,1)S(1)} %copy-done, f32[8,128]{1,0:T(8,128)S(1)} %shard_map.46.refs_1_.step_ref, f32[200,128]{1,0:T(8,128)S(1)} %concatenate.3.refs_2_, f32[200,128]{1,0:T(8,128)S(1)} %collective-permute-done.refs_3_), custom_call_target="tpu_custom_call" | custom-call | flops 786432000 | bytes 1048576 | tf_op jit(solution)/shard_map/pallas_call | solution.py:561
  13.6 0.0 collective-permute-done.2.refs_5_
  13.6 0.4 %collective-permute-done.1.refs_4_ = f32[200,128]{1,0:T(8,128)S(1)} collective-permute-done((f32[200,128]{1,0:T(8,128)S(1)}, f32[200,128]{1,0:T(8,128)S(1)}, u32[]{:S(2)}, u32[]{:S(2)}) %collective-permute-start.1) | collective-permute-done | bytes 102432 | tf_op jit(solution)/shard_map/ppermute | solution.py:596
  14.0 1.5 %shard_map.48 = (f32[4,192,128]{2,1,0:T(8,128)S(1)}, f32[4,8,128]{2,1,0:T(8,128)S(1)}, f32[4,192,128]{2,1,0:T(8,128)S(1)}, f32[4,3,8,128]{3,2,1,0:T(8,128)S(1)}, f32[4,3,8,128]{3,2,1,0:T(8,128)S(1)}) custom-call(bf16[2240,256]{1,0:T(8,128)(2,1)S(1)} %copy-done, f32[8,128]{1,0:T(8,128)S(1)} %shard_map.46.refs_1_.step_ref, f32[200,128]{1,0:T(8,128)S(1)} %concatenate.3.refs_2_, ...), custom_call_target="tpu_custom_call" | custom-call | flops 1572864000 | bytes 1048576 | tf_op jit(solution)/shard_map/pallas_call | solution.py:561
  15.6 1.3 %collective-permute-start.3 = (f32[4,3,8,128]{3,2,1,0:T(8,128)S(1)}, f32[4,3,8,128]{3,2,1,0:T(8,128)S(1)}, u32[]{:S(2)}, u32[]{:S(2)}) collective-permute-start(f32[4,3,8,128]{3,2,1,0:T(8,128)S(1)} %get-tuple-element.34.refs_4_), channel_id=1, source_target_pairs={{0,28},{4,8},{8,4},{12,16},{16,12},{20,24},{24,20},{28,0},{1,29},{... | collective-permute-start | bytes 147464 | tf_op jit(solution)/shard_map/ppermute | solution.py:576
  16.9 0.4 collective-permute-start.4
  17.2 0.4 %shard_map.49 = (f32[6,2,144,128]{3,2,1,0:T(8,128)S(1)}, f32[144,128]{1,0:T(8,128)S(1)}) custom-call(bf16[2240,256]{1,0:T(8,128)(2,1)S(1)} %copy-done, f32[8,128]{1,0:T(8,128)S(1)} %shard_map.46.refs_1_.step_ref, f32[4,192,128]{2,1,0:T(8,128)S(1)} %get-tuple-element.32.field_ref.refs_2_, f32[4,192,128]{2,1,0:T(8,128)S(1)} %get-tuple-element.36.partial_ref), custom_call_target="tpu_custom_call" | custom-call | flops 393216000 | bytes 1048576 | tf_op jit(solution)/shard_map/pallas_call | solution.py:561
  17.7 2.8 %collective-permute-done.3.refs_6_ = f32[4,3,8,128]{3,2,1,0:T(8,128)S(1)} collective-permute-done((f32[4,3,8,128]{3,2,1,0:T(8,128)S(1)}, f32[4,3,8,128]{3,2,1,0:T(8,128)S(1)}, u32[]{:S(2)}, u32[]{:S(2)}) %collective-permute-start.3) | collective-permute-done | bytes 49184 | tf_op jit(solution)/shard_map/ppermute | solution.py:576
  20.5 0.0 collective-permute-done.4.refs_7_
  20.5 1.7 %shard_map.50 = (f32[2,3,8,128]{3,2,1,0:T(8,128)S(1)}, f32[6,192,128]{2,1,0:T(8,128)S(1)}, f32[4,3,8,128]{3,2,1,0:T(8,128)S(1)}, f32[4,3,8,128]{3,2,1,0:T(8,128)S(1)}) custom-call(bf16[2240,256]{1,0:T(8,128)(2,1)S(1)} %copy-done, f32[8,128]{1,0:T(8,128)S(1)} %shard_map.46.refs_1_.step_ref, f32[4,192,128]{2,1,0:T(8,128)S(1)} %get-tuple-element.32.field_ref.refs_2_, ...), custom_call_target="tpu_custom_call" | custom-call | flops 1572864000 | bytes 1048576 | tf_op jit(solution)/shard_map/pallas_call | solution.py:561
  22.2 1.1 %collective-permute-start.5 = (f32[4,3,8,128]{3,2,1,0:T(8,128)S(1)}, f32[4,3,8,128]{3,2,1,0:T(8,128)S(1)}, u32[]{:S(2)}, u32[]{:S(2)}) collective-permute-start(f32[4,3,8,128]{3,2,1,0:T(8,128)S(1)} %get-tuple-element.38.refs_4_), channel_id=1, source_target_pairs={{0,28},{4,8},{8,4},{12,16},{16,12},{20,24},{24,20},{28,0},{1,29},{... | collective-permute-start | bytes 147464 | tf_op jit(solution)/shard_map/ppermute | solution.py:576
  23.3 0.0 collective-permute-start.6
  23.3 0.8 %shard_map.51 = (f32[6,2,144,128]{3,2,1,0:T(8,128)S(1)}, f32[144,128]{1,0:T(8,128)S(1)}) custom-call(bf16[2240,256]{1,0:T(8,128)(2,1)S(1)} %copy-done, f32[8,128]{1,0:T(8,128)S(1)} %shard_map.46.refs_1_.step_ref, f32[4,192,128]{2,1,0:T(8,128)S(1)} %get-tuple-element.32.field_ref.refs_2_, f32[4,8,128]{2,1,0:T(8,128)S(1)} %get-tuple-element.33.refs_3_.heights_ref, ...), custom_call_target="tpu_custom_call" | custom-call | flops 786432000 | bytes 1048576 | tf_op jit(solution)/shard_map/pallas_call | solution.py:561
  24.1 2.6 %collective-permute-done.5.refs_6_ = f32[4,3,8,128]{3,2,1,0:T(8,128)S(1)} collective-permute-done((f32[4,3,8,128]{3,2,1,0:T(8,128)S(1)}, f32[4,3,8,128]{3,2,1,0:T(8,128)S(1)}, u32[]{:S(2)}, u32[]{:S(2)}) %collective-permute-start.5) | collective-permute-done | bytes 49184 | tf_op jit(solution)/shard_map/ppermute | solution.py:576
  26.7 0.0 collective-permute-done.6.refs_7_
  26.7 1.7 %shard_map.52 = (f32[2,3,8,128]{3,2,1,0:T(8,128)S(1)}, f32[6,192,128]{2,1,0:T(8,128)S(1)}, f32[4,3,8,128]{3,2,1,0:T(8,128)S(1)}, f32[4,3,8,128]{3,2,1,0:T(8,128)S(1)}) custom-call(bf16[2240,256]{1,0:T(8,128)(2,1)S(1)} %copy-done, f32[8,128]{1,0:T(8,128)S(1)} %shard_map.46.refs_1_.step_ref, f32[4,192,128]{2,1,0:T(8,128)S(1)} %get-tuple-element.32.field_ref.refs_2_, ...), custom_call_target="tpu_custom_call" | custom-call | flops 1572864000 | bytes 1048576 | tf_op jit(solution)/shard_map/pallas_call | solution.py:561
  28.4 1.1 %collective-permute-start.7 = (f32[4,3,8,128]{3,2,1,0:T(8,128)S(1)}, f32[4,3,8,128]{3,2,1,0:T(8,128)S(1)}, u32[]{:S(2)}, u32[]{:S(2)}) collective-permute-start(f32[4,3,8,128]{3,2,1,0:T(8,128)S(1)} %get-tuple-element.44.refs_4_), channel_id=1, source_target_pairs={{0,28},{4,8},{8,4},{12,16},{16,12},{20,24},{24,20},{28,0},{1,29},{... | collective-permute-start | bytes 147464 | tf_op jit(solution)/shard_map/ppermute | solution.py:576
  29.5 0.0 collective-permute-start.8
  29.5 0.8 %shard_map.53 = (f32[5,2,144,128]{3,2,1,0:T(8,128)S(1)}, f32[144,128]{1,0:T(8,128)S(1)}) custom-call(bf16[2240,256]{1,0:T(8,128)(2,1)S(1)} %copy-done, f32[8,128]{1,0:T(8,128)S(1)} %shard_map.46.refs_1_.step_ref, f32[4,192,128]{2,1,0:T(8,128)S(1)} %get-tuple-element.32.field_ref.refs_2_, f32[4,8,128]{2,1,0:T(8,128)S(1)} %get-tuple-element.33.refs_3_.heights_ref, ...), custom_call_target="tpu_custom_call" | custom-call | flops 589824000 | bytes 1048576 | tf_op jit(solution)/shard_map/pallas_call | solution.py:561
  30.3 2.6 %collective-permute-done.7.refs_6_ = f32[4,3,8,128]{3,2,1,0:T(8,128)S(1)} collective-permute-done((f32[4,3,8,128]{3,2,1,0:T(8,128)S(1)}, f32[4,3,8,128]{3,2,1,0:T(8,128)S(1)}, u32[]{:S(2)}, u32[]{:S(2)}) %collective-permute-start.7) | collective-permute-done | bytes 49184 | tf_op jit(solution)/shard_map/ppermute | solution.py:576
  32.9 0.0 collective-permute-done.8.refs_7_
  32.9 1.6 %shard_map.54 = (f32[2,3,8,128]{3,2,1,0:T(8,128)S(1)}, f32[5,192,128]{2,1,0:T(8,128)S(1)}, f32[3,8,128]{2,1,0:T(8,128)S(1)}, f32[3,8,128]{2,1,0:T(8,128)S(1)}) custom-call(bf16[2240,256]{1,0:T(8,128)(2,1)S(1)} %copy-done, f32[8,128]{1,0:T(8,128)S(1)} %shard_map.46.refs_1_.step_ref, f32[4,192,128]{2,1,0:T(8,128)S(1)} %get-tuple-element.32.field_ref.refs_2_, ...), custom_call_target="tpu_custom_call" | custom-call | flops 1179648000 | bytes 1048576 | tf_op jit(solution)/shard_map/pallas_call | solution.py:561
  34.5 1.1 %collective-permute-start.9 = (f32[3,8,128]{2,1,0:T(8,128)S(1)}, f32[3,8,128]{2,1,0:T(8,128)S(1)}, u32[]{:S(2)}, u32[]{:S(2)}) collective-permute-start(f32[3,8,128]{2,1,0:T(8,128)S(1)} %get-tuple-element.50.own_cross_ref), channel_id=1, source_target_pairs={{0,28},{4,8},{8,4},{12,16},{16,12},{20,24},{24,20},{28,0},{1,29},{... | collective-permute-start | bytes 36872 | tf_op jit(solution)/shard_map/ppermute | solution.py:576
  35.6 0.0 collective-permute-start.10
  35.6 0.4 shard_map.55.inner_ref
  36.0 2.7 %collective-permute-done.9.cross_ref = f32[3,8,128]{2,1,0:T(8,128)S(1)} collective-permute-done((f32[3,8,128]{2,1,0:T(8,128)S(1)}, f32[3,8,128]{2,1,0:T(8,128)S(1)}, u32[]{:S(2)}, u32[]{:S(2)}) %collective-permute-start.9) | collective-permute-done | bytes 12320 | tf_op jit(solution)/shard_map/ppermute | solution.py:576
  38.6 0.0 collective-permute-done.10.core_ref
  38.6 0.7 %shard_map.56 = f32[192,128]{1,0:T(8,128)} custom-call(f32[3,8,128]{2,1,0:T(8,128)S(1)} %get-tuple-element.50.own_cross_ref, f32[3,8,128]{2,1,0:T(8,128)S(1)} %get-tuple-element.51.own_core_ref, f32[3,8,128]{2,1,0:T(8,128)S(1)} %collective-permute-done.9.cross_ref, f32[3,8,128]{2,1,0:T(8,128)S(1)} %collective-permute-done.10.core_ref, ...), custom_call_target="tpu_custom_call" | custom-call | bytes 1048576 | tf_op jit(solution)/shard_map/pallas_call | solution.py:561
Async XLA Ops:
  1.6 10.5 %collective-permute-start = (f32[200,128]{1,0:T(8,128)S(1)}, f32[200,128]{1,0:T(8,128)S(1)}, u32[]{:S(2)}, u32[]{:S(2)}) collective-permute-start(f32[200,128]{1,0:T(8,128)S(1)} %concatenate.3.refs_2_), channel_id=1, source_target_pairs={{0,2},{1,3},{2,0},{3,1},{4,6},{5,7},{6,4},{7,5},{8,10},{9,11},{10,... | collective-permute-start | bytes 307208 | tf_op jit(solution)/shard_map/ppermute | solution.py:596
  5.6 8.0 %collective-permute-start.2 = (f32[200,128]{1,0:T(8,128)S(1)}, f32[200,128]{1,0:T(8,128)S(1)}, u32[]{:S(2)}, u32[]{:S(2)}) collective-permute-start(f32[200,128]{1,0:T(8,128)S(1)} %concatenate.3.refs_2_), channel_id=1, source_target_pairs={{0,1},{1,0},{2,3},{3,2},{4,5},{5,4},{6,7},{7,6},{8,9},{9,8},{10,11... | collective-permute-start | bytes 307208 | tf_op jit(solution)/shard_map/ppermute | solution.py:596
  7.2 6.9 %collective-permute-start.1 = (f32[200,128]{1,0:T(8,128)S(1)}, f32[200,128]{1,0:T(8,128)S(1)}, u32[]{:S(2)}, u32[]{:S(2)}) collective-permute-start(f32[200,128]{1,0:T(8,128)S(1)} %concatenate.3.refs_2_), channel_id=1, source_target_pairs={{0,3},{1,2},{2,1},{3,0},{4,7},{5,6},{6,5},{7,4},{8,11},{9,10},{10,... | collective-permute-start | bytes 307208 | tf_op jit(solution)/shard_map/ppermute | solution.py:596
  7.8 1.3 %copy-start = (bf16[2240,256]{1,0:T(8,128)(2,1)S(1)}, bf16[2240,256]{1,0:T(8,128)(2,1)}, u32[]{:S(2)}) copy-start(bf16[2240,256]{1,0:T(8,128)(2,1)} %constant.2.clone.mats.refs_0_) | copy-start | bytes 3440644
  15.6 4.9 %collective-permute-start.3 = (f32[4,3,8,128]{3,2,1,0:T(8,128)S(1)}, f32[4,3,8,128]{3,2,1,0:T(8,128)S(1)}, u32[]{:S(2)}, u32[]{:S(2)}) collective-permute-start(f32[4,3,8,128]{3,2,1,0:T(8,128)S(1)} %get-tuple-element.34.refs_4_), channel_id=1, source_target_pairs={{0,28},{4,8},{8,4},{12,16},{16,12},{20,24},{24,20},{28,0},{1,29},{... | collective-permute-start | bytes 147464 | tf_op jit(solution)/shard_map/ppermute | solution.py:576
  16.9 3.6 %collective-permute-start.4 = (f32[4,3,8,128]{3,2,1,0:T(8,128)S(1)}, f32[4,3,8,128]{3,2,1,0:T(8,128)S(1)}, u32[]{:S(2)}, u32[]{:S(2)}) collective-permute-start(f32[4,3,8,128]{3,2,1,0:T(8,128)S(1)} %get-tuple-element.35.refs_5_), channel_id=1, source_target_pairs={{0,4},{4,0},{8,12},{12,8},{16,20},{20,16},{24,28},{28,24},{1,5},{5... | collective-permute-start | bytes 147464 | tf_op jit(solution)/shard_map/ppermute | solution.py:576
  22.2 4.5 %collective-permute-start.5 = (f32[4,3,8,128]{3,2,1,0:T(8,128)S(1)}, f32[4,3,8,128]{3,2,1,0:T(8,128)S(1)}, u32[]{:S(2)}, u32[]{:S(2)}) collective-permute-start(f32[4,3,8,128]{3,2,1,0:T(8,128)S(1)} %get-tuple-element.38.refs_4_), channel_id=1, source_target_pairs={{0,28},{4,8},{8,4},{12,16},{16,12},{20,24},{24,20},{28,0},{1,29},{... | collective-permute-start | bytes 147464 | tf_op jit(solution)/shard_map/ppermute | solution.py:576
  23.3 3.4 %collective-permute-start.6 = (f32[4,3,8,128]{3,2,1,0:T(8,128)S(1)}, f32[4,3,8,128]{3,2,1,0:T(8,128)S(1)}, u32[]{:S(2)}, u32[]{:S(2)}) collective-permute-start(f32[4,3,8,128]{3,2,1,0:T(8,128)S(1)} %get-tuple-element.39.refs_5_), channel_id=1, source_target_pairs={{0,4},{4,0},{8,12},{12,8},{16,20},{20,16},{24,28},{28,24},{1,5},{5... | collective-permute-start | bytes 147464 | tf_op jit(solution)/shard_map/ppermute | solution.py:576
  28.4 4.5 %collective-permute-start.7 = (f32[4,3,8,128]{3,2,1,0:T(8,128)S(1)}, f32[4,3,8,128]{3,2,1,0:T(8,128)S(1)}, u32[]{:S(2)}, u32[]{:S(2)}) collective-permute-start(f32[4,3,8,128]{3,2,1,0:T(8,128)S(1)} %get-tuple-element.44.refs_4_), channel_id=1, source_target_pairs={{0,28},{4,8},{8,4},{12,16},{16,12},{20,24},{24,20},{28,0},{1,29},{... | collective-permute-start | bytes 147464 | tf_op jit(solution)/shard_map/ppermute | solution.py:576
  29.5 3.4 %collective-permute-start.8 = (f32[4,3,8,128]{3,2,1,0:T(8,128)S(1)}, f32[4,3,8,128]{3,2,1,0:T(8,128)S(1)}, u32[]{:S(2)}, u32[]{:S(2)}) collective-permute-start(f32[4,3,8,128]{3,2,1,0:T(8,128)S(1)} %get-tuple-element.45.refs_5_), channel_id=1, source_target_pairs={{0,4},{4,0},{8,12},{12,8},{16,20},{20,16},{24,28},{28,24},{1,5},{5... | collective-permute-start | bytes 147464 | tf_op jit(solution)/shard_map/ppermute | solution.py:576
  34.5 4.1 %collective-permute-start.9 = (f32[3,8,128]{2,1,0:T(8,128)S(1)}, f32[3,8,128]{2,1,0:T(8,128)S(1)}, u32[]{:S(2)}, u32[]{:S(2)}) collective-permute-start(f32[3,8,128]{2,1,0:T(8,128)S(1)} %get-tuple-element.50.own_cross_ref), channel_id=1, source_target_pairs={{0,28},{4,8},{8,4},{12,16},{16,12},{20,24},{24,20},{28,0},{1,29},{... | collective-permute-start | bytes 36872 | tf_op jit(solution)/shard_map/ppermute | solution.py:576
  35.6 3.0 %collective-permute-start.10 = (f32[3,8,128]{2,1,0:T(8,128)S(1)}, f32[3,8,128]{2,1,0:T(8,128)S(1)}, u32[]{:S(2)}, u32[]{:S(2)}) collective-permute-start(f32[3,8,128]{2,1,0:T(8,128)S(1)} %get-tuple-element.51.own_core_ref), channel_id=1, source_target_pairs={{0,4},{4,0},{8,12},{12,8},{16,20},{20,16},{24,28},{28,24},{1,5},{5... | collective-permute-start | bytes 36872 | tf_op jit(solution)/shard_map/ppermute | solution.py:576

commit v5 on v4

--- a/solution.py
+++ b/solution.py
@@ -590,7 +590,7 @@
     own_field = velocity.reshape(ROWS, SPAN)
     packed = jnp.concatenate([own_field, jnp.broadcast_to(heights[:, None], (8, SPAN))], axis=0)
     if layers in (1, 2, 4):
-        groups = {1: [[0]], 2: [[0], [1]], 4: [[0, 2], [3, 1]]}[layers]
+        groups = {1: [[0]], 2: [[0], [1]], 4: [[0, 1, 2], [3]]}[layers]
         slots = {0: packed}
         for j in range(layers - 1, 0, -1):
             slots[j] = lax.ppermute(packed, "vert", [(i, i ^ j) for i in range(layers)])

time: 39.5 us -> 39 us (0.987)
  waiting for transfers between devices: 14.1 us -> 13.6 us
  transfers between devices with their start and end apart: 11 -> 11, of which waited for: 6 -> 6; matrix products, arithmetic and copies ran while one was open for 0% -> 0% of each run, Pallas kernels for 10% -> 11%
where the time goes in v5:
time: 39 us; the launch traced here: 38.8 us
  waiting for transfers between devices  13.6 us (35%)
  Pallas kernels  10.9 us (28%)
  starting transfers between devices  10.8 us (28%)
  local copies, waits for them, and re-layouts  2.16 us (6%)
  between operations  1.38 us (4%)
    pallas_call x11, Pallas kernels, call(): pl.pallas_call(kernel, out_shape=shapes[0] if one else shapes, in_specs=[...  10.9 us
    ppermute x4, waiting for transfers between devices, swap_stream(): lax.ppermute(cross, 'horiz', crosses)  10.5 us
    ppermute x3, starting transfers between devices, on_device(): slots[j] = lax.ppermute(packed, 'vert', [(i, i ^ j) for i in range(layers)])  5.62 us
    ppermute x4, starting transfers between devices, swap_stream(): lax.ppermute(cross, 'horiz', crosses)  4.7 us
    ppermute x3, waiting for transfers between devices, on_device(): slots[j] = lax.ppermute(packed, 'vert', [(i, i ^ j) for i in range(layers)])  3.15 us
    unnamed x2, local copies, waits for them, and re-layouts  1.25 us
    concatenate x1, local copies, waits for them, and re-layouts, on_device(): jnp.concatenate([own_field, jnp.broadcast_to(heights[:, None], (8, SPAN))...  0.9 us
  transfers between devices with their start and end apart: 11, of which 6 were waited for; matrix products, arithmetic and copies ran while one was open for 0% of the time, Pallas kernels for 11%

profile of v5, /device:TPU:0, one launch (start us, length us, event | category | flops | bytes accessed | tf_op | source)
XLA Modules:
  0.0 38.8 jit_solution(3183869921957237103)
XLA Ops:
  0.7 0.9 %concatenate.3.refs_2_ = f32[200,128]{1,0:T(8,128)S(1)} pad(f32[192,128]{1,0:T(8,128)} %bitcast.6, f32[]{:T(128)} %bitcast.4), padding=0_8x0_0 | pad | bytes 200708 | tf_op jit(solution)/shard_map/concatenate | solution.py:591
  1.6 4.0 %collective-permute-start.1 = (f32[200,128]{1,0:T(8,128)S(1)}, f32[200,128]{1,0:T(8,128)S(1)}, u32[]{:S(2)}, u32[]{:S(2)}) collective-permute-start(f32[200,128]{1,0:T(8,128)S(1)} %concatenate.3.refs_2_), channel_id=1, source_target_pairs={{0,2},{1,3},{2,0},{3,1},{4,6},{5,7},{6,4},{7,5},{8,10},{9,11},{10,... | collective-permute-start | bytes 307208 | tf_op jit(solution)/shard_map/ppermute | solution.py:596
  5.6 1.6 %collective-permute-start = (f32[200,128]{1,0:T(8,128)S(1)}, f32[200,128]{1,0:T(8,128)S(1)}, u32[]{:S(2)}, u32[]{:S(2)}) collective-permute-start(f32[200,128]{1,0:T(8,128)S(1)} %concatenate.3.refs_2_), channel_id=1, source_target_pairs={{0,1},{1,0},{2,3},{3,2},{4,5},{5,4},{6,7},{7,6},{8,9},{9,8},{10,11... | collective-permute-start | bytes 307208 | tf_op jit(solution)/shard_map/ppermute | solution.py:596
  7.2 0.0 collective-permute-start.2
  7.8 0.0 copy-start
  7.8 1.2 %copy-done = bf16[2240,256]{1,0:T(8,128)(2,1)S(1)} copy-done((bf16[2240,256]{1,0:T(8,128)(2,1)S(1)}, bf16[2240,256]{1,0:T(8,128)(2,1)}, u32[]{:S(2)}) %copy-start) | copy-done | bytes 1146904
  9.1 0.1 shard_map.46.refs_1_.step_ref
  9.2 2.9 %collective-permute-done.1.refs_4_ = f32[200,128]{1,0:T(8,128)S(1)} collective-permute-done((f32[200,128]{1,0:T(8,128)S(1)}, f32[200,128]{1,0:T(8,128)S(1)}, u32[]{:S(2)}, u32[]{:S(2)}) %collective-permute-start.1) | collective-permute-done | bytes 102432 | tf_op jit(solution)/shard_map/ppermute | solution.py:596
  12.1 0.0 collective-permute-done.refs_3_
  12.1 1.7 %shard_map.47 = (f32[192,128]{1,0:T(8,128)S(1)}, f32[192,128]{1,0:T(8,128)S(1)}, f32[192,128]{1,0:T(8,128)S(1)}) custom-call(bf16[2240,256]{1,0:T(8,128)(2,1)S(1)} %copy-done, f32[8,128]{1,0:T(8,128)S(1)} %shard_map.46.refs_1_.step_ref, f32[200,128]{1,0:T(8,128)S(1)} %concatenate.3.refs_2_, f32[200,128]{1,0:T(8,128)S(1)} %collective-permute-done.refs_3_, ...), custom_call_target="tpu_custom_call" | custom-call | flops 1179648000 | bytes 1048576 | tf_op jit(solution)/shard_map/pallas_call | solution.py:561
  13.8 0.2 collective-permute-done.2.refs_5_
  14.0 1.0 %shard_map.48 = (f32[4,192,128]{2,1,0:T(8,128)S(1)}, f32[4,8,128]{2,1,0:T(8,128)S(1)}, f32[4,192,128]{2,1,0:T(8,128)S(1)}, f32[4,3,8,128]{3,2,1,0:T(8,128)S(1)}, f32[4,3,8,128]{3,2,1,0:T(8,128)S(1)}) custom-call(bf16[2240,256]{1,0:T(8,128)(2,1)S(1)} %copy-done, f32[8,128]{1,0:T(8,128)S(1)} %shard_map.46.refs_1_.step_ref, f32[200,128]{1,0:T(8,128)S(1)} %concatenate.3.refs_2_, ...), custom_call_target="tpu_custom_call" | custom-call | flops 1572864000 | bytes 1048576 | tf_op jit(solution)/shard_map/pallas_call | solution.py:561
  15.1 1.3 %collective-permute-start.3 = (f32[4,3,8,128]{3,2,1,0:T(8,128)S(1)}, f32[4,3,8,128]{3,2,1,0:T(8,128)S(1)}, u32[]{:S(2)}, u32[]{:S(2)}) collective-permute-start(f32[4,3,8,128]{3,2,1,0:T(8,128)S(1)} %get-tuple-element.36.refs_4_), channel_id=1, source_target_pairs={{0,28},{4,8},{8,4},{12,16},{16,12},{20,24},{24,20},{28,0},{1,29},{... | collective-permute-start | bytes 147464 | tf_op jit(solution)/shard_map/ppermute | solution.py:576
  16.4 0.4 %collective-permute-start.4 = (f32[4,3,8,128]{3,2,1,0:T(8,128)S(1)}, f32[4,3,8,128]{3,2,1,0:T(8,128)S(1)}, u32[]{:S(2)}, u32[]{:S(2)}) collective-permute-start(f32[4,3,8,128]{3,2,1,0:T(8,128)S(1)} %get-tuple-element.37.refs_5_), channel_id=1, source_target_pairs={{0,4},{4,0},{8,12},{12,8},{16,20},{20,16},{24,28},{28,24},{1,5},{5... | collective-permute-start | bytes 147464 | tf_op jit(solution)/shard_map/ppermute | solution.py:576
  16.8 0.4 %shard_map.49 = (f32[6,2,144,128]{3,2,1,0:T(8,128)S(1)}, f32[144,128]{1,0:T(8,128)S(1)}) custom-call(bf16[2240,256]{1,0:T(8,128)(2,1)S(1)} %copy-done, f32[8,128]{1,0:T(8,128)S(1)} %shard_map.46.refs_1_.step_ref, f32[4,192,128]{2,1,0:T(8,128)S(1)} %get-tuple-element.34.field_ref.refs_2_, f32[4,192,128]{2,1,0:T(8,128)S(1)} %get-tuple-element.38.partial_ref), custom_call_target="tpu_custom_call" | custom-call | flops 393216000 | bytes 1048576 | tf_op jit(solution)/shard_map/pallas_call | solution.py:561
  17.2 2.7 %collective-permute-done.3.refs_6_ = f32[4,3,8,128]{3,2,1,0:T(8,128)S(1)} collective-permute-done((f32[4,3,8,128]{3,2,1,0:T(8,128)S(1)}, f32[4,3,8,128]{3,2,1,0:T(8,128)S(1)}, u32[]{:S(2)}, u32[]{:S(2)}) %collective-permute-start.3) | collective-permute-done | bytes 49184 | tf_op jit(solution)/shard_map/ppermute | solution.py:576
  19.9 0.0 collective-permute-done.4.refs_7_
  19.9 1.7 %shard_map.50 = (f32[2,3,8,128]{3,2,1,0:T(8,128)S(1)}, f32[6,192,128]{2,1,0:T(8,128)S(1)}, f32[4,3,8,128]{3,2,1,0:T(8,128)S(1)}, f32[4,3,8,128]{3,2,1,0:T(8,128)S(1)}) custom-call(bf16[2240,256]{1,0:T(8,128)(2,1)S(1)} %copy-done, f32[8,128]{1,0:T(8,128)S(1)} %shard_map.46.refs_1_.step_ref, f32[4,192,128]{2,1,0:T(8,128)S(1)} %get-tuple-element.34.field_ref.refs_2_, ...), custom_call_target="tpu_custom_call" | custom-call | flops 1572864000 | bytes 1048576 | tf_op jit(solution)/shard_map/pallas_call | solution.py:561
  21.7 1.2 %collective-permute-start.5 = (f32[4,3,8,128]{3,2,1,0:T(8,128)S(1)}, f32[4,3,8,128]{3,2,1,0:T(8,128)S(1)}, u32[]{:S(2)}, u32[]{:S(2)}) collective-permute-start(f32[4,3,8,128]{3,2,1,0:T(8,128)S(1)} %get-tuple-element.40.refs_4_), channel_id=1, source_target_pairs={{0,28},{4,8},{8,4},{12,16},{16,12},{20,24},{24,20},{28,0},{1,29},{... | collective-permute-start | bytes 147464 | tf_op jit(solution)/shard_map/ppermute | solution.py:576
  22.9 0.0 collective-permute-start.6
  22.9 0.8 %shard_map.51 = (f32[6,2,144,128]{3,2,1,0:T(8,128)S(1)}, f32[144,128]{1,0:T(8,128)S(1)}) custom-call(bf16[2240,256]{1,0:T(8,128)(2,1)S(1)} %copy-done, f32[8,128]{1,0:T(8,128)S(1)} %shard_map.46.refs_1_.step_ref, f32[4,192,128]{2,1,0:T(8,128)S(1)} %get-tuple-element.34.field_ref.refs_2_, f32[4,8,128]{2,1,0:T(8,128)S(1)} %get-tuple-element.35.refs_3_.heights_ref, ...), custom_call_target="tpu_custom_call" | custom-call | flops 786432000 | bytes 1048576 | tf_op jit(solution)/shard_map/pallas_call | solution.py:561
  23.7 2.6 %collective-permute-done.5.refs_6_ = f32[4,3,8,128]{3,2,1,0:T(8,128)S(1)} collective-permute-done((f32[4,3,8,128]{3,2,1,0:T(8,128)S(1)}, f32[4,3,8,128]{3,2,1,0:T(8,128)S(1)}, u32[]{:S(2)}, u32[]{:S(2)}) %collective-permute-start.5) | collective-permute-done | bytes 49184 | tf_op jit(solution)/shard_map/ppermute | solution.py:576
  26.2 0.0 collective-permute-done.6.refs_7_
  26.2 1.7 %shard_map.52 = (f32[2,3,8,128]{3,2,1,0:T(8,128)S(1)}, f32[6,192,128]{2,1,0:T(8,128)S(1)}, f32[4,3,8,128]{3,2,1,0:T(8,128)S(1)}, f32[4,3,8,128]{3,2,1,0:T(8,128)S(1)}) custom-call(bf16[2240,256]{1,0:T(8,128)(2,1)S(1)} %copy-done, f32[8,128]{1,0:T(8,128)S(1)} %shard_map.46.refs_1_.step_ref, f32[4,192,128]{2,1,0:T(8,128)S(1)} %get-tuple-element.34.field_ref.refs_2_, ...), custom_call_target="tpu_custom_call" | custom-call | flops 1572864000 | bytes 1048576 | tf_op jit(solution)/shard_map/pallas_call | solution.py:561
  28.0 1.1 %collective-permute-start.7 = (f32[4,3,8,128]{3,2,1,0:T(8,128)S(1)}, f32[4,3,8,128]{3,2,1,0:T(8,128)S(1)}, u32[]{:S(2)}, u32[]{:S(2)}) collective-permute-start(f32[4,3,8,128]{3,2,1,0:T(8,128)S(1)} %get-tuple-element.46.refs_4_), channel_id=1, source_target_pairs={{0,28},{4,8},{8,4},{12,16},{16,12},{20,24},{24,20},{28,0},{1,29},{... | collective-permute-start | bytes 147464 | tf_op jit(solution)/shard_map/ppermute | solution.py:576
  29.1 0.0 collective-permute-start.8
  29.1 0.8 %shard_map.53 = (f32[5,2,144,128]{3,2,1,0:T(8,128)S(1)}, f32[144,128]{1,0:T(8,128)S(1)}) custom-call(bf16[2240,256]{1,0:T(8,128)(2,1)S(1)} %copy-done, f32[8,128]{1,0:T(8,128)S(1)} %shard_map.46.refs_1_.step_ref, f32[4,192,128]{2,1,0:T(8,128)S(1)} %get-tuple-element.34.field_ref.refs_2_, f32[4,8,128]{2,1,0:T(8,128)S(1)} %get-tuple-element.35.refs_3_.heights_ref, ...), custom_call_target="tpu_custom_call" | custom-call | flops 589824000 | bytes 1048576 | tf_op jit(solution)/shard_map/pallas_call | solution.py:561
  29.9 2.6 %collective-permute-done.7.refs_6_ = f32[4,3,8,128]{3,2,1,0:T(8,128)S(1)} collective-permute-done((f32[4,3,8,128]{3,2,1,0:T(8,128)S(1)}, f32[4,3,8,128]{3,2,1,0:T(8,128)S(1)}, u32[]{:S(2)}, u32[]{:S(2)}) %collective-permute-start.7) | collective-permute-done | bytes 49184 | tf_op jit(solution)/shard_map/ppermute | solution.py:576
  32.4 0.0 collective-permute-done.8.refs_7_
  32.5 1.6 %shard_map.54 = (f32[2,3,8,128]{3,2,1,0:T(8,128)S(1)}, f32[5,192,128]{2,1,0:T(8,128)S(1)}, f32[3,8,128]{2,1,0:T(8,128)S(1)}, f32[3,8,128]{2,1,0:T(8,128)S(1)}) custom-call(bf16[2240,256]{1,0:T(8,128)(2,1)S(1)} %copy-done, f32[8,128]{1,0:T(8,128)S(1)} %shard_map.46.refs_1_.step_ref, f32[4,192,128]{2,1,0:T(8,128)S(1)} %get-tuple-element.34.field_ref.refs_2_, ...), custom_call_target="tpu_custom_call" | custom-call | flops 1179648000 | bytes 1048576 | tf_op jit(solution)/shard_map/pallas_call | solution.py:561
  34.1 1.1 %collective-permute-start.9 = (f32[3,8,128]{2,1,0:T(8,128)S(1)}, f32[3,8,128]{2,1,0:T(8,128)S(1)}, u32[]{:S(2)}, u32[]{:S(2)}) collective-permute-start(f32[3,8,128]{2,1,0:T(8,128)S(1)} %get-tuple-element.52.own_cross_ref), channel_id=1, source_target_pairs={{0,28},{4,8},{8,4},{12,16},{16,12},{20,24},{24,20},{28,0},{1,29},{... | collective-permute-start | bytes 36872 | tf_op jit(solution)/shard_map/ppermute | solution.py:576
  35.2 0.0 collective-permute-start.10
  35.2 0.4 shard_map.55.inner_ref
  35.5 2.6 %collective-permute-done.9.cross_ref = f32[3,8,128]{2,1,0:T(8,128)S(1)} collective-permute-done((f32[3,8,128]{2,1,0:T(8,128)S(1)}, f32[3,8,128]{2,1,0:T(8,128)S(1)}, u32[]{:S(2)}, u32[]{:S(2)}) %collective-permute-start.9) | collective-permute-done | bytes 12320 | tf_op jit(solution)/shard_map/ppermute | solution.py:576
  38.1 0.0 collective-permute-done.10.core_ref
  38.2 0.7 %shard_map.56 = f32[192,128]{1,0:T(8,128)} custom-call(f32[3,8,128]{2,1,0:T(8,128)S(1)} %get-tuple-element.52.own_cross_ref, f32[3,8,128]{2,1,0:T(8,128)S(1)} %get-tuple-element.53.own_core_ref, f32[3,8,128]{2,1,0:T(8,128)S(1)} %collective-permute-done.9.cross_ref, f32[3,8,128]{2,1,0:T(8,128)S(1)} %collective-permute-done.10.core_ref, ...), custom_call_target="tpu_custom_call" | custom-call | bytes 1048576 | tf_op jit(solution)/shard_map/pallas_call | solution.py:561
Async XLA Ops:
  1.6 10.5 %collective-permute-start.1 = (f32[200,128]{1,0:T(8,128)S(1)}, f32[200,128]{1,0:T(8,128)S(1)}, u32[]{:S(2)}, u32[]{:S(2)}) collective-permute-start(f32[200,128]{1,0:T(8,128)S(1)} %concatenate.3.refs_2_), channel_id=1, source_target_pairs={{0,2},{1,3},{2,0},{3,1},{4,6},{5,7},{6,4},{7,5},{8,10},{9,11},{10,... | collective-permute-start | bytes 307208 | tf_op jit(solution)/shard_map/ppermute | solution.py:596
  5.6 6.5 %collective-permute-start = (f32[200,128]{1,0:T(8,128)S(1)}, f32[200,128]{1,0:T(8,128)S(1)}, u32[]{:S(2)}, u32[]{:S(2)}) collective-permute-start(f32[200,128]{1,0:T(8,128)S(1)} %concatenate.3.refs_2_), channel_id=1, source_target_pairs={{0,1},{1,0},{2,3},{3,2},{4,5},{5,4},{6,7},{7,6},{8,9},{9,8},{10,11... | collective-permute-start | bytes 307208 | tf_op jit(solution)/shard_map/ppermute | solution.py:596
  7.2 6.9 %collective-permute-start.2 = (f32[200,128]{1,0:T(8,128)S(1)}, f32[200,128]{1,0:T(8,128)S(1)}, u32[]{:S(2)}, u32[]{:S(2)}) collective-permute-start(f32[200,128]{1,0:T(8,128)S(1)} %concatenate.3.refs_2_), channel_id=1, source_target_pairs={{0,3},{1,2},{2,1},{3,0},{4,7},{5,6},{6,5},{7,4},{8,11},{9,10},{10,... | collective-permute-start | bytes 307208 | tf_op jit(solution)/shard_map/ppermute | solution.py:596
  7.8 1.3 %copy-start = (bf16[2240,256]{1,0:T(8,128)(2,1)S(1)}, bf16[2240,256]{1,0:T(8,128)(2,1)}, u32[]{:S(2)}) copy-start(bf16[2240,256]{1,0:T(8,128)(2,1)} %constant.2.clone.mats.refs_0_) | copy-start | bytes 3440644
  15.1 4.8 %collective-permute-start.3 = (f32[4,3,8,128]{3,2,1,0:T(8,128)S(1)}, f32[4,3,8,128]{3,2,1,0:T(8,128)S(1)}, u32[]{:S(2)}, u32[]{:S(2)}) collective-permute-start(f32[4,3,8,128]{3,2,1,0:T(8,128)S(1)} %get-tuple-element.36.refs_4_), channel_id=1, source_target_pairs={{0,28},{4,8},{8,4},{12,16},{16,12},{20,24},{24,20},{28,0},{1,29},{... | collective-permute-start | bytes 147464 | tf_op jit(solution)/shard_map/ppermute | solution.py:576
  16.4 3.5 %collective-permute-start.4 = (f32[4,3,8,128]{3,2,1,0:T(8,128)S(1)}, f32[4,3,8,128]{3,2,1,0:T(8,128)S(1)}, u32[]{:S(2)}, u32[]{:S(2)}) collective-permute-start(f32[4,3,8,128]{3,2,1,0:T(8,128)S(1)} %get-tuple-element.37.refs_5_), channel_id=1, source_target_pairs={{0,4},{4,0},{8,12},{12,8},{16,20},{20,16},{24,28},{28,24},{1,5},{5... | collective-permute-start | bytes 147464 | tf_op jit(solution)/shard_map/ppermute | solution.py:576
  21.7 4.6 %collective-permute-start.5 = (f32[4,3,8,128]{3,2,1,0:T(8,128)S(1)}, f32[4,3,8,128]{3,2,1,0:T(8,128)S(1)}, u32[]{:S(2)}, u32[]{:S(2)}) collective-permute-start(f32[4,3,8,128]{3,2,1,0:T(8,128)S(1)} %get-tuple-element.40.refs_4_), channel_id=1, source_target_pairs={{0,28},{4,8},{8,4},{12,16},{16,12},{20,24},{24,20},{28,0},{1,29},{... | collective-permute-start | bytes 147464 | tf_op jit(solution)/shard_map/ppermute | solution.py:576
  22.9 3.4 %collective-permute-start.6 = (f32[4,3,8,128]{3,2,1,0:T(8,128)S(1)}, f32[4,3,8,128]{3,2,1,0:T(8,128)S(1)}, u32[]{:S(2)}, u32[]{:S(2)}) collective-permute-start(f32[4,3,8,128]{3,2,1,0:T(8,128)S(1)} %get-tuple-element.41.refs_5_), channel_id=1, source_target_pairs={{0,4},{4,0},{8,12},{12,8},{16,20},{20,16},{24,28},{28,24},{1,5},{5... | collective-permute-start | bytes 147464 | tf_op jit(solution)/shard_map/ppermute | solution.py:576
  28.0 4.5 %collective-permute-start.7 = (f32[4,3,8,128]{3,2,1,0:T(8,128)S(1)}, f32[4,3,8,128]{3,2,1,0:T(8,128)S(1)}, u32[]{:S(2)}, u32[]{:S(2)}) collective-permute-start(f32[4,3,8,128]{3,2,1,0:T(8,128)S(1)} %get-tuple-element.46.refs_4_), channel_id=1, source_target_pairs={{0,28},{4,8},{8,4},{12,16},{16,12},{20,24},{24,20},{28,0},{1,29},{... | collective-permute-start | bytes 147464 | tf_op jit(solution)/shard_map/ppermute | solution.py:576
  29.1 3.4 %collective-permute-start.8 = (f32[4,3,8,128]{3,2,1,0:T(8,128)S(1)}, f32[4,3,8,128]{3,2,1,0:T(8,128)S(1)}, u32[]{:S(2)}, u32[]{:S(2)}) collective-permute-start(f32[4,3,8,128]{3,2,1,0:T(8,128)S(1)} %get-tuple-element.47.refs_5_), channel_id=1, source_target_pairs={{0,4},{4,0},{8,12},{12,8},{16,20},{20,16},{24,28},{28,24},{1,5},{5... | collective-permute-start | bytes 147464 | tf_op jit(solution)/shard_map/ppermute | solution.py:576
  34.1 4.1 %collective-permute-start.9 = (f32[3,8,128]{2,1,0:T(8,128)S(1)}, f32[3,8,128]{2,1,0:T(8,128)S(1)}, u32[]{:S(2)}, u32[]{:S(2)}) collective-permute-start(f32[3,8,128]{2,1,0:T(8,128)S(1)} %get-tuple-element.52.own_cross_ref), channel_id=1, source_target_pairs={{0,28},{4,8},{8,4},{12,16},{16,12},{20,24},{24,20},{28,0},{1,29},{... | collective-permute-start | bytes 36872 | tf_op jit(solution)/shard_map/ppermute | solution.py:576
  35.2 3.0 %collective-permute-start.10 = (f32[3,8,128]{2,1,0:T(8,128)S(1)}, f32[3,8,128]{2,1,0:T(8,128)S(1)}, u32[]{:S(2)}, u32[]{:S(2)}) collective-permute-start(f32[3,8,128]{2,1,0:T(8,128)S(1)} %get-tuple-element.53.own_core_ref), channel_id=1, source_target_pairs={{0,4},{4,0},{8,12},{12,8},{16,20},{20,16},{24,28},{28,24},{1,5},{5... | collective-permute-start | bytes 36872 | tf_op jit(solution)/shard_map/ppermute | solution.py:576

commit v6 on v5

--- a/solution.py
+++ b/solution.py
@@ -104,6 +104,8 @@
     span_b = np.concatenate(first_b + second_b, axis=0)
     values = np.kron(interp, interp)
     plane = np.concatenate([values, np.kron(2.0 * deriv, interp), np.kron(interp, 2.0 * deriv)])
+    order = np.concatenate([np.arange(8, 56), np.arange(8), np.arange(56, 64)])
+    plane, values = plane[:, order], values[:, order]
     plane = stack_columns(plane)
     values = stack_columns(values)
     back = interp.T * fine_w[None, :] / gll_w[:, None]
@@ -224,17 +226,23 @@
     return spots
 
 
+def plane_parts(x):
+    out = []
+    for c in range(3):
+        rows = x[c * 64 : c * 64 + 64]
+        out.append(split(jnp.concatenate([rows[8:56], rows[:8], rows[56:]], axis=0)))
+    return out
+
+
 def plane_forward(spots, mats):
     plane, values = read(mats, "plane"), read(mats, "values")
-    interp, deriv = (jnp.concatenate([s[i] for s in spots], axis=1) for i in range(2))
-    interp, deriv = split(interp), split(deriv)
     outs = []
     for c in range(3):
-        rows = slice(c * 64, c * 64 + 64)
-        high, low = interp[0][rows], interp[1][rows]
-        first = dot(plane, jnp.concatenate([high, low, high], axis=0))
-        high, low = deriv[0][rows], deriv[1][rows]
-        outs.append((first, dot(values, jnp.concatenate([high, low, high], axis=0))))
+        pair = []
+        for part, matrix in enumerate((plane, values)):
+            high, low = (jnp.concatenate([s[part][c][k] for s in spots], axis=1) for k in range(2))
+            pair.append(dot(matrix, jnp.concatenate([high, low, high], axis=0)))
+        outs.append(pair)
     return outs
 
 
@@ -310,7 +318,8 @@
         backs.append(back)
         span_back(len(fields), backs, results, mats)
 
-    weak_spots(span_forward(fields, mats), inverses, mats, put)
+    spots = [[plane_parts(x) for x in pair] for pair in span_forward(fields, mats)]
+    weak_spots(spots, inverses, mats, put)
     return results
 
 
@@ -343,6 +352,19 @@
     inner = inner.reshape(3, 6, 8, SPAN)
     faces = faces.reshape(3, 2, 8, SPAN)
     return jnp.concatenate([faces[:, :1], inner, faces[:, 1:]], axis=1).reshape(ROWS, SPAN)
+
+
+def parts_with_faces(inner_ref, faces):
+    out = []
+    for c in range(3):
+        ends = split(faces[c * 16 : c * 16 + 16])
+        out.append(
+            [
+                jnp.concatenate([inner_ref[k, c * 48 : c * 48 + 48], ends[k]], axis=0)
+                for k in range(2)
+            ]
+        )
+    return out
 
 
 def join_heights(layers, heights, joins):
@@ -462,7 +484,8 @@
         fields.append(inner_rows(field_ref[l]) + step * partial(l))
     for i, pair in enumerate(span_forward(fields, mats)):
         for part in range(2):
-            spots_ref[i, part] = pair[part]
+            for k, half in enumerate(split(pair[part])):
+                spots_ref[i, part, k] = half
 
 
 def first_inner_kernel(
@@ -522,7 +545,7 @@
         fields.append(end_rows(field_ref[l]) + step * ends)
     spots = []
     for i, pair in enumerate(face_spots(fields, mats)):
-        spots.append([with_faces(spots_ref[i, part], pair[part]) for part in range(2)])
+        spots.append([parts_with_faces(spots_ref.at[i, part], pair[part]) for part in range(2)])
     ends, results = [], []
 
     def put(i, back):
@@ -556,7 +579,9 @@
 
 
 def call(kernel, outs, args, scratch=(), flops=0):
-    shapes = [jax.ShapeDtypeStruct(shape, f32) for shape in outs]
+    shapes = [
+        jax.ShapeDtypeStruct(shape, bf16 if len(shape) == 5 else f32) for shape in outs
+    ]
     one = len(shapes) == 1
     return pl.pallas_call(
         kernel,
@@ -617,7 +642,7 @@
     for stage, share in enumerate((0.5, 0.5, 1.0)):
         last = stage == 2
         used = 3 if last else layers
-        outs = [(len(spots_of(used)), 2, 144, SPAN), (144, SPAN)]
+        outs = [(len(spots_of(used)), 2, 2, 144, SPAN), (144, SPAN)]
         if stage == 0:
             spots, total = call(
                 functools.partial(first_inner_kernel, layers, share, last),

time: 39 us -> 38.9 us (level)
  no operation moved by 1% of the time
where the time goes in v6:
time: 38.9 us; the launch traced here: 38.7 us
  waiting for transfers between devices  13.6 us (35%)
  starting transfers between devices  10.8 us (28%)
  Pallas kernels  10.8 us (28%)
  local copies, waits for them, and re-layouts  2.16 us (6%)
  between operations  1.38 us (4%)
    pallas_call x11, Pallas kernels, call(): pl.pallas_call(kernel, out_shape=shapes[0] if one else shapes, in_specs=[...  10.8 us
    ppermute x4, waiting for transfers between devices, swap_stream(): lax.ppermute(cross, 'horiz', crosses)  10.4 us
    ppermute x3, starting transfers between devices, on_device(): slots[j] = lax.ppermute(packed, 'vert', [(i, i ^ j) for i in range(layers)])  5.62 us
    ppermute x4, starting transfers between devices, swap_stream(): lax.ppermute(cross, 'horiz', crosses)  4.72 us
    ppermute x3, waiting for transfers between devices, on_device(): slots[j] = lax.ppermute(packed, 'vert', [(i, i ^ j) for i in range(layers)])  3.14 us
    unnamed x2, local copies, waits for them, and re-layouts  1.25 us
    concatenate x1, local copies, waits for them, and re-layouts, on_device(): jnp.concatenate([own_field, jnp.broadcast_to(heights[:, None], (8, SPAN))...  0.9 us
  transfers between devices with their start and end apart: 11, of which 6 were waited for; matrix products, arithmetic and copies ran while one was open for 0% of the time, Pallas kernels for 11%

profile of v6, /device:TPU:0, one launch (start us, length us, event | category | flops | bytes accessed | tf_op | source)
XLA Modules:
  0.0 38.7 jit_solution(12227266974883151289)
XLA Ops:
  0.7 0.9 %concatenate.3.refs_2_ = f32[200,128]{1,0:T(8,128)S(1)} pad(f32[192,128]{1,0:T(8,128)} %bitcast.6, f32[]{:T(128)} %bitcast.4), padding=0_8x0_0 | pad | bytes 200708 | tf_op jit(solution)/shard_map/concatenate | solution.py:616
  1.6 4.0 %collective-permute-start.1 = (f32[200,128]{1,0:T(8,128)S(1)}, f32[200,128]{1,0:T(8,128)S(1)}, u32[]{:S(2)}, u32[]{:S(2)}) collective-permute-start(f32[200,128]{1,0:T(8,128)S(1)} %concatenate.3.refs_2_), channel_id=1, source_target_pairs={{0,2},{1,3},{2,0},{3,1},{4,6},{5,7},{6,4},{7,5},{8,10},{9,11},{10,... | collective-permute-start | bytes 307208 | tf_op jit(solution)/shard_map/ppermute | solution.py:621
  5.6 1.6 %collective-permute-start = (f32[200,128]{1,0:T(8,128)S(1)}, f32[200,128]{1,0:T(8,128)S(1)}, u32[]{:S(2)}, u32[]{:S(2)}) collective-permute-start(f32[200,128]{1,0:T(8,128)S(1)} %concatenate.3.refs_2_), channel_id=1, source_target_pairs={{0,1},{1,0},{2,3},{3,2},{4,5},{5,4},{6,7},{7,6},{8,9},{9,8},{10,11... | collective-permute-start | bytes 307208 | tf_op jit(solution)/shard_map/ppermute | solution.py:621
  7.2 0.0 collective-permute-start.2
  7.8 0.0 copy-start
  7.8 1.2 %copy-done = bf16[2240,256]{1,0:T(8,128)(2,1)S(1)} copy-done((bf16[2240,256]{1,0:T(8,128)(2,1)S(1)}, bf16[2240,256]{1,0:T(8,128)(2,1)}, u32[]{:S(2)}) %copy-start) | copy-done | bytes 1146904
  9.1 0.1 shard_map.46.refs_1_.step_ref
  9.2 2.9 %collective-permute-done.1.refs_4_ = f32[200,128]{1,0:T(8,128)S(1)} collective-permute-done((f32[200,128]{1,0:T(8,128)S(1)}, f32[200,128]{1,0:T(8,128)S(1)}, u32[]{:S(2)}, u32[]{:S(2)}) %collective-permute-start.1) | collective-permute-done | bytes 102432 | tf_op jit(solution)/shard_map/ppermute | solution.py:621
  12.1 0.0 collective-permute-done.refs_3_
  12.1 1.7 %shard_map.47 = (f32[192,128]{1,0:T(8,128)S(1)}, f32[192,128]{1,0:T(8,128)S(1)}, f32[192,128]{1,0:T(8,128)S(1)}) custom-call(bf16[2240,256]{1,0:T(8,128)(2,1)S(1)} %copy-done, f32[8,128]{1,0:T(8,128)S(1)} %shard_map.46.refs_1_.step_ref, f32[200,128]{1,0:T(8,128)S(1)} %concatenate.3.refs_2_, f32[200,128]{1,0:T(8,128)S(1)} %collective-permute-done.refs_3_, ...), custom_call_target="tpu_custom_call" | custom-call | flops 1179648000 | bytes 1048576 | tf_op jit(solution)/shard_map/pallas_call | solution.py:586
  13.8 0.2 collective-permute-done.2.refs_5_
  14.0 1.0 %shard_map.48 = (f32[4,192,128]{2,1,0:T(8,128)S(1)}, f32[4,8,128]{2,1,0:T(8,128)S(1)}, f32[4,192,128]{2,1,0:T(8,128)S(1)}, f32[4,3,8,128]{3,2,1,0:T(8,128)S(1)}, f32[4,3,8,128]{3,2,1,0:T(8,128)S(1)}) custom-call(bf16[2240,256]{1,0:T(8,128)(2,1)S(1)} %copy-done, f32[8,128]{1,0:T(8,128)S(1)} %shard_map.46.refs_1_.step_ref, f32[200,128]{1,0:T(8,128)S(1)} %concatenate.3.refs_2_, ...), custom_call_target="tpu_custom_call" | custom-call | flops 1572864000 | bytes 1048576 | tf_op jit(solution)/shard_map/pallas_call | solution.py:586
  15.1 1.3 %collective-permute-start.3 = (f32[4,3,8,128]{3,2,1,0:T(8,128)S(1)}, f32[4,3,8,128]{3,2,1,0:T(8,128)S(1)}, u32[]{:S(2)}, u32[]{:S(2)}) collective-permute-start(f32[4,3,8,128]{3,2,1,0:T(8,128)S(1)} %get-tuple-element.36.refs_4_), channel_id=1, source_target_pairs={{0,28},{4,8},{8,4},{12,16},{16,12},{20,24},{24,20},{28,0},{1,29},{... | collective-permute-start | bytes 147464 | tf_op jit(solution)/shard_map/ppermute | solution.py:601
  16.4 0.4 %collective-permute-start.4 = (f32[4,3,8,128]{3,2,1,0:T(8,128)S(1)}, f32[4,3,8,128]{3,2,1,0:T(8,128)S(1)}, u32[]{:S(2)}, u32[]{:S(2)}) collective-permute-start(f32[4,3,8,128]{3,2,1,0:T(8,128)S(1)} %get-tuple-element.37.refs_5_), channel_id=1, source_target_pairs={{0,4},{4,0},{8,12},{12,8},{16,20},{20,16},{24,28},{28,24},{1,5},{5... | collective-permute-start | bytes 147464 | tf_op jit(solution)/shard_map/ppermute | solution.py:601
  16.8 0.4 %shard_map.49 = (bf16[6,2,2,144,128]{4,3,2,1,0:T(8,128)(2,1)S(1)}, f32[144,128]{1,0:T(8,128)S(1)}) custom-call(bf16[2240,256]{1,0:T(8,128)(2,1)S(1)} %copy-done, f32[8,128]{1,0:T(8,128)S(1)} %shard_map.46.refs_1_.step_ref, f32[4,192,128]{2,1,0:T(8,128)S(1)} %get-tuple-element.34.field_ref.refs_2_, f32[4,192,128]{2,1,0:T(8,128)S(1)} %get-tuple-element.38.partial_ref), custom_call_target="tpu_custom_call" | custom-call | flops 393216000 | bytes 1048576 | tf_op jit(solution)/shard_map/pallas_call | solution.py:586
  17.3 2.7 %collective-permute-done.3.refs_6_ = f32[4,3,8,128]{3,2,1,0:T(8,128)S(1)} collective-permute-done((f32[4,3,8,128]{3,2,1,0:T(8,128)S(1)}, f32[4,3,8,128]{3,2,1,0:T(8,128)S(1)}, u32[]{:S(2)}, u32[]{:S(2)}) %collective-permute-start.3) | collective-permute-done | bytes 49184 | tf_op jit(solution)/shard_map/ppermute | solution.py:601
  19.9 0.0 collective-permute-done.4.refs_7_
  19.9 1.7 %shard_map.50 = (f32[2,3,8,128]{3,2,1,0:T(8,128)S(1)}, f32[6,192,128]{2,1,0:T(8,128)S(1)}, f32[4,3,8,128]{3,2,1,0:T(8,128)S(1)}, f32[4,3,8,128]{3,2,1,0:T(8,128)S(1)}) custom-call(bf16[2240,256]{1,0:T(8,128)(2,1)S(1)} %copy-done, f32[8,128]{1,0:T(8,128)S(1)} %shard_map.46.refs_1_.step_ref, f32[4,192,128]{2,1,0:T(8,128)S(1)} %get-tuple-element.34.field_ref.refs_2_, ...), custom_call_target="tpu_custom_call" | custom-call | flops 1572864000 | bytes 1048576 | tf_op jit(solution)/shard_map/pallas_call | solution.py:586
  21.6 1.2 %collective-permute-start.5 = (f32[4,3,8,128]{3,2,1,0:T(8,128)S(1)}, f32[4,3,8,128]{3,2,1,0:T(8,128)S(1)}, u32[]{:S(2)}, u32[]{:S(2)}) collective-permute-start(f32[4,3,8,128]{3,2,1,0:T(8,128)S(1)} %get-tuple-element.40.refs_4_), channel_id=1, source_target_pairs={{0,28},{4,8},{8,4},{12,16},{16,12},{20,24},{24,20},{28,0},{1,29},{... | collective-permute-start | bytes 147464 | tf_op jit(solution)/shard_map/ppermute | solution.py:601
  22.8 0.0 collective-permute-start.6
  22.8 0.8 %shard_map.51 = (bf16[6,2,2,144,128]{4,3,2,1,0:T(8,128)(2,1)S(1)}, f32[144,128]{1,0:T(8,128)S(1)}) custom-call(bf16[2240,256]{1,0:T(8,128)(2,1)S(1)} %copy-done, f32[8,128]{1,0:T(8,128)S(1)} %shard_map.46.refs_1_.step_ref, f32[4,192,128]{2,1,0:T(8,128)S(1)} %get-tuple-element.34.field_ref.refs_2_, f32[4,8,128]{2,1,0:T(8,128)S(1)} %get-tuple-element.35.refs_3_.heights_ref, ...), custom_call_target="tpu_custom_call" | custom-call | flops 786432000 | bytes 1048576 | tf_op jit(solution)/shard_map/pallas_call | solution.py:586
  23.6 2.6 %collective-permute-done.5.refs_6_ = f32[4,3,8,128]{3,2,1,0:T(8,128)S(1)} collective-permute-done((f32[4,3,8,128]{3,2,1,0:T(8,128)S(1)}, f32[4,3,8,128]{3,2,1,0:T(8,128)S(1)}, u32[]{:S(2)}, u32[]{:S(2)}) %collective-permute-start.5) | collective-permute-done | bytes 49184 | tf_op jit(solution)/shard_map/ppermute | solution.py:601
  26.2 0.0 collective-permute-done.6.refs_7_
  26.2 1.7 %shard_map.52 = (f32[2,3,8,128]{3,2,1,0:T(8,128)S(1)}, f32[6,192,128]{2,1,0:T(8,128)S(1)}, f32[4,3,8,128]{3,2,1,0:T(8,128)S(1)}, f32[4,3,8,128]{3,2,1,0:T(8,128)S(1)}) custom-call(bf16[2240,256]{1,0:T(8,128)(2,1)S(1)} %copy-done, f32[8,128]{1,0:T(8,128)S(1)} %shard_map.46.refs_1_.step_ref, f32[4,192,128]{2,1,0:T(8,128)S(1)} %get-tuple-element.34.field_ref.refs_2_, ...), custom_call_target="tpu_custom_call" | custom-call | flops 1572864000 | bytes 1048576 | tf_op jit(solution)/shard_map/pallas_call | solution.py:586
  27.9 1.1 %collective-permute-start.7 = (f32[4,3,8,128]{3,2,1,0:T(8,128)S(1)}, f32[4,3,8,128]{3,2,1,0:T(8,128)S(1)}, u32[]{:S(2)}, u32[]{:S(2)}) collective-permute-start(f32[4,3,8,128]{3,2,1,0:T(8,128)S(1)} %get-tuple-element.46.refs_4_), channel_id=1, source_target_pairs={{0,28},{4,8},{8,4},{12,16},{16,12},{20,24},{24,20},{28,0},{1,29},{... | collective-permute-start | bytes 147464 | tf_op jit(solution)/shard_map/ppermute | solution.py:601
  29.0 0.0 collective-permute-start.8
  29.0 0.8 %shard_map.53 = (bf16[5,2,2,144,128]{4,3,2,1,0:T(8,128)(2,1)S(1)}, f32[144,128]{1,0:T(8,128)S(1)}) custom-call(bf16[2240,256]{1,0:T(8,128)(2,1)S(1)} %copy-done, f32[8,128]{1,0:T(8,128)S(1)} %shard_map.46.refs_1_.step_ref, f32[4,192,128]{2,1,0:T(8,128)S(1)} %get-tuple-element.34.field_ref.refs_2_, f32[4,8,128]{2,1,0:T(8,128)S(1)} %get-tuple-element.35.refs_3_.heights_ref, ...), custom_call_target="tpu_custom_call" | custom-call | flops 589824000 | bytes 1048576 | tf_op jit(solution)/shard_map/pallas_call | solution.py:586
  29.8 2.6 %collective-permute-done.7.refs_6_ = f32[4,3,8,128]{3,2,1,0:T(8,128)S(1)} collective-permute-done((f32[4,3,8,128]{3,2,1,0:T(8,128)S(1)}, f32[4,3,8,128]{3,2,1,0:T(8,128)S(1)}, u32[]{:S(2)}, u32[]{:S(2)}) %collective-permute-start.7) | collective-permute-done | bytes 49184 | tf_op jit(solution)/shard_map/ppermute | solution.py:601
  32.3 0.0 collective-permute-done.8.refs_7_
  32.3 1.6 %shard_map.54 = (f32[2,3,8,128]{3,2,1,0:T(8,128)S(1)}, f32[5,192,128]{2,1,0:T(8,128)S(1)}, f32[3,8,128]{2,1,0:T(8,128)S(1)}, f32[3,8,128]{2,1,0:T(8,128)S(1)}) custom-call(bf16[2240,256]{1,0:T(8,128)(2,1)S(1)} %copy-done, f32[8,128]{1,0:T(8,128)S(1)} %shard_map.46.refs_1_.step_ref, f32[4,192,128]{2,1,0:T(8,128)S(1)} %get-tuple-element.34.field_ref.refs_2_, ...), custom_call_target="tpu_custom_call" | custom-call | flops 1179648000 | bytes 1048576 | tf_op jit(solution)/shard_map/pallas_call | solution.py:586
  33.9 1.1 %collective-permute-start.9 = (f32[3,8,128]{2,1,0:T(8,128)S(1)}, f32[3,8,128]{2,1,0:T(8,128)S(1)}, u32[]{:S(2)}, u32[]{:S(2)}) collective-permute-start(f32[3,8,128]{2,1,0:T(8,128)S(1)} %get-tuple-element.52.own_cross_ref), channel_id=1, source_target_pairs={{0,28},{4,8},{8,4},{12,16},{16,12},{20,24},{24,20},{28,0},{1,29},{... | collective-permute-start | bytes 36872 | tf_op jit(solution)/shard_map/ppermute | solution.py:601
  35.1 0.0 collective-permute-start.10
  35.1 0.4 shard_map.55.inner_ref
  35.4 2.6 %collective-permute-done.9.cross_ref = f32[3,8,128]{2,1,0:T(8,128)S(1)} collective-permute-done((f32[3,8,128]{2,1,0:T(8,128)S(1)}, f32[3,8,128]{2,1,0:T(8,128)S(1)}, u32[]{:S(2)}, u32[]{:S(2)}) %collective-permute-start.9) | collective-permute-done | bytes 12320 | tf_op jit(solution)/shard_map/ppermute | solution.py:601
  38.0 0.0 collective-permute-done.10.core_ref
  38.0 0.7 %shard_map.56 = f32[192,128]{1,0:T(8,128)} custom-call(f32[3,8,128]{2,1,0:T(8,128)S(1)} %get-tuple-element.52.own_cross_ref, f32[3,8,128]{2,1,0:T(8,128)S(1)} %get-tuple-element.53.own_core_ref, f32[3,8,128]{2,1,0:T(8,128)S(1)} %collective-permute-done.9.cross_ref, f32[3,8,128]{2,1,0:T(8,128)S(1)} %collective-permute-done.10.core_ref, ...), custom_call_target="tpu_custom_call" | custom-call | bytes 1048576 | tf_op jit(solution)/shard_map/pallas_call | solution.py:586
Async XLA Ops:
  1.6 10.5 %collective-permute-start.1 = (f32[200,128]{1,0:T(8,128)S(1)}, f32[200,128]{1,0:T(8,128)S(1)}, u32[]{:S(2)}, u32[]{:S(2)}) collective-permute-start(f32[200,128]{1,0:T(8,128)S(1)} %concatenate.3.refs_2_), channel_id=1, source_target_pairs={{0,2},{1,3},{2,0},{3,1},{4,6},{5,7},{6,4},{7,5},{8,10},{9,11},{10,... | collective-permute-start | bytes 307208 | tf_op jit(solution)/shard_map/ppermute | solution.py:621
  5.6 6.5 %collective-permute-start = (f32[200,128]{1,0:T(8,128)S(1)}, f32[200,128]{1,0:T(8,128)S(1)}, u32[]{:S(2)}, u32[]{:S(2)}) collective-permute-start(f32[200,128]{1,0:T(8,128)S(1)} %concatenate.3.refs_2_), channel_id=1, source_target_pairs={{0,1},{1,0},{2,3},{3,2},{4,5},{5,4},{6,7},{7,6},{8,9},{9,8},{10,11... | collective-permute-start | bytes 307208 | tf_op jit(solution)/shard_map/ppermute | solution.py:621
  7.2 6.9 %collective-permute-start.2 = (f32[200,128]{1,0:T(8,128)S(1)}, f32[200,128]{1,0:T(8,128)S(1)}, u32[]{:S(2)}, u32[]{:S(2)}) collective-permute-start(f32[200,128]{1,0:T(8,128)S(1)} %concatenate.3.refs_2_), channel_id=1, source_target_pairs={{0,3},{1,2},{2,1},{3,0},{4,7},{5,6},{6,5},{7,4},{8,11},{9,10},{10,... | collective-permute-start | bytes 307208 | tf_op jit(solution)/shard_map/ppermute | solution.py:621
  7.8 1.3 %copy-start = (bf16[2240,256]{1,0:T(8,128)(2,1)S(1)}, bf16[2240,256]{1,0:T(8,128)(2,1)}, u32[]{:S(2)}) copy-start(bf16[2240,256]{1,0:T(8,128)(2,1)} %constant.2.clone.mats.refs_0_) | copy-start | bytes 3440644
  15.1 4.8 %collective-permute-start.3 = (f32[4,3,8,128]{3,2,1,0:T(8,128)S(1)}, f32[4,3,8,128]{3,2,1,0:T(8,128)S(1)}, u32[]{:S(2)}, u32[]{:S(2)}) collective-permute-start(f32[4,3,8,128]{3,2,1,0:T(8,128)S(1)} %get-tuple-element.36.refs_4_), channel_id=1, source_target_pairs={{0,28},{4,8},{8,4},{12,16},{16,12},{20,24},{24,20},{28,0},{1,29},{... | collective-permute-start | bytes 147464 | tf_op jit(solution)/shard_map/ppermute | solution.py:601
  16.4 3.6 %collective-permute-start.4 = (f32[4,3,8,128]{3,2,1,0:T(8,128)S(1)}, f32[4,3,8,128]{3,2,1,0:T(8,128)S(1)}, u32[]{:S(2)}, u32[]{:S(2)}) collective-permute-start(f32[4,3,8,128]{3,2,1,0:T(8,128)S(1)} %get-tuple-element.37.refs_5_), channel_id=1, source_target_pairs={{0,4},{4,0},{8,12},{12,8},{16,20},{20,16},{24,28},{28,24},{1,5},{5... | collective-permute-start | bytes 147464 | tf_op jit(solution)/shard_map/ppermute | solution.py:601
  21.6 4.6 %collective-permute-start.5 = (f32[4,3,8,128]{3,2,1,0:T(8,128)S(1)}, f32[4,3,8,128]{3,2,1,0:T(8,128)S(1)}, u32[]{:S(2)}, u32[]{:S(2)}) collective-permute-start(f32[4,3,8,128]{3,2,1,0:T(8,128)S(1)} %get-tuple-element.40.refs_4_), channel_id=1, source_target_pairs={{0,28},{4,8},{8,4},{12,16},{16,12},{20,24},{24,20},{28,0},{1,29},{... | collective-permute-start | bytes 147464 | tf_op jit(solution)/shard_map/ppermute | solution.py:601
  22.8 3.4 %collective-permute-start.6 = (f32[4,3,8,128]{3,2,1,0:T(8,128)S(1)}, f32[4,3,8,128]{3,2,1,0:T(8,128)S(1)}, u32[]{:S(2)}, u32[]{:S(2)}) collective-permute-start(f32[4,3,8,128]{3,2,1,0:T(8,128)S(1)} %get-tuple-element.41.refs_5_), channel_id=1, source_target_pairs={{0,4},{4,0},{8,12},{12,8},{16,20},{20,16},{24,28},{28,24},{1,5},{5... | collective-permute-start | bytes 147464 | tf_op jit(solution)/shard_map/ppermute | solution.py:601
  27.9 4.5 %collective-permute-start.7 = (f32[4,3,8,128]{3,2,1,0:T(8,128)S(1)}, f32[4,3,8,128]{3,2,1,0:T(8,128)S(1)}, u32[]{:S(2)}, u32[]{:S(2)}) collective-permute-start(f32[4,3,8,128]{3,2,1,0:T(8,128)S(1)} %get-tuple-element.46.refs_4_), channel_id=1, source_target_pairs={{0,28},{4,8},{8,4},{12,16},{16,12},{20,24},{24,20},{28,0},{1,29},{... | collective-permute-start | bytes 147464 | tf_op jit(solution)/shard_map/ppermute | solution.py:601
  29.0 3.4 %collective-permute-start.8 = (f32[4,3,8,128]{3,2,1,0:T(8,128)S(1)}, f32[4,3,8,128]{3,2,1,0:T(8,128)S(1)}, u32[]{:S(2)}, u32[]{:S(2)}) collective-permute-start(f32[4,3,8,128]{3,2,1,0:T(8,128)S(1)} %get-tuple-element.47.refs_5_), channel_id=1, source_target_pairs={{0,4},{4,0},{8,12},{12,8},{16,20},{20,16},{24,28},{28,24},{1,5},{5... | collective-permute-start | bytes 147464 | tf_op jit(solution)/shard_map/ppermute | solution.py:601
  33.9 4.1 %collective-permute-start.9 = (f32[3,8,128]{2,1,0:T(8,128)S(1)}, f32[3,8,128]{2,1,0:T(8,128)S(1)}, u32[]{:S(2)}, u32[]{:S(2)}) collective-permute-start(f32[3,8,128]{2,1,0:T(8,128)S(1)} %get-tuple-element.52.own_cross_ref), channel_id=1, source_target_pairs={{0,28},{4,8},{8,4},{12,16},{16,12},{20,24},{24,20},{28,0},{1,29},{... | collective-permute-start | bytes 36872 | tf_op jit(solution)/shard_map/ppermute | solution.py:601
  35.1 3.0 %collective-permute-start.10 = (f32[3,8,128]{2,1,0:T(8,128)S(1)}, f32[3,8,128]{2,1,0:T(8,128)S(1)}, u32[]{:S(2)}, u32[]{:S(2)}) collective-permute-start(f32[3,8,128]{2,1,0:T(8,128)S(1)} %get-tuple-element.53.own_core_ref), channel_id=1, source_target_pairs={{0,4},{4,0},{8,12},{12,8},{16,20},{20,16},{24,28},{28,24},{1,5},{5... | collective-permute-start | bytes 36872 | tf_op jit(solution)/shard_map/ppermute | solution.py:601

commit v7 on v6

--- a/solution.py
+++ b/solution.py
@@ -529,7 +529,7 @@
     rate_ref[...] = (total_ref[...] + partial_ref[0]) / 6.0
 
 
-def stage_kernel(count, share, first, last, *refs):
+def stage_kernel(count, share, first, next_last, last, *refs):
     mats, step_ref, field_ref, heights_ref, own_cross_ref, own_core_ref = refs[:6]
     cross_ref, core_ref, spots_ref = refs[6:9]
     total = None if first else refs[9]
@@ -539,8 +539,9 @@
     layers = stage_layers(count, last)
     heights = [heights_ref[l] for l in layers]
     fields = []
-    for l in layers:
-        ends = join_ends(own_cross_ref[l], own_core_ref[l], cross_ref[l], core_ref[l])
+    for i, l in enumerate(layers):
+        at = i if last else l
+        ends = join_ends(own_cross_ref[at], own_core_ref[at], cross_ref[at], core_ref[at])
         ends = in_order(*ends).reshape(48, SPAN)
         fields.append(end_rows(field_ref[l]) + step * ends)
     spots = []
@@ -562,8 +563,9 @@
         put_faces(faces_ref[0], next_cross_ref, next_core_ref, slice(None))
     else:
         join_heights(faces, heights, [(l, l + 1, True) for l in range(count - 1)])
-        for l in range(count):
-            put_faces(faces_ref[l], next_cross_ref, next_core_ref, l)
+        for i, l in enumerate(stage_layers(count, next_last)):
+            put_faces(faces_ref[l], next_cross_ref, next_core_ref, i)
+    place = 0 if last else place
     own = join_ends(own_cross_ref[place], own_core_ref[place], cross_ref[place], core_ref[place])
     for k in range(2):
         total_ref[k] = own[k] if first else total[k] + 2.0 * own[k]
@@ -659,9 +661,9 @@
                 flops=used * unit // 2,
             )
         args = [mats, step, fields, all_heights, *own_ends, *ends, spots]
-        end = small if last else face
+        end = (small, (3,) + small, face)[2 - stage]
         face_total, backs, cross, core = call(
-            functools.partial(stage_kernel, layers, share, stage == 0, last),
+            functools.partial(stage_kernel, layers, share, stage == 0, stage == 1, last),
             [(2,) + small, (len(spots_of(used)), ROWS, SPAN), end, end],
             args + ([] if stage == 0 else [face_total]),
             scratch=[pltpu.VMEM((used, 48, SPAN), f32)],

time: 38.9 us -> 38.7 us (level)
  no operation moved by 1% of the time
where the time goes in v7:
time: 38.7 us; the launch traced here: 38.5 us
  waiting for transfers between devices  13.4 us (35%)
  starting transfers between devices  10.8 us (28%)
  Pallas kernels  10.8 us (28%)
  local copies, waits for them, and re-layouts  2.16 us (6%)
  between operations  1.38 us (4%)
    pallas_call x11, Pallas kernels, call(): pl.pallas_call(kernel, out_shape=shapes[0] if one else shapes, in_specs=[...  10.8 us
    ppermute x4, waiting for transfers between devices, swap_stream(): lax.ppermute(cross, 'horiz', crosses)  10.3 us
    ppermute x3, starting transfers between devices, on_device(): slots[j] = lax.ppermute(packed, 'vert', [(i, i ^ j) for i in range(layers)])  5.62 us
    ppermute x4, starting transfers between devices, swap_stream(): lax.ppermute(cross, 'horiz', crosses)  4.72 us
    ppermute x3, waiting for transfers between devices, on_device(): slots[j] = lax.ppermute(packed, 'vert', [(i, i ^ j) for i in range(layers)])  3.14 us
    unnamed x2, local copies, waits for them, and re-layouts  1.25 us
    concatenate x1, local copies, waits for them, and re-layouts, on_device(): jnp.concatenate([own_field, jnp.broadcast_to(heights[:, None], (8, SPAN))...  0.9 us
  transfers between devices with their start and end apart: 11, of which 6 were waited for; matrix products, arithmetic and copies ran while one was open for 0% of the time, Pallas kernels for 11%

profile of v7, /device:TPU:0, one launch (start us, length us, event | category | flops | bytes accessed | tf_op | source)
XLA Modules:
  0.0 38.5 jit_solution(15411957156166758828)
XLA Ops:
  0.7 0.9 %concatenate.3.refs_2_ = f32[200,128]{1,0:T(8,128)S(1)} pad(f32[192,128]{1,0:T(8,128)} %bitcast.6, f32[]{:T(128)} %bitcast.4), padding=0_8x0_0 | pad | bytes 200708 | tf_op jit(solution)/shard_map/concatenate | solution.py:618
  1.6 4.0 %collective-permute-start.1 = (f32[200,128]{1,0:T(8,128)S(1)}, f32[200,128]{1,0:T(8,128)S(1)}, u32[]{:S(2)}, u32[]{:S(2)}) collective-permute-start(f32[200,128]{1,0:T(8,128)S(1)} %concatenate.3.refs_2_), channel_id=1, source_target_pairs={{0,2},{1,3},{2,0},{3,1},{4,6},{5,7},{6,4},{7,5},{8,10},{9,11},{10,... | collective-permute-start | bytes 307208 | tf_op jit(solution)/shard_map/ppermute | solution.py:623
  5.6 1.6 %collective-permute-start = (f32[200,128]{1,0:T(8,128)S(1)}, f32[200,128]{1,0:T(8,128)S(1)}, u32[]{:S(2)}, u32[]{:S(2)}) collective-permute-start(f32[200,128]{1,0:T(8,128)S(1)} %concatenate.3.refs_2_), channel_id=1, source_target_pairs={{0,1},{1,0},{2,3},{3,2},{4,5},{5,4},{6,7},{7,6},{8,9},{9,8},{10,11... | collective-permute-start | bytes 307208 | tf_op jit(solution)/shard_map/ppermute | solution.py:623
  7.2 0.0 collective-permute-start.2
  7.8 0.0 copy-start
  7.8 1.2 %copy-done = bf16[2240,256]{1,0:T(8,128)(2,1)S(1)} copy-done((bf16[2240,256]{1,0:T(8,128)(2,1)S(1)}, bf16[2240,256]{1,0:T(8,128)(2,1)}, u32[]{:S(2)}) %copy-start) | copy-done | bytes 1146904
  9.1 0.1 shard_map.46.refs_1_.step_ref
  9.2 2.9 %collective-permute-done.1.refs_4_ = f32[200,128]{1,0:T(8,128)S(1)} collective-permute-done((f32[200,128]{1,0:T(8,128)S(1)}, f32[200,128]{1,0:T(8,128)S(1)}, u32[]{:S(2)}, u32[]{:S(2)}) %collective-permute-start.1) | collective-permute-done | bytes 102432 | tf_op jit(solution)/shard_map/ppermute | solution.py:623
  12.1 0.0 collective-permute-done.refs_3_
  12.1 1.7 %shard_map.47 = (f32[192,128]{1,0:T(8,128)S(1)}, f32[192,128]{1,0:T(8,128)S(1)}, f32[192,128]{1,0:T(8,128)S(1)}) custom-call(bf16[2240,256]{1,0:T(8,128)(2,1)S(1)} %copy-done, f32[8,128]{1,0:T(8,128)S(1)} %shard_map.46.refs_1_.step_ref, f32[200,128]{1,0:T(8,128)S(1)} %concatenate.3.refs_2_, f32[200,128]{1,0:T(8,128)S(1)} %collective-permute-done.refs_3_, ...), custom_call_target="tpu_custom_call" | custom-call | flops 1179648000 | bytes 1048576 | tf_op jit(solution)/shard_map/pallas_call | solution.py:588
  13.8 0.2 collective-permute-done.2.refs_5_
  14.0 1.0 %shard_map.48 = (f32[4,192,128]{2,1,0:T(8,128)S(1)}, f32[4,8,128]{2,1,0:T(8,128)S(1)}, f32[4,192,128]{2,1,0:T(8,128)S(1)}, f32[4,3,8,128]{3,2,1,0:T(8,128)S(1)}, f32[4,3,8,128]{3,2,1,0:T(8,128)S(1)}) custom-call(bf16[2240,256]{1,0:T(8,128)(2,1)S(1)} %copy-done, f32[8,128]{1,0:T(8,128)S(1)} %shard_map.46.refs_1_.step_ref, f32[200,128]{1,0:T(8,128)S(1)} %concatenate.3.refs_2_, ...), custom_call_target="tpu_custom_call" | custom-call | flops 1572864000 | bytes 1048576 | tf_op jit(solution)/shard_map/pallas_call | solution.py:588
  15.1 1.3 %collective-permute-start.3 = (f32[4,3,8,128]{3,2,1,0:T(8,128)S(1)}, f32[4,3,8,128]{3,2,1,0:T(8,128)S(1)}, u32[]{:S(2)}, u32[]{:S(2)}) collective-permute-start(f32[4,3,8,128]{3,2,1,0:T(8,128)S(1)} %get-tuple-element.36.refs_4_), channel_id=1, source_target_pairs={{0,28},{4,8},{8,4},{12,16},{16,12},{20,24},{24,20},{28,0},{1,29},{... | collective-permute-start | bytes 147464 | tf_op jit(solution)/shard_map/ppermute | solution.py:603
  16.4 0.4 %collective-permute-start.4 = (f32[4,3,8,128]{3,2,1,0:T(8,128)S(1)}, f32[4,3,8,128]{3,2,1,0:T(8,128)S(1)}, u32[]{:S(2)}, u32[]{:S(2)}) collective-permute-start(f32[4,3,8,128]{3,2,1,0:T(8,128)S(1)} %get-tuple-element.37.refs_5_), channel_id=1, source_target_pairs={{0,4},{4,0},{8,12},{12,8},{16,20},{20,16},{24,28},{28,24},{1,5},{5... | collective-permute-start | bytes 147464 | tf_op jit(solution)/shard_map/ppermute | solution.py:603
  16.8 0.4 %shard_map.49 = (bf16[6,2,2,144,128]{4,3,2,1,0:T(8,128)(2,1)S(1)}, f32[144,128]{1,0:T(8,128)S(1)}) custom-call(bf16[2240,256]{1,0:T(8,128)(2,1)S(1)} %copy-done, f32[8,128]{1,0:T(8,128)S(1)} %shard_map.46.refs_1_.step_ref, f32[4,192,128]{2,1,0:T(8,128)S(1)} %get-tuple-element.34.field_ref.refs_2_, f32[4,192,128]{2,1,0:T(8,128)S(1)} %get-tuple-element.38.partial_ref), custom_call_target="tpu_custom_call" | custom-call | flops 393216000 | bytes 1048576 | tf_op jit(solution)/shard_map/pallas_call | solution.py:588
  17.3 2.7 %collective-permute-done.3.refs_6_ = f32[4,3,8,128]{3,2,1,0:T(8,128)S(1)} collective-permute-done((f32[4,3,8,128]{3,2,1,0:T(8,128)S(1)}, f32[4,3,8,128]{3,2,1,0:T(8,128)S(1)}, u32[]{:S(2)}, u32[]{:S(2)}) %collective-permute-start.3) | collective-permute-done | bytes 49184 | tf_op jit(solution)/shard_map/ppermute | solution.py:603
  19.9 0.0 collective-permute-done.4.refs_7_
  19.9 1.7 %shard_map.50 = (f32[2,3,8,128]{3,2,1,0:T(8,128)S(1)}, f32[6,192,128]{2,1,0:T(8,128)S(1)}, f32[4,3,8,128]{3,2,1,0:T(8,128)S(1)}, f32[4,3,8,128]{3,2,1,0:T(8,128)S(1)}) custom-call(bf16[2240,256]{1,0:T(8,128)(2,1)S(1)} %copy-done, f32[8,128]{1,0:T(8,128)S(1)} %shard_map.46.refs_1_.step_ref, f32[4,192,128]{2,1,0:T(8,128)S(1)} %get-tuple-element.34.field_ref.refs_2_, ...), custom_call_target="tpu_custom_call" | custom-call | flops 1572864000 | bytes 1048576 | tf_op jit(solution)/shard_map/pallas_call | solution.py:588
  21.6 1.2 %collective-permute-start.5 = (f32[4,3,8,128]{3,2,1,0:T(8,128)S(1)}, f32[4,3,8,128]{3,2,1,0:T(8,128)S(1)}, u32[]{:S(2)}, u32[]{:S(2)}) collective-permute-start(f32[4,3,8,128]{3,2,1,0:T(8,128)S(1)} %get-tuple-element.40.refs_4_), channel_id=1, source_target_pairs={{0,28},{4,8},{8,4},{12,16},{16,12},{20,24},{24,20},{28,0},{1,29},{... | collective-permute-start | bytes 147464 | tf_op jit(solution)/shard_map/ppermute | solution.py:603
  22.8 0.0 collective-permute-start.6
  22.8 0.8 %shard_map.51 = (bf16[6,2,2,144,128]{4,3,2,1,0:T(8,128)(2,1)S(1)}, f32[144,128]{1,0:T(8,128)S(1)}) custom-call(bf16[2240,256]{1,0:T(8,128)(2,1)S(1)} %copy-done, f32[8,128]{1,0:T(8,128)S(1)} %shard_map.46.refs_1_.step_ref, f32[4,192,128]{2,1,0:T(8,128)S(1)} %get-tuple-element.34.field_ref.refs_2_, f32[4,8,128]{2,1,0:T(8,128)S(1)} %get-tuple-element.35.refs_3_.heights_ref, ...), custom_call_target="tpu_custom_call" | custom-call | flops 786432000 | bytes 1048576 | tf_op jit(solution)/shard_map/pallas_call | solution.py:588
  23.6 2.6 %collective-permute-done.5.refs_6_ = f32[4,3,8,128]{3,2,1,0:T(8,128)S(1)} collective-permute-done((f32[4,3,8,128]{3,2,1,0:T(8,128)S(1)}, f32[4,3,8,128]{3,2,1,0:T(8,128)S(1)}, u32[]{:S(2)}, u32[]{:S(2)}) %collective-permute-start.5) | collective-permute-done | bytes 49184 | tf_op jit(solution)/shard_map/ppermute | solution.py:603
  26.2 0.0 collective-permute-done.6.refs_7_
  26.2 1.7 %shard_map.52 = (f32[2,3,8,128]{3,2,1,0:T(8,128)S(1)}, f32[6,192,128]{2,1,0:T(8,128)S(1)}, f32[3,3,8,128]{3,2,1,0:T(8,128)S(1)}, f32[3,3,8,128]{3,2,1,0:T(8,128)S(1)}) custom-call(bf16[2240,256]{1,0:T(8,128)(2,1)S(1)} %copy-done, f32[8,128]{1,0:T(8,128)S(1)} %shard_map.46.refs_1_.step_ref, f32[4,192,128]{2,1,0:T(8,128)S(1)} %get-tuple-element.34.field_ref.refs_2_, ...), custom_call_target="tpu_custom_call" | custom-call | flops 1572864000 | bytes 1048576 | tf_op jit(solution)/shard_map/pallas_call | solution.py:588
  27.8 1.1 %collective-permute-start.7 = (f32[3,3,8,128]{3,2,1,0:T(8,128)S(1)}, f32[3,3,8,128]{3,2,1,0:T(8,128)S(1)}, u32[]{:S(2)}, u32[]{:S(2)}) collective-permute-start(f32[3,3,8,128]{3,2,1,0:T(8,128)S(1)} %get-tuple-element.46.refs_4_), channel_id=1, source_target_pairs={{0,28},{4,8},{8,4},{12,16},{16,12},{20,24},{24,20},{28,0},{1,29},{... | collective-permute-start | bytes 110600 | tf_op jit(solution)/shard_map/ppermute | solution.py:603
  29.0 0.0 collective-permute-start.8
  29.0 0.8 %shard_map.53 = (bf16[5,2,2,144,128]{4,3,2,1,0:T(8,128)(2,1)S(1)}, f32[144,128]{1,0:T(8,128)S(1)}) custom-call(bf16[2240,256]{1,0:T(8,128)(2,1)S(1)} %copy-done, f32[8,128]{1,0:T(8,128)S(1)} %shard_map.46.refs_1_.step_ref, f32[4,192,128]{2,1,0:T(8,128)S(1)} %get-tuple-element.34.field_ref.refs_2_, f32[4,8,128]{2,1,0:T(8,128)S(1)} %get-tuple-element.35.refs_3_.heights_ref, ...), custom_call_target="tpu_custom_call" | custom-call | flops 589824000 | bytes 1048576 | tf_op jit(solution)/shard_map/pallas_call | solution.py:588
  29.7 2.5 %collective-permute-done.7.refs_6_ = f32[3,3,8,128]{3,2,1,0:T(8,128)S(1)} collective-permute-done((f32[3,3,8,128]{3,2,1,0:T(8,128)S(1)}, f32[3,3,8,128]{3,2,1,0:T(8,128)S(1)}, u32[]{:S(2)}, u32[]{:S(2)}) %collective-permute-start.7) | collective-permute-done | bytes 36896 | tf_op jit(solution)/shard_map/ppermute | solution.py:603
  32.2 0.0 collective-permute-done.8.refs_7_
  32.2 1.6 %shard_map.54 = (f32[2,3,8,128]{3,2,1,0:T(8,128)S(1)}, f32[5,192,128]{2,1,0:T(8,128)S(1)}, f32[3,8,128]{2,1,0:T(8,128)S(1)}, f32[3,8,128]{2,1,0:T(8,128)S(1)}) custom-call(bf16[2240,256]{1,0:T(8,128)(2,1)S(1)} %copy-done, f32[8,128]{1,0:T(8,128)S(1)} %shard_map.46.refs_1_.step_ref, f32[4,192,128]{2,1,0:T(8,128)S(1)} %get-tuple-element.34.field_ref.refs_2_, ...), custom_call_target="tpu_custom_call" | custom-call | flops 1179648000 | bytes 1048576 | tf_op jit(solution)/shard_map/pallas_call | solution.py:588
  33.8 1.1 %collective-permute-start.9 = (f32[3,8,128]{2,1,0:T(8,128)S(1)}, f32[3,8,128]{2,1,0:T(8,128)S(1)}, u32[]{:S(2)}, u32[]{:S(2)}) collective-permute-start(f32[3,8,128]{2,1,0:T(8,128)S(1)} %get-tuple-element.52.own_cross_ref), channel_id=1, source_target_pairs={{0,28},{4,8},{8,4},{12,16},{16,12},{20,24},{24,20},{28,0},{1,29},{... | collective-permute-start | bytes 36872 | tf_op jit(solution)/shard_map/ppermute | solution.py:603
  34.9 0.0 collective-permute-start.10
  34.9 0.4 shard_map.55.inner_ref
  35.3 2.6 %collective-permute-done.9.cross_ref = f32[3,8,128]{2,1,0:T(8,128)S(1)} collective-permute-done((f32[3,8,128]{2,1,0:T(8,128)S(1)}, f32[3,8,128]{2,1,0:T(8,128)S(1)}, u32[]{:S(2)}, u32[]{:S(2)}) %collective-permute-start.9) | collective-permute-done | bytes 12320 | tf_op jit(solution)/shard_map/ppermute | solution.py:603
  37.9 0.0 collective-permute-done.10.core_ref
  37.9 0.7 %shard_map.56 = f32[192,128]{1,0:T(8,128)} custom-call(f32[3,8,128]{2,1,0:T(8,128)S(1)} %get-tuple-element.52.own_cross_ref, f32[3,8,128]{2,1,0:T(8,128)S(1)} %get-tuple-element.53.own_core_ref, f32[3,8,128]{2,1,0:T(8,128)S(1)} %collective-permute-done.9.cross_ref, f32[3,8,128]{2,1,0:T(8,128)S(1)} %collective-permute-done.10.core_ref, ...), custom_call_target="tpu_custom_call" | custom-call | bytes 1048576 | tf_op jit(solution)/shard_map/pallas_call | solution.py:588
Async XLA Ops:
  1.6 10.5 %collective-permute-start.1 = (f32[200,128]{1,0:T(8,128)S(1)}, f32[200,128]{1,0:T(8,128)S(1)}, u32[]{:S(2)}, u32[]{:S(2)}) collective-permute-start(f32[200,128]{1,0:T(8,128)S(1)} %concatenate.3.refs_2_), channel_id=1, source_target_pairs={{0,2},{1,3},{2,0},{3,1},{4,6},{5,7},{6,4},{7,5},{8,10},{9,11},{10,... | collective-permute-start | bytes 307208 | tf_op jit(solution)/shard_map/ppermute | solution.py:623
  5.6 6.5 %collective-permute-start = (f32[200,128]{1,0:T(8,128)S(1)}, f32[200,128]{1,0:T(8,128)S(1)}, u32[]{:S(2)}, u32[]{:S(2)}) collective-permute-start(f32[200,128]{1,0:T(8,128)S(1)} %concatenate.3.refs_2_), channel_id=1, source_target_pairs={{0,1},{1,0},{2,3},{3,2},{4,5},{5,4},{6,7},{7,6},{8,9},{9,8},{10,11... | collective-permute-start | bytes 307208 | tf_op jit(solution)/shard_map/ppermute | solution.py:623
  7.2 6.9 %collective-permute-start.2 = (f32[200,128]{1,0:T(8,128)S(1)}, f32[200,128]{1,0:T(8,128)S(1)}, u32[]{:S(2)}, u32[]{:S(2)}) collective-permute-start(f32[200,128]{1,0:T(8,128)S(1)} %concatenate.3.refs_2_), channel_id=1, source_target_pairs={{0,3},{1,2},{2,1},{3,0},{4,7},{5,6},{6,5},{7,4},{8,11},{9,10},{10,... | collective-permute-start | bytes 307208 | tf_op jit(solution)/shard_map/ppermute | solution.py:623
  7.8 1.3 %copy-start = (bf16[2240,256]{1,0:T(8,128)(2,1)S(1)}, bf16[2240,256]{1,0:T(8,128)(2,1)}, u32[]{:S(2)}) copy-start(bf16[2240,256]{1,0:T(8,128)(2,1)} %constant.2.clone.mats.refs_0_) | copy-start | bytes 3440644
  15.1 4.8 %collective-permute-start.3 = (f32[4,3,8,128]{3,2,1,0:T(8,128)S(1)}, f32[4,3,8,128]{3,2,1,0:T(8,128)S(1)}, u32[]{:S(2)}, u32[]{:S(2)}) collective-permute-start(f32[4,3,8,128]{3,2,1,0:T(8,128)S(1)} %get-tuple-element.36.refs_4_), channel_id=1, source_target_pairs={{0,28},{4,8},{8,4},{12,16},{16,12},{20,24},{24,20},{28,0},{1,29},{... | collective-permute-start | bytes 147464 | tf_op jit(solution)/shard_map/ppermute | solution.py:603
  16.4 3.6 %collective-permute-start.4 = (f32[4,3,8,128]{3,2,1,0:T(8,128)S(1)}, f32[4,3,8,128]{3,2,1,0:T(8,128)S(1)}, u32[]{:S(2)}, u32[]{:S(2)}) collective-permute-start(f32[4,3,8,128]{3,2,1,0:T(8,128)S(1)} %get-tuple-element.37.refs_5_), channel_id=1, source_target_pairs={{0,4},{4,0},{8,12},{12,8},{16,20},{20,16},{24,28},{28,24},{1,5},{5... | collective-permute-start | bytes 147464 | tf_op jit(solution)/shard_map/ppermute | solution.py:603
  21.6 4.6 %collective-permute-start.5 = (f32[4,3,8,128]{3,2,1,0:T(8,128)S(1)}, f32[4,3,8,128]{3,2,1,0:T(8,128)S(1)}, u32[]{:S(2)}, u32[]{:S(2)}) collective-permute-start(f32[4,3,8,128]{3,2,1,0:T(8,128)S(1)} %get-tuple-element.40.refs_4_), channel_id=1, source_target_pairs={{0,28},{4,8},{8,4},{12,16},{16,12},{20,24},{24,20},{28,0},{1,29},{... | collective-permute-start | bytes 147464 | tf_op jit(solution)/shard_map/ppermute | solution.py:603
  22.8 3.4 %collective-permute-start.6 = (f32[4,3,8,128]{3,2,1,0:T(8,128)S(1)}, f32[4,3,8,128]{3,2,1,0:T(8,128)S(1)}, u32[]{:S(2)}, u32[]{:S(2)}) collective-permute-start(f32[4,3,8,128]{3,2,1,0:T(8,128)S(1)} %get-tuple-element.41.refs_5_), channel_id=1, source_target_pairs={{0,4},{4,0},{8,12},{12,8},{16,20},{20,16},{24,28},{28,24},{1,5},{5... | collective-permute-start | bytes 147464 | tf_op jit(solution)/shard_map/ppermute | solution.py:603
  27.8 4.3 %collective-permute-start.7 = (f32[3,3,8,128]{3,2,1,0:T(8,128)S(1)}, f32[3,3,8,128]{3,2,1,0:T(8,128)S(1)}, u32[]{:S(2)}, u32[]{:S(2)}) collective-permute-start(f32[3,3,8,128]{3,2,1,0:T(8,128)S(1)} %get-tuple-element.46.refs_4_), channel_id=1, source_target_pairs={{0,28},{4,8},{8,4},{12,16},{16,12},{20,24},{24,20},{28,0},{1,29},{... | collective-permute-start | bytes 110600 | tf_op jit(solution)/shard_map/ppermute | solution.py:603
  29.0 3.2 %collective-permute-start.8 = (f32[3,3,8,128]{3,2,1,0:T(8,128)S(1)}, f32[3,3,8,128]{3,2,1,0:T(8,128)S(1)}, u32[]{:S(2)}, u32[]{:S(2)}) collective-permute-start(f32[3,3,8,128]{3,2,1,0:T(8,128)S(1)} %get-tuple-element.47.refs_5_), channel_id=1, source_target_pairs={{0,4},{4,0},{8,12},{12,8},{16,20},{20,16},{24,28},{28,24},{1,5},{5... | collective-permute-start | bytes 110600 | tf_op jit(solution)/shard_map/ppermute | solution.py:603
  33.8 4.1 %collective-permute-start.9 = (f32[3,8,128]{2,1,0:T(8,128)S(1)}, f32[3,8,128]{2,1,0:T(8,128)S(1)}, u32[]{:S(2)}, u32[]{:S(2)}) collective-permute-start(f32[3,8,128]{2,1,0:T(8,128)S(1)} %get-tuple-element.52.own_cross_ref), channel_id=1, source_target_pairs={{0,28},{4,8},{8,4},{12,16},{16,12},{20,24},{24,20},{28,0},{1,29},{... | collective-permute-start | bytes 36872 | tf_op jit(solution)/shard_map/ppermute | solution.py:603
  34.9 3.0 %collective-permute-start.10 = (f32[3,8,128]{2,1,0:T(8,128)S(1)}, f32[3,8,128]{2,1,0:T(8,128)S(1)}, u32[]{:S(2)}, u32[]{:S(2)}) collective-permute-start(f32[3,8,128]{2,1,0:T(8,128)S(1)} %get-tuple-element.53.own_core_ref), channel_id=1, source_target_pairs={{0,4},{4,0},{8,12},{12,8},{16,20},{20,16},{24,28},{28,24},{1,5},{5... | collective-permute-start | bytes 36872 | tf_op jit(solution)/shard_map/ppermute | solution.py:603

commit v8 on v7

--- a/solution.py
+++ b/solution.py
@@ -529,11 +529,18 @@
     rate_ref[...] = (total_ref[...] + partial_ref[0]) / 6.0
 
 
-def stage_kernel(count, share, first, next_last, last, *refs):
+def ends_kernel(first, last, *refs):
+    own_cross_ref, own_core_ref, cross_ref, core_ref = refs[:4]
+    place = 0 if last else lax.axis_index("vert")
+    own = join_ends(own_cross_ref[place], own_core_ref[place], cross_ref[place], core_ref[place])
+    for k in range(2):
+        refs[-1][k] = own[k] if first else refs[4][k] + 2.0 * own[k]
+
+
+def stage_kernel(count, share, next_last, last, *refs):
     mats, step_ref, field_ref, heights_ref, own_cross_ref, own_core_ref = refs[:6]
     cross_ref, core_ref, spots_ref = refs[6:9]
-    total = None if first else refs[9]
-    total_ref, backs_ref, next_cross_ref, next_core_ref, faces_ref = refs[-5:]
+    backs_ref, next_cross_ref, next_core_ref, faces_ref = refs[-4:]
     place = lax.axis_index("vert")
     step = step_ref[:1] * share
     layers = stage_layers(count, last)
@@ -565,10 +572,6 @@
         join_heights(faces, heights, [(l, l + 1, True) for l in range(count - 1)])
         for i, l in enumerate(stage_layers(count, next_last)):
             put_faces(faces_ref[l], next_cross_ref, next_core_ref, i)
-    place = 0 if last else place
-    own = join_ends(own_cross_ref[place], own_core_ref[place], cross_ref[place], core_ref[place])
-    for k in range(2):
-        total_ref[k] = own[k] if first else total[k] + 2.0 * own[k]
 
 
 def rate_kernel(own_cross_ref, own_core_ref, cross_ref, core_ref, inner_ref, total_ref, rate_ref):
@@ -662,15 +665,21 @@
             )
         args = [mats, step, fields, all_heights, *own_ends, *ends, spots]
         end = (small, (3,) + small, face)[2 - stage]
-        face_total, backs, cross, core = call(
-            functools.partial(stage_kernel, layers, share, stage == 0, stage == 1, last),
-            [(2,) + small, (len(spots_of(used)), ROWS, SPAN), end, end],
-            args + ([] if stage == 0 else [face_total]),
+        backs, cross, core = call(
+            functools.partial(stage_kernel, layers, share, stage == 1, last),
+            [(len(spots_of(used)), ROWS, SPAN), end, end],
+            args,
             scratch=[pltpu.VMEM((used, 48, SPAN), f32)],
             flops=used * unit,
         )
+        before = [*own_ends, *ends]
         own_ends = cross, core
         ends = swap_stream(cross, core)
+        face_total = call(
+            functools.partial(ends_kernel, stage == 0, last),
+            [(2,) + small],
+            before + ([] if stage == 0 else [face_total]),
+        )
     inner = call(
         functools.partial(last_inner_kernel, layers),
         [(144, SPAN)],

time: 38.7 us -> 38.8 us (level)
    pallas_call x11 -> x14, Pallas kernels: 10.8 us -> 10.9 us  [call(): pl.pallas_call(kernel, out_shape=shapes[0] if one else shapes, in_specs=[...]
    unnamed x2 -> x4, local copies, waits for them, and re-layouts: 1.25 us -> 1.26 us
where the time goes in v8:
time: 38.8 us; the launch traced here: 38.6 us
  waiting for transfers between devices  13.4 us (35%)
  Pallas kernels  10.9 us (28%)
  starting transfers between devices  10.8 us (28%)
  local copies, waits for them, and re-layouts  2.16 us (6%)
  between operations  1.4 us (4%)
    pallas_call x14, Pallas kernels, call(): pl.pallas_call(kernel, out_shape=shapes[0] if one else shapes, in_specs=[...  10.9 us
    ppermute x4, waiting for transfers between devices, swap_stream(): lax.ppermute(cross, 'horiz', crosses)  10.2 us
    ppermute x3, starting transfers between devices, on_device(): slots[j] = lax.ppermute(packed, 'vert', [(i, i ^ j) for i in range(layers)])  5.62 us
    ppermute x4, starting transfers between devices, swap_stream(): lax.ppermute(cross, 'horiz', crosses)  4.71 us
    ppermute x3, waiting for transfers between devices, on_device(): slots[j] = lax.ppermute(packed, 'vert', [(i, i ^ j) for i in range(layers)])  3.14 us
    unnamed x4, local copies, waits for them, and re-layouts  1.26 us
    concatenate x1, local copies, waits for them, and re-layouts, on_device(): jnp.concatenate([own_field, jnp.broadcast_to(heights[:, None], (8, SPAN))...  0.9 us
  transfers between devices with their start and end apart: 11, of which 6 were waited for; matrix products, arithmetic and copies ran while one was open for 0% of the time, Pallas kernels for 11%

profile of v8, /device:TPU:0, one launch (start us, length us, event | category | flops | bytes accessed | tf_op | source)
XLA Modules:
  0.0 38.6 jit_solution(9410950806453337290)
XLA Ops:
  0.7 0.9 %concatenate.3.refs_2_ = f32[200,128]{1,0:T(8,128)S(1)} pad(f32[192,128]{1,0:T(8,128)} %bitcast.6, f32[]{:T(128)} %bitcast.4), padding=0_8x0_0 | pad | bytes 200708 | tf_op jit(solution)/shard_map/concatenate | solution.py:621
  1.6 4.0 %collective-permute-start.1 = (f32[200,128]{1,0:T(8,128)S(1)}, f32[200,128]{1,0:T(8,128)S(1)}, u32[]{:S(2)}, u32[]{:S(2)}) collective-permute-start(f32[200,128]{1,0:T(8,128)S(1)} %concatenate.3.refs_2_), channel_id=1, source_target_pairs={{0,2},{1,3},{2,0},{3,1},{4,6},{5,7},{6,4},{7,5},{8,10},{9,11},{10,... | collective-permute-start | bytes 307208 | tf_op jit(solution)/shard_map/ppermute | solution.py:626
  5.6 1.6 %collective-permute-start = (f32[200,128]{1,0:T(8,128)S(1)}, f32[200,128]{1,0:T(8,128)S(1)}, u32[]{:S(2)}, u32[]{:S(2)}) collective-permute-start(f32[200,128]{1,0:T(8,128)S(1)} %concatenate.3.refs_2_), channel_id=1, source_target_pairs={{0,1},{1,0},{2,3},{3,2},{4,5},{5,4},{6,7},{7,6},{8,9},{9,8},{10,11... | collective-permute-start | bytes 307208 | tf_op jit(solution)/shard_map/ppermute | solution.py:626
  7.2 0.0 collective-permute-start.2
  7.8 0.0 copy-start
  7.8 1.2 %copy-done = bf16[2240,256]{1,0:T(8,128)(2,1)S(1)} copy-done((bf16[2240,256]{1,0:T(8,128)(2,1)S(1)}, bf16[2240,256]{1,0:T(8,128)(2,1)}, u32[]{:S(2)}) %copy-start) | copy-done | bytes 1146904
  9.1 0.1 shard_map.46.refs_1_.step_ref
  9.2 2.9 %collective-permute-done.1.refs_4_ = f32[200,128]{1,0:T(8,128)S(1)} collective-permute-done((f32[200,128]{1,0:T(8,128)S(1)}, f32[200,128]{1,0:T(8,128)S(1)}, u32[]{:S(2)}, u32[]{:S(2)}) %collective-permute-start.1) | collective-permute-done | bytes 102432 | tf_op jit(solution)/shard_map/ppermute | solution.py:626
  12.1 0.0 collective-permute-done.refs_3_
  12.1 1.7 %shard_map.47 = (f32[192,128]{1,0:T(8,128)S(1)}, f32[192,128]{1,0:T(8,128)S(1)}, f32[192,128]{1,0:T(8,128)S(1)}) custom-call(bf16[2240,256]{1,0:T(8,128)(2,1)S(1)} %copy-done, f32[8,128]{1,0:T(8,128)S(1)} %shard_map.46.refs_1_.step_ref, f32[200,128]{1,0:T(8,128)S(1)} %concatenate.3.refs_2_, f32[200,128]{1,0:T(8,128)S(1)} %collective-permute-done.refs_3_, ...), custom_call_target="tpu_custom_call" | custom-call | flops 1179648000 | bytes 1048576 | tf_op jit(solution)/shard_map/pallas_call | solution.py:591
  13.8 0.2 collective-permute-done.2.refs_5_
  14.0 1.0 %shard_map.48 = (f32[4,192,128]{2,1,0:T(8,128)S(1)}, f32[4,8,128]{2,1,0:T(8,128)S(1)}, f32[4,192,128]{2,1,0:T(8,128)S(1)}, f32[4,3,8,128]{3,2,1,0:T(8,128)S(1)}, f32[4,3,8,128]{3,2,1,0:T(8,128)S(1)}) custom-call(bf16[2240,256]{1,0:T(8,128)(2,1)S(1)} %copy-done, f32[8,128]{1,0:T(8,128)S(1)} %shard_map.46.refs_1_.step_ref, f32[200,128]{1,0:T(8,128)S(1)} %concatenate.3.refs_2_, ...), custom_call_target="tpu_custom_call" | custom-call | flops 1572864000 | bytes 1048576 | tf_op jit(solution)/shard_map/pallas_call | solution.py:591
  15.1 1.3 %collective-permute-start.3 = (f32[4,3,8,128]{3,2,1,0:T(8,128)S(1)}, f32[4,3,8,128]{3,2,1,0:T(8,128)S(1)}, u32[]{:S(2)}, u32[]{:S(2)}) collective-permute-start(f32[4,3,8,128]{3,2,1,0:T(8,128)S(1)} %get-tuple-element.33.refs_4_.refs_0_), channel_id=1, source_target_pairs={{0,28},{4,8},{8,4},{12,16},{16,12},{20,24},{24,20},{28,0},{1,29},{... | collective-permute-start | bytes 147464 | tf_op jit(solution)/shard_map/ppermute | solution.py:606
  16.4 0.4 %collective-permute-start.4 = (f32[4,3,8,128]{3,2,1,0:T(8,128)S(1)}, f32[4,3,8,128]{3,2,1,0:T(8,128)S(1)}, u32[]{:S(2)}, u32[]{:S(2)}) collective-permute-start(f32[4,3,8,128]{3,2,1,0:T(8,128)S(1)} %get-tuple-element.34.refs_5_.refs_1_), channel_id=1, source_target_pairs={{0,4},{4,0},{8,12},{12,8},{16,20},{20,16},{24,28},{28,24},{1,5},{5... | collective-permute-start | bytes 147464 | tf_op jit(solution)/shard_map/ppermute | solution.py:606
  16.8 0.4 %shard_map.49 = (bf16[6,2,2,144,128]{4,3,2,1,0:T(8,128)(2,1)S(1)}, f32[144,128]{1,0:T(8,128)S(1)}) custom-call(bf16[2240,256]{1,0:T(8,128)(2,1)S(1)} %copy-done, f32[8,128]{1,0:T(8,128)S(1)} %shard_map.46.refs_1_.step_ref, f32[4,192,128]{2,1,0:T(8,128)S(1)} %get-tuple-element.31.field_ref.refs_2_, f32[4,192,128]{2,1,0:T(8,128)S(1)} %get-tuple-element.35.partial_ref), custom_call_target="tpu_custom_call" | custom-call | flops 393216000 | bytes 1048576 | tf_op jit(solution)/shard_map/pallas_call | solution.py:591
  17.3 2.7 %collective-permute-done.3.refs_6_.refs_2_ = f32[4,3,8,128]{3,2,1,0:T(8,128)S(1)} collective-permute-done((f32[4,3,8,128]{3,2,1,0:T(8,128)S(1)}, f32[4,3,8,128]{3,2,1,0:T(8,128)S(1)}, u32[]{:S(2)}, u32[]{:S(2)}) %collective-permute-start.3) | collective-permute-done | bytes 49184 | tf_op jit(solution)/shard_map/ppermute | solution.py:606
  19.9 0.0 collective-permute-done.4.refs_7_.refs_3_
  19.9 0.0 copy-start.1
  19.9 1.7 %shard_map.50 = (f32[6,192,128]{2,1,0:T(8,128)S(1)}, f32[4,3,8,128]{3,2,1,0:T(8,128)S(1)}, f32[4,3,8,128]{3,2,1,0:T(8,128)S(1)}) custom-call(bf16[2240,256]{1,0:T(8,128)(2,1)S(1)} %copy-done, f32[8,128]{1,0:T(8,128)S(1)} %shard_map.46.refs_1_.step_ref, f32[4,192,128]{2,1,0:T(8,128)S(1)} %get-tuple-element.31.field_ref.refs_2_, ...), custom_call_target="tpu_custom_call" | custom-call | flops 1572864000 | bytes 1048576 | tf_op jit(solution)/shard_map/pallas_call | solution.py:591
  21.6 1.2 %collective-permute-start.5 = (f32[4,3,8,128]{3,2,1,0:T(8,128)S(1)}, f32[4,3,8,128]{3,2,1,0:T(8,128)S(1)}, u32[]{:S(2)}, u32[]{:S(2)}) collective-permute-start(f32[4,3,8,128]{3,2,1,0:T(8,128)S(1)} %get-tuple-element.37.refs_4_.refs_0_), channel_id=1, source_target_pairs={{0,28},{4,8},{8,4},{12,16},{16,12},{20,24},{24,20},{28,0},{1,29},{... | collective-permute-start | bytes 147464 | tf_op jit(solution)/shard_map/ppermute | solution.py:606
  22.8 0.0 collective-permute-start.6
  22.8 0.0 copy-done.1
  22.8 0.8 %shard_map.51 = (bf16[6,2,2,144,128]{4,3,2,1,0:T(8,128)(2,1)S(1)}, f32[144,128]{1,0:T(8,128)S(1)}) custom-call(bf16[2240,256]{1,0:T(8,128)(2,1)S(1)} %copy-done.1, f32[8,128]{1,0:T(8,128)S(1)} %shard_map.46.refs_1_.step_ref, f32[4,192,128]{2,1,0:T(8,128)S(1)} %get-tuple-element.31.field_ref.refs_2_, f32[4,8,128]{2,1,0:T(8,128)S(1)} %get-tuple-element.32.refs_3_.heights_ref, ...), custom_call_target="tpu_custom_call" | custom-call | flops 786432000 | bytes 1048576 | tf_op jit(solution)/shard_map/pallas_call | solution.py:591
  23.6 2.5 %collective-permute-done.5.refs_6_.refs_2_ = f32[4,3,8,128]{3,2,1,0:T(8,128)S(1)} collective-permute-done((f32[4,3,8,128]{3,2,1,0:T(8,128)S(1)}, f32[4,3,8,128]{3,2,1,0:T(8,128)S(1)}, u32[]{:S(2)}, u32[]{:S(2)}) %collective-permute-start.5) | collective-permute-done | bytes 49184 | tf_op jit(solution)/shard_map/ppermute | solution.py:606
  26.2 0.0 collective-permute-done.6.refs_7_.refs_3_
  26.2 1.7 %shard_map.52 = (f32[6,192,128]{2,1,0:T(8,128)S(1)}, f32[3,3,8,128]{3,2,1,0:T(8,128)S(1)}, f32[3,3,8,128]{3,2,1,0:T(8,128)S(1)}) custom-call(bf16[2240,256]{1,0:T(8,128)(2,1)S(1)} %copy-done.1, f32[8,128]{1,0:T(8,128)S(1)} %shard_map.46.refs_1_.step_ref, f32[4,192,128]{2,1,0:T(8,128)S(1)} %get-tuple-element.31.field_ref.refs_2_, ...), custom_call_target="tpu_custom_call" | custom-call | flops 1572864000 | bytes 1048576 | tf_op jit(solution)/shard_map/pallas_call | solution.py:591
  27.9 1.1 %collective-permute-start.7 = (f32[3,3,8,128]{3,2,1,0:T(8,128)S(1)}, f32[3,3,8,128]{3,2,1,0:T(8,128)S(1)}, u32[]{:S(2)}, u32[]{:S(2)}) collective-permute-start(f32[3,3,8,128]{3,2,1,0:T(8,128)S(1)} %get-tuple-element.42.refs_4_.refs_0_), channel_id=1, source_target_pairs={{0,28},{4,8},{8,4},{12,16},{16,12},{20,24},{24,20},{28,0},{1,29},{... | collective-permute-start | bytes 110600 | tf_op jit(solution)/shard_map/ppermute | solution.py:606
  29.0 0.0 collective-permute-start.8
  29.0 0.8 %shard_map.53 = (bf16[5,2,2,144,128]{4,3,2,1,0:T(8,128)(2,1)S(1)}, f32[144,128]{1,0:T(8,128)S(1)}) custom-call(bf16[2240,256]{1,0:T(8,128)(2,1)S(1)} %copy-done.1, f32[8,128]{1,0:T(8,128)S(1)} %shard_map.46.refs_1_.step_ref, f32[4,192,128]{2,1,0:T(8,128)S(1)} %get-tuple-element.31.field_ref.refs_2_, f32[4,8,128]{2,1,0:T(8,128)S(1)} %get-tuple-element.32.refs_3_.heights_ref, ...), custom_call_target="tpu_custom_call" | custom-call | flops 589824000 | bytes 1048576 | tf_op jit(solution)/shard_map/pallas_call | solution.py:591
  29.8 2.4 %collective-permute-done.7.refs_6_.refs_2_ = f32[3,3,8,128]{3,2,1,0:T(8,128)S(1)} collective-permute-done((f32[3,3,8,128]{3,2,1,0:T(8,128)S(1)}, f32[3,3,8,128]{3,2,1,0:T(8,128)S(1)}, u32[]{:S(2)}, u32[]{:S(2)}) %collective-permute-start.7) | collective-permute-done | bytes 36896 | tf_op jit(solution)/shard_map/ppermute | solution.py:606
  32.2 0.0 collective-permute-done.8.refs_7_.refs_3_
  32.2 1.7 %shard_map.54 = (f32[5,192,128]{2,1,0:T(8,128)S(1)}, f32[3,8,128]{2,1,0:T(8,128)S(1)}, f32[3,8,128]{2,1,0:T(8,128)S(1)}) custom-call(bf16[2240,256]{1,0:T(8,128)(2,1)S(1)} %copy-done.1, f32[8,128]{1,0:T(8,128)S(1)} %shard_map.46.refs_1_.step_ref, f32[4,192,128]{2,1,0:T(8,128)S(1)} %get-tuple-element.31.field_ref.refs_2_, ...), custom_call_target="tpu_custom_call" | custom-call | flops 1179648000 | bytes 1048576 | tf_op jit(solution)/shard_map/pallas_call | solution.py:591
  33.9 1.1 %collective-permute-start.9 = (f32[3,8,128]{2,1,0:T(8,128)S(1)}, f32[3,8,128]{2,1,0:T(8,128)S(1)}, u32[]{:S(2)}, u32[]{:S(2)}) collective-permute-start(f32[3,8,128]{2,1,0:T(8,128)S(1)} %get-tuple-element.47.own_cross_ref), channel_id=1, source_target_pairs={{0,28},{4,8},{8,4},{12,16},{16,12},{20,24},{24,20},{28,0},{1,29},{... | collective-permute-start | bytes 36872 | tf_op jit(solution)/shard_map/ppermute | solution.py:606
  35.0 0.0 collective-permute-start.10
  35.0 0.4 shard_map.55.inner_ref
  35.4 2.6 %collective-permute-done.9.cross_ref = f32[3,8,128]{2,1,0:T(8,128)S(1)} collective-permute-done((f32[3,8,128]{2,1,0:T(8,128)S(1)}, f32[3,8,128]{2,1,0:T(8,128)S(1)}, u32[]{:S(2)}, u32[]{:S(2)}) %collective-permute-start.9) | collective-permute-done | bytes 12320 | tf_op jit(solution)/shard_map/ppermute | solution.py:606
  38.0 0.0 collective-permute-done.10.core_ref
  38.0 0.7 %shard_map.59 = f32[192,128]{1,0:T(8,128)} custom-call(f32[3,8,128]{2,1,0:T(8,128)S(1)} %get-tuple-element.47.own_cross_ref, f32[3,8,128]{2,1,0:T(8,128)S(1)} %get-tuple-element.48.own_core_ref, f32[3,8,128]{2,1,0:T(8,128)S(1)} %collective-permute-done.9.cross_ref, f32[3,8,128]{2,1,0:T(8,128)S(1)} %collective-permute-done.10.core_ref, ...), custom_call_target="tpu_custom_call" | custom-call | bytes 1048576 | tf_op jit(solution)/shard_map/pallas_call | solution.py:591
  (3 shorter events, 0.0 us)
Async XLA Ops:
  1.6 10.5 %collective-permute-start.1 = (f32[200,128]{1,0:T(8,128)S(1)}, f32[200,128]{1,0:T(8,128)S(1)}, u32[]{:S(2)}, u32[]{:S(2)}) collective-permute-start(f32[200,128]{1,0:T(8,128)S(1)} %concatenate.3.refs_2_), channel_id=1, source_target_pairs={{0,2},{1,3},{2,0},{3,1},{4,6},{5,7},{6,4},{7,5},{8,10},{9,11},{10,... | collective-permute-start | bytes 307208 | tf_op jit(solution)/shard_map/ppermute | solution.py:626
  5.6 6.5 %collective-permute-start = (f32[200,128]{1,0:T(8,128)S(1)}, f32[200,128]{1,0:T(8,128)S(1)}, u32[]{:S(2)}, u32[]{:S(2)}) collective-permute-start(f32[200,128]{1,0:T(8,128)S(1)} %concatenate.3.refs_2_), channel_id=1, source_target_pairs={{0,1},{1,0},{2,3},{3,2},{4,5},{5,4},{6,7},{7,6},{8,9},{9,8},{10,11... | collective-permute-start | bytes 307208 | tf_op jit(solution)/shard_map/ppermute | solution.py:626
  7.2 6.9 %collective-permute-start.2 = (f32[200,128]{1,0:T(8,128)S(1)}, f32[200,128]{1,0:T(8,128)S(1)}, u32[]{:S(2)}, u32[]{:S(2)}) collective-permute-start(f32[200,128]{1,0:T(8,128)S(1)} %concatenate.3.refs_2_), channel_id=1, source_target_pairs={{0,3},{1,2},{2,1},{3,0},{4,7},{5,6},{6,5},{7,4},{8,11},{9,10},{10,... | collective-permute-start | bytes 307208 | tf_op jit(solution)/shard_map/ppermute | solution.py:626
  7.8 1.3 %copy-start = (bf16[2240,256]{1,0:T(8,128)(2,1)S(1)}, bf16[2240,256]{1,0:T(8,128)(2,1)}, u32[]{:S(2)}) copy-start(bf16[2240,256]{1,0:T(8,128)(2,1)} %constant.2.clone.mats.refs_0_) | copy-start | bytes 3440644
  15.1 4.8 %collective-permute-start.3 = (f32[4,3,8,128]{3,2,1,0:T(8,128)S(1)}, f32[4,3,8,128]{3,2,1,0:T(8,128)S(1)}, u32[]{:S(2)}, u32[]{:S(2)}) collective-permute-start(f32[4,3,8,128]{3,2,1,0:T(8,128)S(1)} %get-tuple-element.33.refs_4_.refs_0_), channel_id=1, source_target_pairs={{0,28},{4,8},{8,4},{12,16},{16,12},{20,24},{24,20},{28,0},{1,29},{... | collective-permute-start | bytes 147464 | tf_op jit(solution)/shard_map/ppermute | solution.py:606
  16.4 3.6 %collective-permute-start.4 = (f32[4,3,8,128]{3,2,1,0:T(8,128)S(1)}, f32[4,3,8,128]{3,2,1,0:T(8,128)S(1)}, u32[]{:S(2)}, u32[]{:S(2)}) collective-permute-start(f32[4,3,8,128]{3,2,1,0:T(8,128)S(1)} %get-tuple-element.34.refs_5_.refs_1_), channel_id=1, source_target_pairs={{0,4},{4,0},{8,12},{12,8},{16,20},{20,16},{24,28},{28,24},{1,5},{5... | collective-permute-start | bytes 147464 | tf_op jit(solution)/shard_map/ppermute | solution.py:606
  19.9 2.9 %copy-start.1 = (bf16[2240,256]{1,0:T(8,128)(2,1)S(1)}, bf16[2240,256]{1,0:T(8,128)(2,1)}, u32[]{:S(2)}) copy-start(bf16[2240,256]{1,0:T(8,128)(2,1)} %constant.2.clone.mats.refs_0_) | copy-start | bytes 3440644
  21.6 4.6 %collective-permute-start.5 = (f32[4,3,8,128]{3,2,1,0:T(8,128)S(1)}, f32[4,3,8,128]{3,2,1,0:T(8,128)S(1)}, u32[]{:S(2)}, u32[]{:S(2)}) collective-permute-start(f32[4,3,8,128]{3,2,1,0:T(8,128)S(1)} %get-tuple-element.37.refs_4_.refs_0_), channel_id=1, source_target_pairs={{0,28},{4,8},{8,4},{12,16},{16,12},{20,24},{24,20},{28,0},{1,29},{... | collective-permute-start | bytes 147464 | tf_op jit(solution)/shard_map/ppermute | solution.py:606
  22.8 3.4 %collective-permute-start.6 = (f32[4,3,8,128]{3,2,1,0:T(8,128)S(1)}, f32[4,3,8,128]{3,2,1,0:T(8,128)S(1)}, u32[]{:S(2)}, u32[]{:S(2)}) collective-permute-start(f32[4,3,8,128]{3,2,1,0:T(8,128)S(1)} %get-tuple-element.38.refs_5_.refs_1_), channel_id=1, source_target_pairs={{0,4},{4,0},{8,12},{12,8},{16,20},{20,16},{24,28},{28,24},{1,5},{5... | collective-permute-start | bytes 147464 | tf_op jit(solution)/shard_map/ppermute | solution.py:606
  27.9 4.3 %collective-permute-start.7 = (f32[3,3,8,128]{3,2,1,0:T(8,128)S(1)}, f32[3,3,8,128]{3,2,1,0:T(8,128)S(1)}, u32[]{:S(2)}, u32[]{:S(2)}) collective-permute-start(f32[3,3,8,128]{3,2,1,0:T(8,128)S(1)} %get-tuple-element.42.refs_4_.refs_0_), channel_id=1, source_target_pairs={{0,28},{4,8},{8,4},{12,16},{16,12},{20,24},{24,20},{28,0},{1,29},{... | collective-permute-start | bytes 110600 | tf_op jit(solution)/shard_map/ppermute | solution.py:606
  29.0 3.2 %collective-permute-start.8 = (f32[3,3,8,128]{3,2,1,0:T(8,128)S(1)}, f32[3,3,8,128]{3,2,1,0:T(8,128)S(1)}, u32[]{:S(2)}, u32[]{:S(2)}) collective-permute-start(f32[3,3,8,128]{3,2,1,0:T(8,128)S(1)} %get-tuple-element.43.refs_5_.refs_1_), channel_id=1, source_target_pairs={{0,4},{4,0},{8,12},{12,8},{16,20},{20,16},{24,28},{28,24},{1,5},{5... | collective-permute-start | bytes 110600 | tf_op jit(solution)/shard_map/ppermute | solution.py:606
  33.9 4.1 %collective-permute-start.9 = (f32[3,8,128]{2,1,0:T(8,128)S(1)}, f32[3,8,128]{2,1,0:T(8,128)S(1)}, u32[]{:S(2)}, u32[]{:S(2)}) collective-permute-start(f32[3,8,128]{2,1,0:T(8,128)S(1)} %get-tuple-element.47.own_cross_ref), channel_id=1, source_target_pairs={{0,28},{4,8},{8,4},{12,16},{16,12},{20,24},{24,20},{28,0},{1,29},{... | collective-permute-start | bytes 36872 | tf_op jit(solution)/shard_map/ppermute | solution.py:606
  35.0 3.0 %collective-permute-start.10 = (f32[3,8,128]{2,1,0:T(8,128)S(1)}, f32[3,8,128]{2,1,0:T(8,128)S(1)}, u32[]{:S(2)}, u32[]{:S(2)}) collective-permute-start(f32[3,8,128]{2,1,0:T(8,128)S(1)} %get-tuple-element.48.own_core_ref), channel_id=1, source_target_pairs={{0,4},{4,0},{8,12},{12,8},{16,20},{20,16},{24,28},{28,24},{1,5},{5... | collective-permute-start | bytes 36872 | tf_op jit(solution)/shard_map/ppermute | solution.py:606
